TPU v7x, 32 devices: a whole 2x2x4 slice. The times are simulated.
32 devices in a mesh: prow: 4 (over y, x), pcol: 8 (over z, core).
Axes of the slice: x: 2, y: 2, z: 4, core: 2. Of those that a mesh axis runs over, the one named last changes fastest.
Arguments:
- panel: bfloat16 [4, 4, 512, 512], P(None, 'prow', 'pcol'), may hold values from -1.5 to 1.5
- diag_inv: bfloat16 [512, 512], replicated, as said below
- nonzero: int32 [4, 4], P(None, 'prow'), may hold values from 0 to 1
- trailing: bfloat16 [4, 4, 1, 8, 512, 512], P(None, 'prow', None, 'pcol'), may hold values from -6 to 6
Outputs:
- panel_factor: bfloat16 [4, 4, 512, 512], P(None, 'prow', 'pcol')
- trailing_out: bfloat16 [4, 4, 1, 8, 512, 512], P(None, 'prow', None, 'pcol')
Inputs may be any that keep to these rules, and one draw needn't show every extreme that they name: `diag_inv`: lower triangular with a positive diagonal.
All inputs are finite; a program needn't handle non-finite values.
Results may differ from a plain program's by a relative error of at most 0.0017.
Values may be sent and summed in bfloat16 or wider, within the bound.
No kernel may reach another device: no remote copies, remote signals or barrier semaphores. Data moves between devices by JAX's collectives and lax.ppermute only.
A program may use at most 64 MiB of HBM per device.

v0:
```python
import jax
import jax.numpy as jnp
from jax import lax
from jax.sharding import PartitionSpec as P


def spread(x, axis, root):
    mine = lax.axis_index(axis) == root
    return lax.psum(jnp.where(mine, x, jnp.zeros_like(x)), axis)


def solve_rows(tiles_in, diag_inv, live_rows):
    product = jnp.einsum("snb,ab->sna", tiles_in, diag_inv, preferred_element_type=jnp.float32)
    return (product * live_rows[:, None, None]).astype(jnp.bfloat16)


def renew(previous, row_part, column_tiles, active):
    product = jnp.einsum(
        "sna,tba->stnb", row_part, column_tiles, preferred_element_type=jnp.float32
    )
    updated = (previous.astype(jnp.float32) - product).astype(jnp.bfloat16)
    return jnp.where(active[:, :, None, None], updated, previous)


def body(panel, diag_inv, nonzero, trailing):
    rows_dev = panel.shape[0]
    cols_dev = trailing.shape[2]
    grid_rows = lax.axis_size("prow")
    grid_cols = lax.axis_size("pcol")
    own_row = lax.axis_index("prow")
    own_col = lax.axis_index("pcol")
    live_rows = nonzero[:, 0].astype(jnp.float32)
    factor_strips = solve_rows(panel[:, 0], diag_inv, live_rows)
    row_ids = jnp.arange(rows_dev, dtype=jnp.int32) * grid_rows + own_row
    column_ids = jnp.arange(cols_dev, dtype=jnp.int32) * grid_cols + own_col
    below_diag = row_ids[:, None] >= column_ids[None, :]
    previous = trailing[:, 0, :, 0]
    row_full = lax.all_gather(factor_strips, "pcol", axis=1, tiled=True)
    stride = grid_cols // grid_rows
    column_picks = jnp.arange(cols_dev, dtype=jnp.int32) * stride + own_col // grid_rows
    chosen = jnp.take(row_full, column_picks, axis=0)
    column_tiles = spread(chosen, "prow", own_col % grid_rows)
    renewed = renew(previous, row_full, column_tiles, below_diag)
    return (factor_strips[:, None], renewed[:, None, :, None])


def solution(mesh):
    placed = (
        P(None, "prow", "pcol", None),
        P(),
        P(None, "prow"),
        P(None, "prow", None, "pcol", None, None),
    )
    return jax.shard_map(
        body,
        mesh=mesh,
        in_specs=placed,
        out_specs=(P(None, "prow", "pcol", None), P(None, "prow", None, "pcol", None, None)),
        check_vma=False,
    )
```

profile of v0, /device:TPU:0, one launch (start us, length us, event | category | flops | bytes accessed | tf_op | source)
XLA Modules:
  0.0 102.9 jit_solution(9969734736213631752)
XLA Ops:
  7.2 0.0 copy-start
  7.2 0.0 copy-start.1
  7.2 0.0 all-gather.2.cloned.1.call-start
  7.2 0.8 convert_bitcast_fusion
  8.0 0.2 copy-done
  8.2 2.0 %fusion.3 = bf16[4,64,512]{2,1,0:T(8,128)(2,1)} fusion(bf16[512,512]{1,0:T(8,128)(2,1)S(1)} %copy-done, bf16[4,1,64,512]{3,2,1,0:T(8,128)(2,1)} %param.4, f32[4]{0:T(128)S(1)} %convert_bitcast_fusion), kind=kOutput, calls=%fused_computation.5 | convolution fusion | flops 134479872 | bytes 1048592 | tf_op jit(solution)/shard_map/snb,ab->sna/dot_general | solution.py:13
  10.2 0.0 all-gather.2.cloned.1.call-update
  10.2 0.0 all-reduce.2.cloned.1.call-start
  10.3 31.9 %all-gather.2.cloned.1.call-done = bf16[4,512,512]{2,1,0:T(8,128)(2,1)} async-done(((bf16[4,64,512]{2,1,0:T(8,128)(2,1)}), bf16[4,512,512]{2,1,0:T(8,128)(2,1)}) %all-gather.2.cloned.1.call-update) | async-done | bytes 2097168 | tf_op jit(solution)/shard_map/all_gather | solution.py:38
  42.2 1.9 %fusion.7 = bf16[512,512]{1,0:T(8,128)(2,1)} fusion(bf16[4,512,512]{2,1,0:T(8,128)(2,1)} %all-gather.2.cloned.1.call-done, s32[]{:T(128)} %bitcast.8, pred[]{:T(512)} %bitcast.7, pred[]{:T(512)S(6)} %eq.5), kind=kLoop, calls=%fused_computation.10 | loop fusion | flops 524288 | bytes 1048582 | tf_op jit(solution)/shard_map/reshape.6
  44.1 0.0 all-reduce.2.cloned.1.call-update
  44.1 0.0 copy-done.1
  44.1 2.4 %copy.6 = bf16[4,1,1,1,512,512]{4,5,0,3,2,1:T(8,128)(2,1)} copy(bf16[4,1,1,1,512,512]{5,4,3,2,1,0:T(8,128)(2,1)S(1)} %copy-done.1) | data formatting | bytes 4194304 | tf_op args[3]
  46.5 43.5 %all-reduce.2.cloned.1.call-done = bf16[512,512]{1,0:T(8,128)(2,1)} async-done(((bf16[512,512]{1,0:T(8,128)(2,1)}), bf16[512,512]{1,0:T(8,128)(2,1)}) %all-reduce.2.cloned.1.call-update) | async-done | bytes 524304 | tf_op jit(solution)/shard_map/psum | solution.py:9
  90.0 3.7 %fusion.2 = bf16[4,1,1,1,512,512]{4,5,0,3,2,1:T(8,128)(2,1)S(1)} fusion(bf16[4,512,512]{2,1,0:T(8,128)(2,1)} %all-gather.2.cloned.1.call-done, bf16[4,1,1,1,512,512]{4,5,0,3,2,1:T(8,128)(2,1)} %copy.6, pred[4]{0:T(512)(128)(4,1)S(1)} %add_compare_fusion, bf16[512,512]{1,0:T(8,128)(2,1)} %all-reduce.2.cloned.1.call-done), kind=kOutput, calls=%fused_computation.3 | convolution fusion | flops 1077936128 | bytes 6815748 | tf_op jit(solution)/shard_map/sna,tba->stnb/dot_general | solution.py:18
  93.7 2.4 %copy.8 = bf16[4,1,1,1,512,512]{5,4,3,2,1,0:T(8,128)(2,1)} copy(bf16[4,1,1,1,512,512]{4,5,0,3,2,1:T(8,128)(2,1)S(1)} %fusion.2) | data formatting | bytes 4194304
  (1 shorter events, 0.0 us)
Async XLA Ops:
  7.2 1.0 %copy-start = (bf16[512,512]{1,0:T(8,128)(2,1)S(1)}, bf16[512,512]{1,0:T(8,128)(2,1)}, u32[]{:S(2)}) copy-start(bf16[512,512]{1,0:T(8,128)(2,1)} %param.5) | copy-start | bytes 1572868
  7.2 36.9 %copy-start.1 = (bf16[4,1,1,1,512,512]{5,4,3,2,1,0:T(8,128)(2,1)S(1)}, bf16[4,1,1,1,512,512]{5,4,3,2,1,0:T(8,128)(2,1)}, u32[]{:S(2)}) copy-start(bf16[4,1,1,1,512,512]{5,4,3,2,1,0:T(8,128)(2,1)} %param.7) | copy-start | bytes 6291460
  7.2 35.0 %all-gather.2.cloned.1.call-start = ((), (), s32[]{:S(2)}) async-start(), calls=%async_computation | async-start | bytes 2359296 | tf_op jit(solution)/shard_map/all_gather | solution.py:38
  10.2 79.8 %all-reduce.2.cloned.1.call-start = ((), (), s32[]{:S(2)}) async-start(), calls=%async_computation.1 | async-start | bytes 1048576 | tf_op jit(solution)/shard_map/psum | solution.py:9
Sparse Core Ops, SparseCore 0:
  10.3 31.7 all-gather.1
  45.2 44.8 all-reduce.1
where the time goes:
time: 103 us
  waiting for transfers between devices  75.4 us (73%)
  between operations  14.1 us (14%)
  matrix products  5.65 us (5%)
  local copies, waits for them, and re-layouts  4.9 us (5%)
  other arithmetic  2.72 us (3%)
    psum x1, waiting for transfers between devices, spread(): return lax.psum(jnp.where(mine, x, jnp.zeros_like(x)), axis)  43.5 us
    all_gather x1, waiting for transfers between devices, body(): row_full = lax.all_gather(factor_strips, 'pcol', axis=1, tiled=True)  31.9 us
    unnamed x6, local copies, waits for them, and re-layouts  4.9 us
    dot_general x1, matrix products, renew(): jnp.einsum('sna,tba->stnb', row_part, column_tiles, preferred_element_typ...  3.66 us
  transfers between devices with their start and end apart: 2, of which 2 were waited for; matrix products, arithmetic and copies ran while one was open for 2% of the time, Pallas kernels for 0%

commit v1 on v0

v1 whole, which is shorter than its diff:
```python
import functools

import jax
import jax.numpy as jnp
from jax import lax
from jax.experimental import pallas as pl
from jax.experimental.pallas import tpu as pltpu
from jax.sharding import PartitionSpec as P

TRANSPOSED = (((1,), (1,)), ((), ()))
HBM = pl.BlockSpec(memory_space=pl.ANY)
VMEM = pl.BlockSpec(memory_space=pltpu.VMEM)
SMEM = pl.BlockSpec(memory_space=pltpu.SMEM)
LIMIT = 60 * 1024 * 1024
SMALL = 8 * 1024 * 1024


def swap(x, axis, distance):
    size = lax.axis_size(axis)
    return lax.ppermute(x, axis, [(i, i ^ distance) for i in range(size)])


def solve_kernel(classes, nonzero, panel, diag_inv, factor, *refs):
    slabs, rests = refs[:classes], refs[classes:2 * classes]
    live, strips, inverse, sems = refs[2 * classes:]
    copies = [pltpu.make_async_copy(*pair, sems.at[n])
              for n, pair in enumerate(((nonzero, live), (panel, strips), (diag_inv, inverse)))]
    for copy in copies:
        copy.start()
    for copy in copies:
        copy.wait()
    steps, _, rows, size = strips.shape
    tiles_in = strips[...].reshape(steps * rows, size)
    product = lax.dot_general(tiles_in, inverse[...], TRANSPOSED, preferred_element_type=jnp.float32)
    product = product.reshape(steps, rows, size)
    for s in range(steps):
        factor[s, 0] = (product[s] * live[s].astype(jnp.float32)).astype(factor.dtype)
    own = lax.axis_index("pcol") // lax.axis_size("prow")
    for n in range(classes):
        first = jnp.bitwise_xor(own, n)
        slabs[n][...] = factor[first, 0]
        for m in range(1, steps):
            rests[n][m - 1] = factor[lax.rem(first + m, steps), 0]


def solve(panel, diag_inv, nonzero, classes):
    steps, _, rows, size = panel.shape
    slab = jax.ShapeDtypeStruct((rows, size), panel.dtype)
    rest = jax.ShapeDtypeStruct((steps - 1, rows, size), panel.dtype)
    outs = pl.pallas_call(
        functools.partial(solve_kernel, classes),
        out_shape=[jax.ShapeDtypeStruct(panel.shape, panel.dtype)] + [slab] * classes + [rest] * classes,
        in_specs=[HBM, HBM, HBM],
        out_specs=[VMEM] * (1 + 2 * classes),
        scratch_shapes=[
            pltpu.SMEM(nonzero[:, 0].shape, nonzero.dtype),
            pltpu.VMEM(panel.shape, panel.dtype),
            pltpu.VMEM(diag_inv.shape, diag_inv.dtype),
            pltpu.SemaphoreType.DMA((3,)),
        ],
        cost_estimate=pl.CostEstimate(flops=0, bytes_accessed=1024, transcendentals=0),
        compiler_params=pltpu.CompilerParams(vmem_limit_bytes=LIMIT),
        name="solve",
    )(nonzero[:, 0], panel, diag_inv)
    return outs[0], outs[1:1 + classes], outs[1 + classes:]


def pick_kernel(sources, *refs):
    ins, (keep, give) = refs[:sources], refs[sources:]
    c, r = lax.axis_index("pcol"), lax.axis_index("prow")
    for target, column in ((keep, c), (give, jnp.bitwise_xor(c, 1))):
        away = jnp.bitwise_xor(r, lax.rem(column, sources))
        for k in range(sources):
            @pl.when(away == k)
            def _():
                target[...] = ins[k][...]


def pick(slabs):
    shape = jax.ShapeDtypeStruct(slabs[0].shape, slabs[0].dtype)
    return pl.pallas_call(
        functools.partial(pick_kernel, len(slabs)),
        out_shape=[shape, shape],
        in_specs=[VMEM] * len(slabs),
        out_specs=[VMEM, VMEM],
        cost_estimate=pl.CostEstimate(flops=0, bytes_accessed=1024, transcendentals=0),
        compiler_params=pltpu.CompilerParams(vmem_limit_bytes=SMALL),
        name="pick",
    )(*slabs)


def renew_kernel(chips, *refs):
    firsts, rests, columns = refs[:2], refs[2:2 + 2 * chips], refs[2 + 2 * chips:4 + 2 * chips]
    trailing, out, rows_full, column, held, strip_sems, column_sems, in_sems, out_sems = refs[4 + 2 * chips:]
    steps, size = held.shape[0], held.shape[1]
    rows = firsts[0].shape[1]
    c, r = lax.axis_index("pcol"), lax.axis_index("prow")
    grid_rows = lax.axis_size("prow")
    own = c // grid_rows
    order = [lax.rem(own + m, steps) for m in range(steps)]

    def offset(core, k):
        source = jnp.bitwise_xor(c, 2 * k + core)
        return pl.ds(pl.multiple_of(source * rows, rows), rows)

    column_copies, strip_copies, in_copies = [], [], []
    for core in range(2):
        for k in range(chips):
            n = core * chips + k
            column_copies.append(pltpu.make_async_copy(columns[core].at[k], column.at[offset(core, k)], column_sems.at[n]))
    for copy in column_copies:
        copy.start()
    for m in range(steps):
        these = []
        for core in range(2):
            for k in range(chips):
                n = core * chips + k
                source = firsts[core].at[k] if m == 0 else rests[n].at[m - 1]
                these.append(pltpu.make_async_copy(source, rows_full.at[m, offset(core, k)], strip_sems.at[m, n]))
        strip_copies.append(these)
        in_copies.append(pltpu.make_async_copy(trailing.at[order[m], 0, 0, 0], held.at[m], in_sems.at[m]))
        for copy in these + in_copies[-1:]:
            copy.start()
    for copy in column_copies:
        copy.wait()
    for m in range(steps):
        for copy in strip_copies[m]:
            copy.wait()
        in_copies[m].wait()

        @pl.when(order[m] * grid_rows + r >= c)
        def _():
            product = lax.dot_general(rows_full[m], column[...], TRANSPOSED, preferred_element_type=jnp.float32)
            held[m] = (held[m].astype(jnp.float32) - product).astype(held.dtype)

        pltpu.make_async_copy(held.at[m], out.at[order[m], 0, 0, 0], out_sems.at[m]).start()
    for m in range(steps):
        pltpu.make_async_copy(held.at[m], out.at[order[m], 0, 0, 0], out_sems.at[m]).wait()


def renew(trailing, firsts, rests, columns):
    chips = len(rests) // 2
    steps, size = trailing.shape[0], trailing.shape[-1]
    tiles = pltpu.VMEM((steps, size, size), trailing.dtype)
    return pl.pallas_call(
        functools.partial(renew_kernel, chips),
        out_shape=jax.ShapeDtypeStruct(trailing.shape, trailing.dtype),
        in_specs=[HBM] * (5 + 2 * chips),
        out_specs=HBM,
        scratch_shapes=[
            tiles,
            pltpu.VMEM((size, size), trailing.dtype),
            tiles,
            pltpu.SemaphoreType.DMA((steps, 2 * chips)),
            pltpu.SemaphoreType.DMA((2 * chips,)),
            pltpu.SemaphoreType.DMA((steps,)),
            pltpu.SemaphoreType.DMA((steps,)),
        ],
        compiler_params=pltpu.CompilerParams(vmem_limit_bytes=LIMIT),
        name="renew",
    )(*firsts, *rests, *columns, trailing)


def body(panel, diag_inv, nonzero, trailing):
    grid_rows, grid_cols = lax.axis_size("prow"), lax.axis_size("pcol")
    chips = grid_cols // 2
    classes = max(1, grid_cols // grid_rows)
    factor, slabs, rests = solve(panel, diag_inv, nonzero, classes)

    def kind(k):
        return 2 * k // grid_rows

    near = [slabs[0]] + [swap(slabs[kind(k)], "pcol", 2 * k) for k in range(1, chips)]
    first = jnp.stack(near)
    rest = {0: rests[0]}
    for k in range(1, chips):
        low = k & -k
        if low == k:
            rest[k] = swap(rests[kind(k)], "pcol", 2 * k)
        else:
            rest[k] = None
    for k in range(1, chips):
        if rest[k] is None:
            low = k & -k
            rest[k] = swap(rests[kind(k)], "pcol", 2 * k) if RELAY == 0 else swap(rest[k ^ low], "pcol", 2 * low)
    spread = [first] + [swap(first, "prow", k) for k in range(1, grid_rows)]
    keep, give = pick(spread)
    columns = [keep, swap(give, "pcol", 1)]
    firsts = [first, swap(first, "pcol", 1)]
    own_rest = [rest[k] for k in range(chips)]
    other_rest = [swap(x, "pcol", 1) for x in own_rest]
    renewed = renew(trailing, firsts, own_rest + other_rest, columns)
    return factor, renewed


RELAY = 1


def solution(mesh):
    placed = (
        P(None, "prow", "pcol", None),
        P(),
        P(None, "prow"),
        P(None, "prow", None, "pcol", None, None),
    )
    return jax.shard_map(
        body,
        mesh=mesh,
        in_specs=placed,
        out_specs=(P(None, "prow", "pcol", None), P(None, "prow", None, "pcol", None, None)),
        check_vma=False,
    )
```

time: 103 us -> 48.2 us (0.47)
  waiting for transfers between devices: 75.4 us -> 24.6 us
  between operations: 14.1 us -> 0.8 us
  starting transfers between devices: 0.08 us -> 12.6 us
  Pallas kernels: 0 us -> 7.77 us
  matrix products: 5.65 us -> 0 us
  local copies, waits for them, and re-layouts: 4.9 us -> 1.34 us
  other arithmetic: 2.72 us -> 0.87 us
    psum x1 -> x0, waiting for transfers between devices: 43.5 us -> none  [spread(): return lax.psum(jnp.where(mine, x, jnp.zeros_like(x)), axis)]
    all_gather x1 -> x0, waiting for transfers between devices: 31.9 us -> none  [body(): row_full = lax.all_gather(factor_strips, 'pcol', axis=1, tiled=True)]
    ppermute x0 -> x15, waiting for transfers between devices: none -> 24.6 us  [swap(): return lax.ppermute(x, axis, [(i, i ^ distance) for i in range(size)])]
    ppermute x0 -> x15, starting transfers between devices: none -> 12.6 us  [swap(): return lax.ppermute(x, axis, [(i, i ^ distance) for i in range(size)])]
    pallas_call x0 -> x3, Pallas kernels: none -> 7.77 us  [the longest x1 5.32 us: renew(): pl.pallas_call(functools.partial(renew_kernel, chips), out_shape=jax.Shap...]
    dot_general x2 -> x0, matrix products: 5.65 us -> none  [the longest x1 3.66 us: renew(): jnp.einsum('sna,tba->stnb', row_part, column_tiles, preferred_element_typ...]
    unnamed x6 -> x22, local copies, waits for them, and re-layouts: 4.9 us -> 1.34 us
  transfers between devices with their start and end apart: 2 -> 15, of which waited for: 2 -> 6; matrix products, arithmetic and copies ran while one was open for 2% -> 0% of each run, Pallas kernels for 0% -> 0%
where the time goes in v1:
time: 48.2 us; the launch traced here: 48 us
  waiting for transfers between devices  24.6 us (51%)
  starting transfers between devices  12.6 us (26%)
  Pallas kernels  7.77 us (16%)
  local copies, waits for them, and re-layouts  1.34 us (3%)
  other arithmetic  0.87 us (2%)
  between operations  0.8 us (2%)
    ppermute x15, waiting for transfers between devices, swap(): return lax.ppermute(x, axis, [(i, i ^ distance) for i in range(size)])  24.6 us
    ppermute x15, starting transfers between devices, swap(): return lax.ppermute(x, axis, [(i, i ^ distance) for i in range(size)])  12.6 us
    pallas_call x1, Pallas kernels, renew(): pl.pallas_call(functools.partial(renew_kernel, chips), out_shape=jax.Shap...  5.32 us
    pallas_call x1, Pallas kernels, solve(): pl.pallas_call(functools.partial(solve_kernel, classes), out_shape=[jax.S...  2.37 us
    unnamed x22, local copies, waits for them, and re-layouts  1.34 us
  transfers between devices with their start and end apart: 15, of which 6 were waited for; matrix products, arithmetic and copies ran while one was open for 0% of the time, Pallas kernels for 0%

profile of v1, /device:TPU:0, one launch (start us, length us, event | category | flops | bytes accessed | tf_op | source)
XLA Modules:
  0.0 48.0 jit_solution(1993043082759187860)
XLA Ops:
  0.6 2.4 %solve.1 = (bf16[4,1,64,512]{3,2,1,0:T(8,128)(2,1)}, bf16[64,512]{1,0:T(8,128)(2,1)}, bf16[64,512]{1,0:T(8,128)(2,1)}, bf16[3,64,512]{2,1,0:T(8,128)(2,1)}, bf16[3,64,512]{2,1,0:T(8,128)(2,1)}) custom-call(s32[4]{0:T(128)} %bitcast.9, bf16[4,1,64,512]{3,2,1,0:T(8,128)(2,1)} %panel.1, bf16[512,512]{1,0:T(8,128)(2,1)} %diag_inv.1), custom_call_target="tpu_custom_call" | custom-call | bytes 1024 | tf_op jit(solution)/shard_map/solve/pallas_call | solution.py:50
  3.0 3.1 %collective-permute-start = (bf16[64,512]{1,0:T(8,128)(2,1)}, bf16[64,512]{1,0:T(8,128)(2,1)S(1)}, u32[]{:S(2)}, u32[]{:S(2)}) collective-permute-start(bf16[64,512]{1,0:T(8,128)(2,1)} %get-tuple-element.10), channel_id=1, source_target_pairs={{0,2},{1,3},{2,0},{3,1},{4,6},{5,7},{6,4},{7,5},{8,10},{9,11},{10,... | collective-permute-start | bytes 196616 | tf_op jit(solution)/shard_map/ppermute | solution.py:20
  6.1 2.5 %collective-permute-start.2 = (bf16[64,512]{1,0:T(8,128)(2,1)}, bf16[64,512]{1,0:T(8,128)(2,1)S(1)}, u32[]{:S(2)}, u32[]{:S(2)}) collective-permute-start(bf16[64,512]{1,0:T(8,128)(2,1)} %get-tuple-element.11), channel_id=1, source_target_pairs={{0,6},{1,7},{2,4},{3,5},{4,2},{5,3},{6,0},{7,1},{8,14},{9,15},{10,... | collective-permute-start | bytes 196616 | tf_op jit(solution)/shard_map/ppermute | solution.py:20
  8.6 0.1 collective-permute-start.1
  8.7 4.5 %collective-permute-done.2 = bf16[64,512]{1,0:T(8,128)(2,1)S(1)} collective-permute-done((bf16[64,512]{1,0:T(8,128)(2,1)}, bf16[64,512]{1,0:T(8,128)(2,1)S(1)}, u32[]{:S(2)}, u32[]{:S(2)}) %collective-permute-start.2) | collective-permute-done | bytes 65568 | tf_op jit(solution)/shard_map/ppermute | solution.py:20
  13.2 2.1 %collective-permute-done.1 = bf16[64,512]{1,0:T(8,128)(2,1)S(1)} collective-permute-done((bf16[64,512]{1,0:T(8,128)(2,1)}, bf16[64,512]{1,0:T(8,128)(2,1)S(1)}, u32[]{:S(2)}, u32[]{:S(2)}) %collective-permute-start.1) | collective-permute-done | bytes 65568 | tf_op jit(solution)/shard_map/ppermute | solution.py:20
  15.2 0.9 %pad_maximum_fusion.refs_0_ = bf16[4,64,512]{2,1,0:T(8,128)(2,1)S(1)} fusion(bf16[1,64,512]{2,1,0:T(8,128)(2,1)S(1)} %bitcast.7, bf16[1,64,512]{2,1,0:T(8,128)(2,1)S(1)} %bitcast.8, bf16[1,64,512]{2,1,0:T(8,128)(2,1)S(1)} %bitcast.6, bf16[1,64,512]{2,1,0:T(8,128)(2,1)} %bitcast.5), kind=kLoop, calls=%fused_computation | loop fusion | flops 393216 | bytes 524288 | tf_op jit(solution)/shard_map/stack | solution.py:174
  16.1 2.5 %collective-permute-start.13 = (bf16[4,64,512]{2,1,0:T(8,128)(2,1)S(1)}, bf16[4,64,512]{2,1,0:T(8,128)(2,1)S(1)}, u32[]{:S(2)}, u32[]{:S(2)}) collective-permute-start(bf16[4,64,512]{2,1,0:T(8,128)(2,1)S(1)} %pad_maximum_fusion.refs_0_), channel_id=1, source_target_pairs={{0,24},{8,16},{16,8},{24,0},{1,25},{9,17},{17,9},{25,1},{2,26},{10... | collective-permute-start | bytes 786440 | tf_op jit(solution)/shard_map/ppermute | solution.py:20
  18.6 0.8 %collective-permute-start.5 = (bf16[3,64,512]{2,1,0:T(8,128)(2,1)}, bf16[3,64,512]{2,1,0:T(8,128)(2,1)S(1)}, u32[]{:S(2)}, u32[]{:S(2)}) collective-permute-start(bf16[3,64,512]{2,1,0:T(8,128)(2,1)} %get-tuple-element.13), channel_id=1, source_target_pairs={{0,4},{1,5},{2,6},{3,7},{4,0},{5,1},{6,2},{7,3},{8,12},{9,13},{10,... | collective-permute-start | bytes 589832 | tf_op jit(solution)/shard_map/ppermute | solution.py:20
  19.4 0.5 %collective-permute-start.12 = (bf16[4,64,512]{2,1,0:T(8,128)(2,1)S(1)}, bf16[4,64,512]{2,1,0:T(8,128)(2,1)S(1)}, u32[]{:S(2)}, u32[]{:S(2)}) collective-permute-start(bf16[4,64,512]{2,1,0:T(8,128)(2,1)S(1)} %pad_maximum_fusion.refs_0_), channel_id=1, source_target_pairs={{0,16},{8,24},{16,0},{24,8},{1,17},{9,25},{17,1},{25,9},{2,18},{10... | collective-permute-start | bytes 786440 | tf_op jit(solution)/shard_map/ppermute | solution.py:20
  20.0 0.5 %collective-permute-start.11 = (bf16[4,64,512]{2,1,0:T(8,128)(2,1)S(1)}, bf16[4,64,512]{2,1,0:T(8,128)(2,1)S(1)}, u32[]{:S(2)}, u32[]{:S(2)}) collective-permute-start(bf16[4,64,512]{2,1,0:T(8,128)(2,1)S(1)} %pad_maximum_fusion.refs_0_), channel_id=1, source_target_pairs={{0,8},{8,0},{16,24},{24,16},{1,9},{9,1},{17,25},{25,17},{2,10},{10... | collective-permute-start | bytes 786440 | tf_op jit(solution)/shard_map/ppermute | solution.py:20
  20.5 8.8 %collective-permute-done.5.refs_4_ = bf16[3,64,512]{2,1,0:T(8,128)(2,1)S(1)} collective-permute-done((bf16[3,64,512]{2,1,0:T(8,128)(2,1)}, bf16[3,64,512]{2,1,0:T(8,128)(2,1)S(1)}, u32[]{:S(2)}, u32[]{:S(2)}) %collective-permute-start.5) | collective-permute-done | bytes 196640 | tf_op jit(solution)/shard_map/ppermute | solution.py:20
  29.3 0.0 collective-permute-start.4
  29.3 0.0 collective-permute-done.13.refs_3_
  29.3 2.0 %collective-permute-start.6 = (bf16[3,64,512]{2,1,0:T(8,128)(2,1)S(1)}, bf16[3,64,512]{2,1,0:T(8,128)(2,1)S(1)}, u32[]{:S(2)}, u32[]{:S(2)}) collective-permute-start(bf16[3,64,512]{2,1,0:T(8,128)(2,1)S(1)} %collective-permute-done.5.refs_4_), channel_id=1, source_target_pairs={{0,2},{1,3},{2,0},{3,1},{4,6},{5,7},{6,4},{7,5},{8,10},{9,11},{10,... | collective-permute-start | bytes 589832 | tf_op jit(solution)/shard_map/ppermute | solution.py:20
  31.4 0.1 pick.1
  31.5 0.7 %copy-done.1 = bf16[4,64,512]{2,1,0:T(8,128)(2,1)} copy-done((bf16[4,64,512]{2,1,0:T(8,128)(2,1)}, bf16[4,64,512]{2,1,0:T(8,128)(2,1)S(1)}, u32[]{:S(2)}) %copy-start.1) | copy-done | bytes 262168
  32.2 0.5 %collective-permute-start.14 = (bf16[4,64,512]{2,1,0:T(8,128)(2,1)S(1)}, bf16[4,64,512]{2,1,0:T(8,128)(2,1)S(1)}, u32[]{:S(2)}, u32[]{:S(2)}) collective-permute-start(bf16[4,64,512]{2,1,0:T(8,128)(2,1)S(1)} %get-tuple-element.15), channel_id=1, source_target_pairs={{0,1},{1,0},{2,3},{3,2},{4,5},{5,4},{6,7},{7,6},{8,9},{9,8},{10,11... | collective-permute-start | bytes 786440 | tf_op jit(solution)/shard_map/ppermute | solution.py:20
  32.6 0.1 collective-permute-start.9
  32.7 4.6 %collective-permute-done.4.refs_3_ = bf16[3,64,512]{2,1,0:T(8,128)(2,1)S(1)} collective-permute-done((bf16[3,64,512]{2,1,0:T(8,128)(2,1)}, bf16[3,64,512]{2,1,0:T(8,128)(2,1)S(1)}, u32[]{:S(2)}, u32[]{:S(2)}) %collective-permute-start.4) | collective-permute-done | bytes 196640 | tf_op jit(solution)/shard_map/ppermute | solution.py:20
  37.3 3.3 %collective-permute-done.6.refs_5_ = bf16[3,64,512]{2,1,0:T(8,128)(2,1)S(1)} collective-permute-done((bf16[3,64,512]{2,1,0:T(8,128)(2,1)S(1)}, bf16[3,64,512]{2,1,0:T(8,128)(2,1)S(1)}, u32[]{:S(2)}, u32[]{:S(2)}) %collective-permute-start.6) | collective-permute-done | bytes 196640 | tf_op jit(solution)/shard_map/ppermute | solution.py:20
  40.7 1.4 %collective-permute-done.10.refs_9_ = bf16[3,64,512]{2,1,0:T(8,128)(2,1)S(1)} collective-permute-done((bf16[3,64,512]{2,1,0:T(8,128)(2,1)S(1)}, bf16[3,64,512]{2,1,0:T(8,128)(2,1)S(1)}, u32[]{:S(2)}, u32[]{:S(2)}) %collective-permute-start.10) | collective-permute-done | bytes 196640 | tf_op jit(solution)/shard_map/ppermute | solution.py:20
  42.1 0.6 %copy-done.10 = bf16[3,64,512]{2,1,0:T(8,128)(2,1)} copy-done((bf16[3,64,512]{2,1,0:T(8,128)(2,1)}, bf16[3,64,512]{2,1,0:T(8,128)(2,1)S(1)}, u32[]{:S(2)}) %copy-start.10) | copy-done | bytes 196632
  42.7 5.3 %renew.1 = bf16[4,1,1,1,512,512]{5,4,3,2,1,0:T(8,128)(2,1)} custom-call(bf16[4,64,512]{2,1,0:T(8,128)(2,1)} %copy-done, bf16[4,64,512]{2,1,0:T(8,128)(2,1)} %copy-done.2, bf16[3,64,512]{2,1,0:T(8,128)(2,1)} %get-tuple-element.12.refs_2_, bf16[3,64,512]{2,1,0:T(8,128)(2,1)} %copy-done.6, bf16[3,64,512]{2,1,0:T(8,128)(2,1)} %copy-done.4, ...), custom_call_target="tpu_custom_call" | custom-call | tf_op jit(solution)/shard_map/renew/pallas_call | solution.py:145
  (32 shorter events, 0.1 us)
Async XLA Ops:
  3.0 5.7 %collective-permute-start = (bf16[64,512]{1,0:T(8,128)(2,1)}, bf16[64,512]{1,0:T(8,128)(2,1)S(1)}, u32[]{:S(2)}, u32[]{:S(2)}) collective-permute-start(bf16[64,512]{1,0:T(8,128)(2,1)} %get-tuple-element.10), channel_id=1, source_target_pairs={{0,2},{1,3},{2,0},{3,1},{4,6},{5,7},{6,4},{7,5},{8,10},{9,11},{10,... | collective-permute-start | bytes 196616 | tf_op jit(solution)/shard_map/ppermute | solution.py:20
  6.1 7.1 %collective-permute-start.2 = (bf16[64,512]{1,0:T(8,128)(2,1)}, bf16[64,512]{1,0:T(8,128)(2,1)S(1)}, u32[]{:S(2)}, u32[]{:S(2)}) collective-permute-start(bf16[64,512]{1,0:T(8,128)(2,1)} %get-tuple-element.11), channel_id=1, source_target_pairs={{0,6},{1,7},{2,4},{3,5},{4,2},{5,3},{6,0},{7,1},{8,14},{9,15},{10,... | collective-permute-start | bytes 196616 | tf_op jit(solution)/shard_map/ppermute | solution.py:20
  8.6 6.7 %collective-permute-start.1 = (bf16[64,512]{1,0:T(8,128)(2,1)}, bf16[64,512]{1,0:T(8,128)(2,1)S(1)}, u32[]{:S(2)}, u32[]{:S(2)}) collective-permute-start(bf16[64,512]{1,0:T(8,128)(2,1)} %get-tuple-element.11), channel_id=1, source_target_pairs={{0,4},{1,5},{2,6},{3,7},{4,0},{5,1},{6,2},{7,3},{8,12},{9,13},{10,... | collective-permute-start | bytes 196616 | tf_op jit(solution)/shard_map/ppermute | solution.py:20
  16.1 25.9 %copy-start = (bf16[4,64,512]{2,1,0:T(8,128)(2,1)}, bf16[4,64,512]{2,1,0:T(8,128)(2,1)S(1)}, u32[]{:S(2)}) copy-start(bf16[4,64,512]{2,1,0:T(8,128)(2,1)S(1)} %pad_maximum_fusion.refs_0_) | copy-start | bytes 786436
  16.1 13.2 %collective-permute-start.13 = (bf16[4,64,512]{2,1,0:T(8,128)(2,1)S(1)}, bf16[4,64,512]{2,1,0:T(8,128)(2,1)S(1)}, u32[]{:S(2)}, u32[]{:S(2)}) collective-permute-start(bf16[4,64,512]{2,1,0:T(8,128)(2,1)S(1)} %pad_maximum_fusion.refs_0_), channel_id=1, source_target_pairs={{0,24},{8,16},{16,8},{24,0},{1,25},{9,17},{17,9},{25,1},{2,26},{10... | collective-permute-start | bytes 786440 | tf_op jit(solution)/shard_map/ppermute | solution.py:20
  18.6 10.7 %collective-permute-start.5 = (bf16[3,64,512]{2,1,0:T(8,128)(2,1)}, bf16[3,64,512]{2,1,0:T(8,128)(2,1)S(1)}, u32[]{:S(2)}, u32[]{:S(2)}) collective-permute-start(bf16[3,64,512]{2,1,0:T(8,128)(2,1)} %get-tuple-element.13), channel_id=1, source_target_pairs={{0,4},{1,5},{2,6},{3,7},{4,0},{5,1},{6,2},{7,3},{8,12},{9,13},{10,... | collective-permute-start | bytes 589832 | tf_op jit(solution)/shard_map/ppermute | solution.py:20
  19.4 11.9 %collective-permute-start.12 = (bf16[4,64,512]{2,1,0:T(8,128)(2,1)S(1)}, bf16[4,64,512]{2,1,0:T(8,128)(2,1)S(1)}, u32[]{:S(2)}, u32[]{:S(2)}) collective-permute-start(bf16[4,64,512]{2,1,0:T(8,128)(2,1)S(1)} %pad_maximum_fusion.refs_0_), channel_id=1, source_target_pairs={{0,16},{8,24},{16,0},{24,8},{1,17},{9,25},{17,1},{25,9},{2,18},{10... | collective-permute-start | bytes 786440 | tf_op jit(solution)/shard_map/ppermute | solution.py:20
  20.0 11.4 %collective-permute-start.11 = (bf16[4,64,512]{2,1,0:T(8,128)(2,1)S(1)}, bf16[4,64,512]{2,1,0:T(8,128)(2,1)S(1)}, u32[]{:S(2)}, u32[]{:S(2)}) collective-permute-start(bf16[4,64,512]{2,1,0:T(8,128)(2,1)S(1)} %pad_maximum_fusion.refs_0_), channel_id=1, source_target_pairs={{0,8},{8,0},{16,24},{24,16},{1,9},{9,1},{17,25},{25,17},{2,10},{10... | collective-permute-start | bytes 786440 | tf_op jit(solution)/shard_map/ppermute | solution.py:20
  20.5 12.2 %collective-permute-start.7 = (bf16[3,64,512]{2,1,0:T(8,128)(2,1)}, bf16[3,64,512]{2,1,0:T(8,128)(2,1)S(1)}, u32[]{:S(2)}, u32[]{:S(2)}) collective-permute-start(bf16[3,64,512]{2,1,0:T(8,128)(2,1)} %get-tuple-element.12.refs_2_), channel_id=1, source_target_pairs={{0,1},{1,0},{2,3},{3,2},{4,5},{5,4},{6,7},{7,6},{8,9},{9,8},{10,11... | collective-permute-start | bytes 589832 | tf_op jit(solution)/shard_map/ppermute | solution.py:20
  29.3 12.7 %copy-start.4 = (bf16[3,64,512]{2,1,0:T(8,128)(2,1)}, bf16[3,64,512]{2,1,0:T(8,128)(2,1)S(1)}, u32[]{:S(2)}) copy-start(bf16[3,64,512]{2,1,0:T(8,128)(2,1)S(1)} %collective-permute-done.5.refs_4_) | copy-start | bytes 589828
  29.3 8.0 %collective-permute-start.4 = (bf16[3,64,512]{2,1,0:T(8,128)(2,1)}, bf16[3,64,512]{2,1,0:T(8,128)(2,1)S(1)}, u32[]{:S(2)}, u32[]{:S(2)}) collective-permute-start(bf16[3,64,512]{2,1,0:T(8,128)(2,1)} %get-tuple-element.12.refs_2_), channel_id=1, source_target_pairs={{0,2},{1,3},{2,0},{3,1},{4,6},{5,7},{6,4},{7,5},{8,10},{9,11},{10,... | collective-permute-start | bytes 589832 | tf_op jit(solution)/shard_map/ppermute | solution.py:20
  29.3 11.2 %collective-permute-start.6 = (bf16[3,64,512]{2,1,0:T(8,128)(2,1)S(1)}, bf16[3,64,512]{2,1,0:T(8,128)(2,1)S(1)}, u32[]{:S(2)}, u32[]{:S(2)}) collective-permute-start(bf16[3,64,512]{2,1,0:T(8,128)(2,1)S(1)} %collective-permute-done.5.refs_4_), channel_id=1, source_target_pairs={{0,2},{1,3},{2,0},{3,1},{4,6},{5,7},{6,4},{7,5},{8,10},{9,11},{10,... | collective-permute-start | bytes 589832 | tf_op jit(solution)/shard_map/ppermute | solution.py:20
  31.4 9.2 %collective-permute-start.3 = (bf16[4,64,512]{2,1,0:T(8,128)(2,1)S(1)}, bf16[4,64,512]{2,1,0:T(8,128)(2,1)S(1)}, u32[]{:S(2)}, u32[]{:S(2)}) collective-permute-start(bf16[4,64,512]{2,1,0:T(8,128)(2,1)S(1)} %pad_maximum_fusion.refs_0_), channel_id=1, source_target_pairs={{0,1},{1,0},{2,3},{3,2},{4,5},{5,4},{6,7},{7,6},{8,9},{9,8},{10,11... | collective-permute-start | bytes 786440 | tf_op jit(solution)/shard_map/ppermute | solution.py:20
  32.2 8.5 %collective-permute-start.14 = (bf16[4,64,512]{2,1,0:T(8,128)(2,1)S(1)}, bf16[4,64,512]{2,1,0:T(8,128)(2,1)S(1)}, u32[]{:S(2)}, u32[]{:S(2)}) collective-permute-start(bf16[4,64,512]{2,1,0:T(8,128)(2,1)S(1)} %get-tuple-element.15), channel_id=1, source_target_pairs={{0,1},{1,0},{2,3},{3,2},{4,5},{5,4},{6,7},{7,6},{8,9},{9,8},{10,11... | collective-permute-start | bytes 786440 | tf_op jit(solution)/shard_map/ppermute | solution.py:20
  32.6 9.4 %copy-start.5 = (bf16[3,64,512]{2,1,0:T(8,128)(2,1)}, bf16[3,64,512]{2,1,0:T(8,128)(2,1)S(1)}, u32[]{:S(2)}) copy-start(bf16[3,64,512]{2,1,0:T(8,128)(2,1)S(1)} %collective-permute-done.7.refs_6_) | copy-start | bytes 589828
  32.6 7.9 %collective-permute-start.9 = (bf16[3,64,512]{2,1,0:T(8,128)(2,1)S(1)}, bf16[3,64,512]{2,1,0:T(8,128)(2,1)S(1)}, u32[]{:S(2)}, u32[]{:S(2)}) collective-permute-start(bf16[3,64,512]{2,1,0:T(8,128)(2,1)S(1)} %collective-permute-done.5.refs_4_), channel_id=1, source_target_pairs={{0,1},{1,0},{2,3},{3,2},{4,5},{5,4},{6,7},{7,6},{8,9},{9,8},{10,11... | collective-permute-start | bytes 589832 | tf_op jit(solution)/shard_map/ppermute | solution.py:20
  37.3 4.7 %copy-start.6 = (bf16[3,64,512]{2,1,0:T(8,128)(2,1)}, bf16[3,64,512]{2,1,0:T(8,128)(2,1)S(1)}, u32[]{:S(2)}) copy-start(bf16[3,64,512]{2,1,0:T(8,128)(2,1)S(1)} %collective-permute-done.4.refs_3_) | copy-start | bytes 589828
  37.3 3.3 %collective-permute-start.8 = (bf16[3,64,512]{2,1,0:T(8,128)(2,1)S(1)}, bf16[3,64,512]{2,1,0:T(8,128)(2,1)S(1)}, u32[]{:S(2)}, u32[]{:S(2)}) collective-permute-start(bf16[3,64,512]{2,1,0:T(8,128)(2,1)S(1)} %collective-permute-done.4.refs_3_), channel_id=1, source_target_pairs={{0,1},{1,0},{2,3},{3,2},{4,5},{5,4},{6,7},{7,6},{8,9},{9,8},{10,11... | collective-permute-start | bytes 589832 | tf_op jit(solution)/shard_map/ppermute | solution.py:20
  40.6 1.5 %copy-start.7 = (bf16[3,64,512]{2,1,0:T(8,128)(2,1)}, bf16[3,64,512]{2,1,0:T(8,128)(2,1)S(1)}, u32[]{:S(2)}) copy-start(bf16[3,64,512]{2,1,0:T(8,128)(2,1)S(1)} %collective-permute-done.6.refs_5_) | copy-start | bytes 589828
  40.6 1.4 %collective-permute-start.10 = (bf16[3,64,512]{2,1,0:T(8,128)(2,1)S(1)}, bf16[3,64,512]{2,1,0:T(8,128)(2,1)S(1)}, u32[]{:S(2)}, u32[]{:S(2)}) collective-permute-start(bf16[3,64,512]{2,1,0:T(8,128)(2,1)S(1)} %collective-permute-done.6.refs_5_), channel_id=1, source_target_pairs={{0,1},{1,0},{2,3},{3,2},{4,5},{5,4},{6,7},{7,6},{8,9},{9,8},{10,11... | collective-permute-start | bytes 589832 | tf_op jit(solution)/shard_map/ppermute | solution.py:20
  40.6 1.5 %copy-start.2 = (bf16[4,64,512]{2,1,0:T(8,128)(2,1)}, bf16[4,64,512]{2,1,0:T(8,128)(2,1)S(1)}, u32[]{:S(2)}) copy-start(bf16[4,64,512]{2,1,0:T(8,128)(2,1)S(1)} %collective-permute-done.3.refs_1_) | copy-start | bytes 786436
  40.6 1.5 %copy-start.8 = (bf16[3,64,512]{2,1,0:T(8,128)(2,1)}, bf16[3,64,512]{2,1,0:T(8,128)(2,1)S(1)}, u32[]{:S(2)}) copy-start(bf16[3,64,512]{2,1,0:T(8,128)(2,1)S(1)} %collective-permute-done.9.refs_8_) | copy-start | bytes 589828
  40.6 1.4 %copy-start.9 = (bf16[3,64,512]{2,1,0:T(8,128)(2,1)}, bf16[3,64,512]{2,1,0:T(8,128)(2,1)S(1)}, u32[]{:S(2)}) copy-start(bf16[3,64,512]{2,1,0:T(8,128)(2,1)S(1)} %collective-permute-done.8.refs_7_) | copy-start | bytes 589828
  40.6 1.4 %copy-start.3 = (bf16[4,64,512]{2,1,0:T(8,128)(2,1)}, bf16[4,64,512]{2,1,0:T(8,128)(2,1)S(1)}, u32[]{:S(2)}) copy-start(bf16[4,64,512]{2,1,0:T(8,128)(2,1)S(1)} %collective-permute-done.14.refs_11_) | copy-start | bytes 786436
  (2 other events, 1.4 us)

commit v2 on v1

v2 whole, which is shorter than its diff:
```python
import functools

import jax
import jax.numpy as jnp
from jax import lax
from jax.experimental import pallas as pl
from jax.experimental.pallas import tpu as pltpu
from jax.sharding import PartitionSpec as P

TRANSPOSED = (((1,), (1,)), ((), ()))
HBM = pl.BlockSpec(memory_space=pl.ANY)
VMEM = pl.BlockSpec(memory_space=pltpu.VMEM)
SMEM = pl.BlockSpec(memory_space=pltpu.SMEM)
LIMIT = 16 * 1024 * 1024
SOLVE = 62914560
SMALL = 8 * 1024 * 1024


def swap(x, axis, distance):
    size = lax.axis_size(axis)
    return lax.ppermute(x, axis, [(i, i ^ distance) for i in range(size)])


def solve_kernel(classes, nonzero, panel, diag_inv, factor, *refs):
    slabs, rests = refs[:classes], refs[classes:2 * classes]
    live, strips, inverse, sems = refs[2 * classes:]
    copies = [pltpu.make_async_copy(*pair, sems.at[n])
              for n, pair in enumerate(((nonzero, live), (panel, strips), (diag_inv, inverse)))]
    for copy in copies:
        copy.start()
    for copy in copies:
        copy.wait()
    steps, _, rows, size = strips.shape
    tiles_in = strips[...].reshape(steps * rows, size)
    product = lax.dot_general(tiles_in, inverse[...], TRANSPOSED, preferred_element_type=jnp.float32)
    product = product.reshape(steps, rows, size)
    for s in range(steps):
        factor[s, 0] = (product[s] * live[s].astype(jnp.float32)).astype(factor.dtype)
    own = lax.axis_index("pcol") // lax.axis_size("prow")
    for n in range(classes):
        first = jnp.bitwise_xor(own, n)
        slabs[n][0] = factor[first, 0]
        for m in range(1, steps):
            rests[n][m - 1] = factor[lax.rem(first + m, steps), 0]


def solve(panel, diag_inv, nonzero, classes):
    steps, _, rows, size = panel.shape
    slab = jax.ShapeDtypeStruct((1, rows, size), panel.dtype)
    rest = jax.ShapeDtypeStruct((steps - 1, rows, size), panel.dtype)
    outs = pl.pallas_call(
        functools.partial(solve_kernel, classes),
        out_shape=[jax.ShapeDtypeStruct(panel.shape, panel.dtype)] + [slab] * classes + [rest] * classes,
        in_specs=[pl.BlockSpec(memory_space=pltpu.HBM)] * 3,
        out_specs=[VMEM] * (1 + 2 * classes),
        scratch_shapes=[
            pltpu.SMEM(nonzero[:, 0].shape, nonzero.dtype),
            pltpu.VMEM(panel.shape, panel.dtype),
            pltpu.VMEM(diag_inv.shape, diag_inv.dtype),
            pltpu.SemaphoreType.DMA((3,)),
        ],
        cost_estimate=pl.CostEstimate(flops=0, bytes_accessed=1024, transcendentals=0),
        compiler_params=pltpu.CompilerParams(vmem_limit_bytes=SOLVE),
        name="solve",
    )(nonzero[:, 0], panel, diag_inv)
    return outs[0], outs[1:1 + classes], outs[1 + classes:]


def pick_kernel(sources, *refs):
    ins, (keep, packed) = refs[:sources], refs[sources:]
    span = ins[0].shape[0]
    c, r = lax.axis_index("pcol"), lax.axis_index("prow")
    packed[span:] = ins[0][...]
    for k in range(sources):
        @pl.when(jnp.bitwise_xor(r, lax.rem(c, sources)) == k)
        def _():
            keep[...] = ins[k][...]

        @pl.when(jnp.bitwise_xor(r, lax.rem(jnp.bitwise_xor(c, 1), sources)) == k)
        def _():
            packed[:span] = ins[k][...]


def pick(slabs):
    span, *rest = slabs[0].shape
    outs = [jax.ShapeDtypeStruct(slabs[0].shape, slabs[0].dtype), jax.ShapeDtypeStruct((2 * span, *rest), slabs[0].dtype)]
    return small_call(functools.partial(pick_kernel, len(slabs)), outs, slabs, "pick")


def small_call(kernel, outs, args, name):
    return pl.pallas_call(
        kernel,
        out_shape=outs,
        in_specs=[VMEM] * len(args),
        out_specs=jax.tree.map(lambda _: VMEM, outs),
        cost_estimate=pl.CostEstimate(flops=0, bytes_accessed=1024, transcendentals=0),
        compiler_params=pltpu.CompilerParams(vmem_limit_bytes=SMALL),
        name=name,
    )(*args)


def choose_kernel(bit, mine, came, out):
    away = jnp.bitwise_xor(lax.axis_index("prow"), lax.rem(lax.axis_index("pcol"), lax.axis_size("prow")))
    here = jnp.bitwise_and(away, bit) == 0

    @pl.when(here)
    def _():
        out[...] = mine[...]

    @pl.when(jnp.logical_not(here))
    def _():
        out[...] = came[...]


def choose(bit, mine, came):
    shape = jax.ShapeDtypeStruct(mine.shape, mine.dtype)
    return small_call(functools.partial(choose_kernel, bit), shape, (mine, came), "choose")


def pack_kernel(mine, came, first, keep, packed):
    span = first.shape[0]
    here = lax.rem(lax.axis_index("prow"), 2) == lax.rem(lax.axis_index("pcol"), 2)
    packed[span:] = first[...]

    @pl.when(here)
    def _():
        keep[...] = mine[...]
        packed[:span] = came[...]

    @pl.when(jnp.logical_not(here))
    def _():
        keep[...] = came[...]
        packed[:span] = mine[...]


def pack(mine, came, first):
    span, *rest = first.shape
    outs = [jax.ShapeDtypeStruct(first.shape, first.dtype), jax.ShapeDtypeStruct((2 * span, *rest), first.dtype)]
    return small_call(pack_kernel, outs, (mine, came, first), "pack")


def join_kernel(*refs):
    at = 0
    for ref in refs[:-1]:
        refs[-1][at:at + ref.shape[0]] = ref[...]
        at += ref.shape[0]


def join(parts):
    total = sum(x.shape[0] for x in parts)
    return small_call(join_kernel, jax.ShapeDtypeStruct((total, *parts[0].shape[1:]), parts[0].dtype), parts, "join")


def hold_kernel(x, _, out):
    del x, out


def hold(x, until):
    return pl.pallas_call(
        hold_kernel,
        out_shape=jax.ShapeDtypeStruct(x.shape, x.dtype),
        in_specs=[HBM, HBM],
        out_specs=HBM,
        input_output_aliases={0: 0},
        cost_estimate=pl.CostEstimate(flops=0, bytes_accessed=1024, transcendentals=0),
        compiler_params=pltpu.CompilerParams(vmem_limit_bytes=SMALL),
        name="hold",
    )(x, until)


def renew_kernel(chips, groups, *refs):
    firsts, keeps, gots = refs[:groups], refs[groups:2 * groups], refs[2 * groups:3 * groups]
    rests, others = refs[3 * groups:3 * groups + chips - 1], refs[3 * groups + chips - 1:-6]
    trailing, out, rows_full, column, held, out_sems = refs[-6:]
    steps = held.shape[0]
    span, rows = firsts[0].shape[0], firsts[0].shape[1]
    c, r = lax.axis_index("pcol"), lax.axis_index("prow")
    grid_rows = lax.axis_size("prow")
    own = c // grid_rows
    order = [lax.rem(own + m, steps) for m in range(steps)]
    for core in range(2):
        for k in range(chips):
            source = jnp.bitwise_xor(c, 2 * k + core)
            here = pl.ds(pl.multiple_of(source * rows, rows), rows)
            n, at = k // span, k % span
            if core == 0:
                column[here] = keeps[n][at]
                rows_full[0, here] = firsts[n][at]
            else:
                column[here] = gots[n][at]
                rows_full[0, here] = gots[n][span + at]
            for m in range(1, steps):
                parts = (rests, others)[core]
                rows_full[m, here] = parts[0][k * (steps - 1) + m - 1] if k < 2 else parts[k - 1][m - 1]
    for m in range(steps):
        active = order[m] * grid_rows + r >= c

        @pl.when(active)
        def _():
            product = lax.dot_general(rows_full[m], column[...], TRANSPOSED, preferred_element_type=jnp.float32)
            before = trailing[order[m], 0, 0, 0].astype(jnp.float32)
            held[m] = (before - product).astype(held.dtype)

        @pl.when(jnp.logical_not(active))
        def _():
            held[m] = trailing[order[m], 0, 0, 0]

        pltpu.make_async_copy(held.at[m], out.at[order[m], 0, 0, 0], out_sems.at[m]).start()
    for m in range(steps):
        pltpu.make_async_copy(held.at[m], out.at[order[m], 0, 0, 0], out_sems.at[m]).wait()


def renew(trailing, firsts, keeps, gots, rests, others):
    chips, groups = len(rests) + 1, len(firsts)
    steps, size = trailing.shape[0], trailing.shape[-1]
    tiles = pltpu.VMEM((steps, size, size), trailing.dtype)
    args = (*firsts, *keeps, *gots, *rests, *others, trailing)
    return pl.pallas_call(
        functools.partial(renew_kernel, chips, groups),
        out_shape=jax.ShapeDtypeStruct(trailing.shape, trailing.dtype),
        in_specs=[VMEM] * len(args),
        out_specs=HBM,
        scratch_shapes=[
            tiles,
            pltpu.VMEM((size, size), trailing.dtype),
            tiles,
            pltpu.SemaphoreType.DMA((steps,)),
        ],
        compiler_params=pltpu.CompilerParams(vmem_limit_bytes=LIMIT),
        name="renew",
    )(*args)


def body(panel, diag_inv, nonzero, trailing):
    grid_rows, grid_cols = lax.axis_size("prow"), lax.axis_size("pcol")
    chips = grid_cols // 2
    classes = max(1, grid_cols // grid_rows)
    factor, slabs, rests = solve(panel, diag_inv, nonzero, classes)
    slabs, rests = list(slabs), list(rests)

    def kind(k):
        return 2 * k // grid_rows

    def gather(parts, relay, gates):
        held = [parts[0]]
        for k in range(1, chips):
            low = k & -k
            relayed = relay and low != k and kind(low) == 0
            if k in gates:
                if relayed:
                    held[k ^ low] = hold(held[k ^ low], gates[k](held))
                else:
                    parts[kind(k)] = hold(parts[kind(k)], gates[k](held))
                    held[0] = parts[0]
            source = held[k ^ low] if relayed else parts[kind(k)]
            held.append(swap(source, "pcol", 2 * low if relayed else 2 * k))
        return held

    top = chips // 2
    near = gather(slabs, PREL, {top + 1: lambda held: held[1]} if G3 else {})
    half = max(1, chips // GROUPS)
    firsts = [join(near[n:n + half]) for n in range(0, chips, half)]
    marks = {"p1": near[1], "p2": near[top], "p3": near[-1], "b": firsts[-1], "a": firsts[0]}
    gates = {}
    if G2:
        gates[top] = lambda held: marks[G2]
    if G1:
        gates[1] = lambda held: marks[G1]
    rest = gather(rests, QREL, gates)
    keeps, gots = [], []
    for first in firsts:
        if XY == "hyper":
            mine = first
            bit = grid_rows // 2
            while bit > 1:
                mine = choose(bit, mine, swap(mine, "prow", bit))
                bit //= 2
            keep, packed = pack(mine, swap(mine, "prow", 1), first)
        else:
            keep, packed = pick([first] + [swap(first, "prow", k) for k in range(1, grid_rows)])
        keeps.append(keep)
        gots.append(swap(packed, "pcol", 1))
    pair = join(rest[:2])
    others = [swap(pair, "pcol", 1)] + [swap(x, "pcol", 1) for x in rest[2:]]
    renewed = renew(trailing, firsts, keeps, gots, [pair] + rest[2:], others)
    return factor, renewed


PREL = True
QREL = True
GROUPS = 2
G1 = None
G2 = None
G3 = False
XY = 'hyper'


def solution(mesh):
    placed = (
        P(None, "prow", "pcol", None),
        P(),
        P(None, "prow"),
        P(None, "prow", None, "pcol", None, None),
    )
    return jax.shard_map(
        body,
        mesh=mesh,
        in_specs=placed,
        out_specs=(P(None, "prow", "pcol", None), P(None, "prow", None, "pcol", None, None)),
        check_vma=False,
    )
```

time: 48.2 us -> 34.7 us (0.72)
  the two profiles are of different devices: /device:TPU:0 before, /device:TPU:21 now
where the time goes in v2:
time: 34.7 us; the launch traced here: 34.5 us
  starting transfers between devices  21.5 us (62%)
  Pallas kernels  5.25 us (15%)
  waiting for transfers between devices  5.24 us (15%)
  local copies, waits for them, and re-layouts  1.77 us (5%)
  between operations  0.7 us (2%)
    ppermute x15, starting transfers between devices, swap(): return lax.ppermute(x, axis, [(i, i ^ distance) for i in range(size)])  21.5 us
    ppermute x15, waiting for transfers between devices, swap(): return lax.ppermute(x, axis, [(i, i ^ distance) for i in range(size)])  5.24 us
    pallas_call x1, Pallas kernels, renew(): pl.pallas_call(functools.partial(renew_kernel, chips, groups), out_shape=...  2.62 us
    pallas_call x1, Pallas kernels, solve(): pl.pallas_call(functools.partial(solve_kernel, classes), out_shape=[jax.S...  2.5 us
    unnamed x6, local copies, waits for them, and re-layouts  1.77 us
  transfers between devices with their start and end apart: 15, of which 5 were waited for; matrix products, arithmetic and copies ran while one was open for 0% of the time, Pallas kernels for 0%

profile of v2, /device:TPU:21, one launch (start us, length us, event | category | flops | bytes accessed | tf_op | source)
XLA Modules:
  0.0 34.5 jit_solution(11612133565347201892)
XLA Ops:
  0.6 2.5 %solve.1 = (bf16[4,1,64,512]{3,2,1,0:T(8,128)(2,1)}, bf16[1,64,512]{2,1,0:T(8,128)(2,1)}, bf16[1,64,512]{2,1,0:T(8,128)(2,1)}, bf16[3,64,512]{2,1,0:T(8,128)(2,1)}, bf16[3,64,512]{2,1,0:T(8,128)(2,1)}) custom-call(s32[4]{0:T(128)} %bitcast.1, bf16[4,1,64,512]{3,2,1,0:T(8,128)(2,1)} %panel.1, bf16[512,512]{1,0:T(8,128)(2,1)} %diag_inv.1), custom_call_target="tpu_custom_call" | custom-call | bytes 1024 | tf_op jit(solution)/shard_map/solve/pallas_call | solution.py:51
  3.2 0.1 collective-permute-start.1
  3.3 1.3 %collective-permute-start = (bf16[1,64,512]{2,1,0:T(8,128)(2,1)}, bf16[1,64,512]{2,1,0:T(8,128)(2,1)S(1)}, u32[]{:S(2)}, u32[]{:S(2)}) collective-permute-start(bf16[1,64,512]{2,1,0:T(8,128)(2,1)} %get-tuple-element.12.refs_0_), channel_id=1, source_target_pairs={{0,2},{1,3},{2,0},{3,1},{4,6},{5,7},{6,4},{7,5},{8,10},{9,11},{10,... | collective-permute-start | bytes 196616 | tf_op jit(solution)/shard_map/ppermute | solution.py:21
  4.6 2.3 %collective-permute-start.10 = (bf16[3,64,512]{2,1,0:T(8,128)(2,1)}, bf16[3,64,512]{2,1,0:T(8,128)(2,1)S(1)}, u32[]{:S(2)}, u32[]{:S(2)}) collective-permute-start(bf16[3,64,512]{2,1,0:T(8,128)(2,1)} %get-tuple-element.19), channel_id=1, source_target_pairs={{0,4},{1,5},{2,6},{3,7},{4,0},{5,1},{6,2},{7,3},{8,12},{9,13},{10,... | collective-permute-start | bytes 589832 | tf_op jit(solution)/shard_map/ppermute | solution.py:21
  6.9 0.6 %collective-permute-done.1.refs_0_ = bf16[1,64,512]{2,1,0:T(8,128)(2,1)S(1)} collective-permute-done((bf16[1,64,512]{2,1,0:T(8,128)(2,1)}, bf16[1,64,512]{2,1,0:T(8,128)(2,1)S(1)}, u32[]{:S(2)}, u32[]{:S(2)}) %collective-permute-start.1) | collective-permute-done | bytes 65568 | tf_op jit(solution)/shard_map/ppermute | solution.py:21
  7.5 3.0 %collective-permute-start.2 = (bf16[1,64,512]{2,1,0:T(8,128)(2,1)S(1)}, bf16[1,64,512]{2,1,0:T(8,128)(2,1)S(1)}, u32[]{:S(2)}, u32[]{:S(2)}) collective-permute-start(bf16[1,64,512]{2,1,0:T(8,128)(2,1)S(1)} %collective-permute-done.1.refs_0_), channel_id=1, source_target_pairs={{0,2},{1,3},{2,0},{3,1},{4,6},{5,7},{6,4},{7,5},{8,10},{9,11},{10,... | collective-permute-start | bytes 196616 | tf_op jit(solution)/shard_map/ppermute | solution.py:21
  10.5 0.0 collective-permute-start.9
  10.6 0.8 %copy-done.2 = bf16[1,64,512]{2,1,0:T(8,128)(2,1)S(1)} copy-done((bf16[1,64,512]{2,1,0:T(8,128)(2,1)S(1)}, bf16[1,64,512]{2,1,0:T(8,128)(2,1)}, u32[]{:S(2)}) %copy-start.2) | copy-done | bytes 65560
  11.4 0.3 collective-permute-start.3
  11.7 1.5 %collective-permute-done.2.refs_1_ = bf16[1,64,512]{2,1,0:T(8,128)(2,1)S(1)} collective-permute-done((bf16[1,64,512]{2,1,0:T(8,128)(2,1)S(1)}, bf16[1,64,512]{2,1,0:T(8,128)(2,1)S(1)}, u32[]{:S(2)}, u32[]{:S(2)}) %collective-permute-start.2) | collective-permute-done | bytes 65568 | tf_op jit(solution)/shard_map/ppermute | solution.py:21
  13.3 0.3 collective-permute-start.5
  13.6 1.9 %collective-permute-done.3.came = bf16[2,64,512]{2,1,0:T(8,128)(2,1)S(1)} collective-permute-done((bf16[2,64,512]{2,1,0:T(8,128)(2,1)S(1)}, bf16[2,64,512]{2,1,0:T(8,128)(2,1)S(1)}, u32[]{:S(2)}, u32[]{:S(2)}) %collective-permute-start.3) | collective-permute-done | bytes 131104 | tf_op jit(solution)/shard_map/ppermute | solution.py:21
  15.4 1.3 %collective-permute-start.4 = (bf16[2,64,512]{2,1,0:T(8,128)(2,1)S(1)}, bf16[2,64,512]{2,1,0:T(8,128)(2,1)S(1)}, u32[]{:S(2)}, u32[]{:S(2)}) collective-permute-start(bf16[2,64,512]{2,1,0:T(8,128)(2,1)S(1)} %choose.2.mine), channel_id=1, source_target_pairs={{0,8},{8,0},{16,24},{24,16},{1,9},{9,1},{17,25},{25,17},{2,10},{10... | collective-permute-start | bytes 393224 | tf_op jit(solution)/shard_map/ppermute | solution.py:21
  16.7 2.3 %collective-permute-start.11 = (bf16[3,64,512]{2,1,0:T(8,128)(2,1)S(1)}, bf16[3,64,512]{2,1,0:T(8,128)(2,1)S(1)}, u32[]{:S(2)}, u32[]{:S(2)}) collective-permute-start(bf16[3,64,512]{2,1,0:T(8,128)(2,1)S(1)} %collective-permute-done.10.refs_7_), channel_id=1, source_target_pairs={{0,2},{1,3},{2,0},{3,1},{4,6},{5,7},{6,4},{7,5},{8,10},{9,11},{10,... | collective-permute-start | bytes 589832 | tf_op jit(solution)/shard_map/ppermute | solution.py:21
  19.1 1.3 %collective-permute-start.6 = (bf16[2,64,512]{2,1,0:T(8,128)(2,1)S(1)}, bf16[2,64,512]{2,1,0:T(8,128)(2,1)S(1)}, u32[]{:S(2)}, u32[]{:S(2)}) collective-permute-start(bf16[2,64,512]{2,1,0:T(8,128)(2,1)S(1)} %choose.3.mine), channel_id=1, source_target_pairs={{0,8},{8,0},{16,24},{24,16},{1,9},{9,1},{17,25},{25,17},{2,10},{10... | collective-permute-start | bytes 393224 | tf_op jit(solution)/shard_map/ppermute | solution.py:21
  20.4 0.9 %copy-done.1 = bf16[3,64,512]{2,1,0:T(8,128)(2,1)S(1)} copy-done((bf16[3,64,512]{2,1,0:T(8,128)(2,1)S(1)}, bf16[3,64,512]{2,1,0:T(8,128)(2,1)}, u32[]{:S(2)}) %copy-start.1) | copy-done | bytes 196632
  21.3 5.3 %collective-permute-start.12 = (bf16[6,64,512]{2,1,0:T(8,128)(2,1)S(1)}, bf16[6,64,512]{2,1,0:T(8,128)(2,1)S(1)}, u32[]{:S(2)}, u32[]{:S(2)}) collective-permute-start(bf16[6,64,512]{2,1,0:T(8,128)(2,1)S(1)} %join.5.refs_6_), channel_id=1, source_target_pairs={{0,1},{1,0},{2,3},{3,2},{4,5},{5,4},{6,7},{7,6},{8,9},{9,8},{10,11... | collective-permute-start | bytes 1179656 | tf_op jit(solution)/shard_map/ppermute | solution.py:21
  26.6 0.1 collective-permute-start.7
  26.8 3.3 %collective-permute-start.8 = (bf16[4,64,512]{2,1,0:T(8,128)(2,1)S(1)}, bf16[4,64,512]{2,1,0:T(8,128)(2,1)S(1)}, u32[]{:S(2)}, u32[]{:S(2)}) collective-permute-start(bf16[4,64,512]{2,1,0:T(8,128)(2,1)S(1)} %get-tuple-element.17), channel_id=1, source_target_pairs={{0,1},{1,0},{2,3},{3,2},{4,5},{5,4},{6,7},{7,6},{8,9},{9,8},{10,11... | collective-permute-start | bytes 786440 | tf_op jit(solution)/shard_map/ppermute | solution.py:21
  30.1 0.1 collective-permute-start.13
  30.2 0.4 %collective-permute-start.14 = (bf16[3,64,512]{2,1,0:T(8,128)(2,1)S(1)}, bf16[3,64,512]{2,1,0:T(8,128)(2,1)S(1)}, u32[]{:S(2)}, u32[]{:S(2)}) collective-permute-start(bf16[3,64,512]{2,1,0:T(8,128)(2,1)S(1)} %collective-permute-done.11.refs_8_), channel_id=1, source_target_pairs={{0,1},{1,0},{2,3},{3,2},{4,5},{5,4},{6,7},{7,6},{8,9},{9,8},{10,11... | collective-permute-start | bytes 589832 | tf_op jit(solution)/shard_map/ppermute | solution.py:21
  30.6 0.9 %collective-permute-done.13.refs_10_ = bf16[3,64,512]{2,1,0:T(8,128)(2,1)S(1)} collective-permute-done((bf16[3,64,512]{2,1,0:T(8,128)(2,1)S(1)}, bf16[3,64,512]{2,1,0:T(8,128)(2,1)S(1)}, u32[]{:S(2)}, u32[]{:S(2)}) %collective-permute-start.13) | collective-permute-done | bytes 196640 | tf_op jit(solution)/shard_map/ppermute | solution.py:21
  31.5 0.3 collective-permute-done.14.refs_11_
  31.8 2.6 %renew.1 = bf16[4,1,1,1,512,512]{5,4,3,2,1,0:T(8,128)(2,1)} custom-call(bf16[2,64,512]{2,1,0:T(8,128)(2,1)S(1)} %join.3.mine.first.refs_0_, bf16[2,64,512]{2,1,0:T(8,128)(2,1)S(1)} %join.4.mine.first.refs_1_, bf16[2,64,512]{2,1,0:T(8,128)(2,1)S(1)} %get-tuple-element.14.refs_2_, bf16[2,64,512]{2,1,0:T(8,128)(2,1)S(1)} %get-tuple-element.15.refs_3_, ...), custom_call_target="tpu_custom_call" | custom-call | tf_op jit(solution)/shard_map/renew/pallas_call | solution.py:218
  (21 shorter events, 0.2 us)
Async XLA Ops:
  0.6 31.2 %copy-start = (bf16[4,1,1,1,512,512]{5,4,3,2,1,0:T(8,128)(2,1)S(1)}, bf16[4,1,1,1,512,512]{5,4,3,2,1,0:T(8,128)(2,1)}, u32[]{:S(2)}) copy-start(bf16[4,1,1,1,512,512]{5,4,3,2,1,0:T(8,128)(2,1)} %refs_12_.1) | copy-start | bytes 6291460
  3.2 4.4 %collective-permute-start.1 = (bf16[1,64,512]{2,1,0:T(8,128)(2,1)}, bf16[1,64,512]{2,1,0:T(8,128)(2,1)S(1)}, u32[]{:S(2)}, u32[]{:S(2)}) collective-permute-start(bf16[1,64,512]{2,1,0:T(8,128)(2,1)} %get-tuple-element.13), channel_id=1, source_target_pairs={{0,4},{1,5},{2,6},{3,7},{4,0},{5,1},{6,2},{7,3},{8,12},{9,13},{10,... | collective-permute-start | bytes 196616 | tf_op jit(solution)/shard_map/ppermute | solution.py:21
  3.3 7.3 %collective-permute-start = (bf16[1,64,512]{2,1,0:T(8,128)(2,1)}, bf16[1,64,512]{2,1,0:T(8,128)(2,1)S(1)}, u32[]{:S(2)}, u32[]{:S(2)}) collective-permute-start(bf16[1,64,512]{2,1,0:T(8,128)(2,1)} %get-tuple-element.12.refs_0_), channel_id=1, source_target_pairs={{0,2},{1,3},{2,0},{3,1},{4,6},{5,7},{6,4},{7,5},{8,10},{9,11},{10,... | collective-permute-start | bytes 196616 | tf_op jit(solution)/shard_map/ppermute | solution.py:21
  4.6 12.1 %collective-permute-start.10 = (bf16[3,64,512]{2,1,0:T(8,128)(2,1)}, bf16[3,64,512]{2,1,0:T(8,128)(2,1)S(1)}, u32[]{:S(2)}, u32[]{:S(2)}) collective-permute-start(bf16[3,64,512]{2,1,0:T(8,128)(2,1)} %get-tuple-element.19), channel_id=1, source_target_pairs={{0,4},{1,5},{2,6},{3,7},{4,0},{5,1},{6,2},{7,3},{8,12},{9,13},{10,... | collective-permute-start | bytes 589832 | tf_op jit(solution)/shard_map/ppermute | solution.py:21
  7.5 5.7 %collective-permute-start.2 = (bf16[1,64,512]{2,1,0:T(8,128)(2,1)S(1)}, bf16[1,64,512]{2,1,0:T(8,128)(2,1)S(1)}, u32[]{:S(2)}, u32[]{:S(2)}) collective-permute-start(bf16[1,64,512]{2,1,0:T(8,128)(2,1)S(1)} %collective-permute-done.1.refs_0_), channel_id=1, source_target_pairs={{0,2},{1,3},{2,0},{3,1},{4,6},{5,7},{6,4},{7,5},{8,10},{9,11},{10,... | collective-permute-start | bytes 196616 | tf_op jit(solution)/shard_map/ppermute | solution.py:21
  10.5 9.8 %collective-permute-start.9 = (bf16[3,64,512]{2,1,0:T(8,128)(2,1)}, bf16[3,64,512]{2,1,0:T(8,128)(2,1)S(1)}, u32[]{:S(2)}, u32[]{:S(2)}) collective-permute-start(bf16[3,64,512]{2,1,0:T(8,128)(2,1)} %get-tuple-element.18.refs_0_), channel_id=1, source_target_pairs={{0,2},{1,3},{2,0},{3,1},{4,6},{5,7},{6,4},{7,5},{8,10},{9,11},{10,... | collective-permute-start | bytes 589832 | tf_op jit(solution)/shard_map/ppermute | solution.py:21
  10.6 0.8 %copy-start.2 = (bf16[1,64,512]{2,1,0:T(8,128)(2,1)S(1)}, bf16[1,64,512]{2,1,0:T(8,128)(2,1)}, u32[]{:S(2)}) copy-start(bf16[1,64,512]{2,1,0:T(8,128)(2,1)} %get-tuple-element.12.refs_0_) | copy-start | bytes 196612
  11.4 4.0 %collective-permute-start.3 = (bf16[2,64,512]{2,1,0:T(8,128)(2,1)S(1)}, bf16[2,64,512]{2,1,0:T(8,128)(2,1)S(1)}, u32[]{:S(2)}, u32[]{:S(2)}) collective-permute-start(bf16[2,64,512]{2,1,0:T(8,128)(2,1)S(1)} %join.3.mine.first.refs_0_), channel_id=1, source_target_pairs={{0,16},{8,24},{16,0},{24,8},{1,17},{9,25},{17,1},{25,9},{2,18},{10... | collective-permute-start | bytes 393224 | tf_op jit(solution)/shard_map/ppermute | solution.py:21
  13.3 5.8 %collective-permute-start.5 = (bf16[2,64,512]{2,1,0:T(8,128)(2,1)S(1)}, bf16[2,64,512]{2,1,0:T(8,128)(2,1)S(1)}, u32[]{:S(2)}, u32[]{:S(2)}) collective-permute-start(bf16[2,64,512]{2,1,0:T(8,128)(2,1)S(1)} %join.4.mine.first.refs_1_), channel_id=1, source_target_pairs={{0,16},{8,24},{16,0},{24,8},{1,17},{9,25},{17,1},{25,9},{2,18},{10... | collective-permute-start | bytes 393224 | tf_op jit(solution)/shard_map/ppermute | solution.py:21
  15.4 11.2 %collective-permute-start.4 = (bf16[2,64,512]{2,1,0:T(8,128)(2,1)S(1)}, bf16[2,64,512]{2,1,0:T(8,128)(2,1)S(1)}, u32[]{:S(2)}, u32[]{:S(2)}) collective-permute-start(bf16[2,64,512]{2,1,0:T(8,128)(2,1)S(1)} %choose.2.mine), channel_id=1, source_target_pairs={{0,8},{8,0},{16,24},{24,16},{1,9},{9,1},{17,25},{25,17},{2,10},{10... | collective-permute-start | bytes 393224 | tf_op jit(solution)/shard_map/ppermute | solution.py:21
  16.7 13.5 %collective-permute-start.11 = (bf16[3,64,512]{2,1,0:T(8,128)(2,1)S(1)}, bf16[3,64,512]{2,1,0:T(8,128)(2,1)S(1)}, u32[]{:S(2)}, u32[]{:S(2)}) collective-permute-start(bf16[3,64,512]{2,1,0:T(8,128)(2,1)S(1)} %collective-permute-done.10.refs_7_), channel_id=1, source_target_pairs={{0,2},{1,3},{2,0},{3,1},{4,6},{5,7},{6,4},{7,5},{8,10},{9,11},{10,... | collective-permute-start | bytes 589832 | tf_op jit(solution)/shard_map/ppermute | solution.py:21
  19.1 7.7 %collective-permute-start.6 = (bf16[2,64,512]{2,1,0:T(8,128)(2,1)S(1)}, bf16[2,64,512]{2,1,0:T(8,128)(2,1)S(1)}, u32[]{:S(2)}, u32[]{:S(2)}) collective-permute-start(bf16[2,64,512]{2,1,0:T(8,128)(2,1)S(1)} %choose.3.mine), channel_id=1, source_target_pairs={{0,8},{8,0},{16,24},{24,16},{1,9},{9,1},{17,25},{25,17},{2,10},{10... | collective-permute-start | bytes 393224 | tf_op jit(solution)/shard_map/ppermute | solution.py:21
  20.4 0.9 %copy-start.1 = (bf16[3,64,512]{2,1,0:T(8,128)(2,1)S(1)}, bf16[3,64,512]{2,1,0:T(8,128)(2,1)}, u32[]{:S(2)}) copy-start(bf16[3,64,512]{2,1,0:T(8,128)(2,1)} %get-tuple-element.18.refs_0_) | copy-start | bytes 589828
  21.3 10.5 %collective-permute-start.12 = (bf16[6,64,512]{2,1,0:T(8,128)(2,1)S(1)}, bf16[6,64,512]{2,1,0:T(8,128)(2,1)S(1)}, u32[]{:S(2)}, u32[]{:S(2)}) collective-permute-start(bf16[6,64,512]{2,1,0:T(8,128)(2,1)S(1)} %join.5.refs_6_), channel_id=1, source_target_pairs={{0,1},{1,0},{2,3},{3,2},{4,5},{5,4},{6,7},{7,6},{8,9},{9,8},{10,11... | collective-permute-start | bytes 1179656 | tf_op jit(solution)/shard_map/ppermute | solution.py:21
  26.6 4.9 %collective-permute-start.7 = (bf16[4,64,512]{2,1,0:T(8,128)(2,1)S(1)}, bf16[4,64,512]{2,1,0:T(8,128)(2,1)S(1)}, u32[]{:S(2)}, u32[]{:S(2)}) collective-permute-start(bf16[4,64,512]{2,1,0:T(8,128)(2,1)S(1)} %get-tuple-element.16), channel_id=1, source_target_pairs={{0,1},{1,0},{2,3},{3,2},{4,5},{5,4},{6,7},{7,6},{8,9},{9,8},{10,11... | collective-permute-start | bytes 786440 | tf_op jit(solution)/shard_map/ppermute | solution.py:21
  26.8 5.1 %collective-permute-start.8 = (bf16[4,64,512]{2,1,0:T(8,128)(2,1)S(1)}, bf16[4,64,512]{2,1,0:T(8,128)(2,1)S(1)}, u32[]{:S(2)}, u32[]{:S(2)}) collective-permute-start(bf16[4,64,512]{2,1,0:T(8,128)(2,1)S(1)} %get-tuple-element.17), channel_id=1, source_target_pairs={{0,1},{1,0},{2,3},{3,2},{4,5},{5,4},{6,7},{7,6},{8,9},{9,8},{10,11... | collective-permute-start | bytes 786440 | tf_op jit(solution)/shard_map/ppermute | solution.py:21
  30.1 1.4 %collective-permute-start.13 = (bf16[3,64,512]{2,1,0:T(8,128)(2,1)S(1)}, bf16[3,64,512]{2,1,0:T(8,128)(2,1)S(1)}, u32[]{:S(2)}, u32[]{:S(2)}) collective-permute-start(bf16[3,64,512]{2,1,0:T(8,128)(2,1)S(1)} %collective-permute-done.10.refs_7_), channel_id=1, source_target_pairs={{0,1},{1,0},{2,3},{3,2},{4,5},{5,4},{6,7},{7,6},{8,9},{9,8},{10,11... | collective-permute-start | bytes 589832 | tf_op jit(solution)/shard_map/ppermute | solution.py:21
  30.2 1.6 %collective-permute-start.14 = (bf16[3,64,512]{2,1,0:T(8,128)(2,1)S(1)}, bf16[3,64,512]{2,1,0:T(8,128)(2,1)S(1)}, u32[]{:S(2)}, u32[]{:S(2)}) collective-permute-start(bf16[3,64,512]{2,1,0:T(8,128)(2,1)S(1)} %collective-permute-done.11.refs_8_), channel_id=1, source_target_pairs={{0,1},{1,0},{2,3},{3,2},{4,5},{5,4},{6,7},{7,6},{8,9},{9,8},{10,11... | collective-permute-start | bytes 589832 | tf_op jit(solution)/shard_map/ppermute | solution.py:21

commit v3 on v2

v3 whole, which is shorter than its diff:
```python
import functools

import jax
import jax.numpy as jnp
from jax import lax
from jax.experimental import pallas as pl
from jax.experimental.pallas import tpu as pltpu
from jax.sharding import PartitionSpec as P

TRANSPOSED = (((1,), (1,)), ((), ()))
HBM = pl.BlockSpec(memory_space=pl.ANY)
VMEM = pl.BlockSpec(memory_space=pltpu.VMEM)
SMEM = pl.BlockSpec(memory_space=pltpu.SMEM)
LIMIT = 16 * 1024 * 1024
FIRST = 56418304
SOLVE = 62914560
SMALL = 8 * 1024 * 1024


def swap(x, axis, distance):
    size = lax.axis_size(axis)
    return lax.ppermute(x, axis, [(i, i ^ distance) for i in range(size)])


def load(pairs, sems):
    copies = [pltpu.make_async_copy(*pair, sems.at[n]) for n, pair in enumerate(pairs)]
    for copy in copies:
        copy.start()
    for copy in copies:
        copy.wait()


def first_kernel(classes, panel, diag_inv, *refs):
    slabs, (strips, inverse, sems) = refs[:classes], refs[classes:]
    own = lax.axis_index("pcol") // lax.axis_size("prow")
    load([(diag_inv, inverse)]
         + [(panel.at[jnp.bitwise_xor(own, n), 0], strips.at[n]) for n in range(classes)], sems)
    rows, size = strips.shape[1:]
    product = lax.dot_general(strips[...].reshape(classes * rows, size), inverse[...], TRANSPOSED,
                              preferred_element_type=jnp.float32).reshape(classes, rows, size)
    for n in range(classes):
        slabs[n][0] = product[n].astype(strips.dtype)


def rest_kernel(classes, nonzero, panel, diag_inv, factor, mask, *refs):
    rests, (live, strips, inverse, sems) = refs[:-4], refs[-4:]
    load([(nonzero, live), (panel, strips), (diag_inv, inverse)], sems)
    steps, _, rows, size = strips.shape
    product = lax.dot_general(strips[...].reshape(steps * rows, size), inverse[...], TRANSPOSED,
                              preferred_element_type=jnp.float32).reshape(steps, rows, size)
    for s in range(steps):
        factor[s, 0] = (product[s] * live[s].astype(jnp.float32)).astype(factor.dtype)
    own = lax.axis_index("pcol") // lax.axis_size("prow")
    mask[...] = jnp.full(mask.shape, live[own].astype(jnp.float32), mask.dtype)
    at = 0
    for n in range(classes):
        m = 1
        while m < steps:
            for i in range(rests[at].shape[0]):
                rests[at][i] = factor[lax.rem(jnp.bitwise_xor(own, n) + m + i, steps), 0]
            m += rests[at].shape[0]
            at += 1


def solve_call(kernel, outs, scratch, copies, limit, args, name):
    return pl.pallas_call(
        kernel,
        out_shape=outs,
        in_specs=[pl.BlockSpec(memory_space=pltpu.HBM)] * len(args),
        out_specs=[VMEM] * len(outs),
        scratch_shapes=scratch + [pltpu.SemaphoreType.DMA((copies,))],
        cost_estimate=pl.CostEstimate(flops=0, bytes_accessed=1024, transcendentals=0),
        compiler_params=pltpu.CompilerParams(vmem_limit_bytes=limit),
        name=name,
    )(*args)


def solve(panel, diag_inv, nonzero, classes):
    steps, _, rows, size = panel.shape
    dtype = panel.dtype
    slab = jax.ShapeDtypeStruct((1, rows, size), dtype)
    cuts = [[steps - 1]] + [CUTS(steps)] * (classes - 1)
    rest = [jax.ShapeDtypeStruct((n, rows, size), dtype) for cut in cuts for n in cut]
    mask = jax.ShapeDtypeStruct((1, size), jnp.float32)
    inverse = pltpu.VMEM(diag_inv.shape, dtype)
    slabs = solve_call(functools.partial(first_kernel, classes), [slab] * classes,
                       [pltpu.VMEM((classes, rows, size), dtype), inverse], 1 + classes, FIRST,
                       (panel, diag_inv), "solve_first")
    factor, mask, *rests = solve_call(functools.partial(rest_kernel, classes),
                                      [jax.ShapeDtypeStruct(panel.shape, dtype), mask] + rest,
                                      [pltpu.SMEM((steps,), nonzero.dtype), pltpu.VMEM(panel.shape, dtype), inverse], 3,
                                      SOLVE, (nonzero[:, 0], panel, diag_inv), "solve_rest")
    far = len(cuts[-1])
    return factor, mask, slabs, [rests[:1]] + [rests[i:i + far] for i in range(1, len(rests), far)]


def pick_kernel(sources, *refs):
    ins, (keep, packed) = refs[:sources], refs[sources:]
    span = ins[0].shape[0]
    c, r = lax.axis_index("pcol"), lax.axis_index("prow")
    packed[span:] = ins[0][...]
    for k in range(sources):
        @pl.when(jnp.bitwise_xor(r, lax.rem(c, sources)) == k)
        def _():
            keep[...] = ins[k][...]

        @pl.when(jnp.bitwise_xor(r, lax.rem(jnp.bitwise_xor(c, 1), sources)) == k)
        def _():
            packed[:span] = ins[k][...]


def pick(slabs):
    span, *rest = slabs[0].shape
    outs = [jax.ShapeDtypeStruct(slabs[0].shape, slabs[0].dtype), jax.ShapeDtypeStruct((2 * span, *rest), slabs[0].dtype)]
    return small_call(functools.partial(pick_kernel, len(slabs)), outs, slabs, "pick")


def small_call(kernel, outs, args, name):
    return pl.pallas_call(
        kernel,
        out_shape=outs,
        in_specs=[VMEM] * len(args),
        out_specs=jax.tree.map(lambda _: VMEM, outs),
        cost_estimate=pl.CostEstimate(flops=0, bytes_accessed=1024, transcendentals=0),
        compiler_params=pltpu.CompilerParams(vmem_limit_bytes=SMALL),
        name=name,
    )(*args)


def choose_kernel(bit, mine, came, out):
    away = jnp.bitwise_xor(lax.axis_index("prow"), lax.rem(lax.axis_index("pcol"), lax.axis_size("prow")))
    here = jnp.bitwise_and(away, bit) == 0

    @pl.when(here)
    def _():
        out[...] = mine[...]

    @pl.when(jnp.logical_not(here))
    def _():
        out[...] = came[...]


def choose(bit, mine, came):
    shape = jax.ShapeDtypeStruct(mine.shape, mine.dtype)
    return small_call(functools.partial(choose_kernel, bit), shape, (mine, came), "choose")


def pack_kernel(mine, came, first, keep, packed):
    span = first.shape[0]
    here = lax.rem(lax.axis_index("prow"), 2) == lax.rem(lax.axis_index("pcol"), 2)
    packed[span:] = first[...]

    @pl.when(here)
    def _():
        keep[...] = mine[...]
        packed[:span] = came[...]

    @pl.when(jnp.logical_not(here))
    def _():
        keep[...] = came[...]
        packed[:span] = mine[...]


def pack(mine, came, first):
    span, *rest = first.shape
    outs = [jax.ShapeDtypeStruct(first.shape, first.dtype), jax.ShapeDtypeStruct((2 * span, *rest), first.dtype)]
    return small_call(pack_kernel, outs, (mine, came, first), "pack")


def join_kernel(*refs):
    at = 0
    for ref in refs[:-1]:
        refs[-1][at:at + ref.shape[0]] = ref[...]
        at += ref.shape[0]


def join(parts):
    total = sum(x.shape[0] for x in parts)
    return small_call(join_kernel, jax.ShapeDtypeStruct((total, *parts[0].shape[1:]), parts[0].dtype), parts, "join")


def masked_kernel(mask, *refs):
    for n, ref in enumerate(refs[:-1]):
        refs[-1][n] = (ref[0].astype(jnp.float32) * mask[...]).astype(ref.dtype)


def masked(mask, parts):
    shape = jax.ShapeDtypeStruct((len(parts), *parts[0].shape[1:]), parts[0].dtype)
    return small_call(masked_kernel, shape, (mask, *parts), "masked")


def hold_kernel(x, _, out):
    del x, out


def hold(x, until):
    return pl.pallas_call(
        hold_kernel,
        out_shape=jax.ShapeDtypeStruct(x.shape, x.dtype),
        in_specs=[HBM, HBM],
        out_specs=HBM,
        input_output_aliases={0: 0},
        cost_estimate=pl.CostEstimate(flops=0, bytes_accessed=1024, transcendentals=0),
        compiler_params=pltpu.CompilerParams(vmem_limit_bytes=SMALL),
        name="hold",
    )(x, until)


def renew_kernel(plan, chips, *refs):
    operands, (trailing, out, rows_full, column, held, out_sems) = refs[:len(plan)], refs[len(plan):]
    steps, size = held.shape[0], held.shape[1]
    rows = size // (2 * chips)
    c, r = lax.axis_index("pcol"), lax.axis_index("prow")
    grid_rows = lax.axis_size("prow")
    own = c // grid_rows
    order = [lax.rem(own + m, steps) for m in range(steps)]
    for ref, places in zip(operands, plan):
        for at, (m, core, k) in enumerate(places):
            source = jnp.bitwise_xor(c, 2 * k + core)
            here = pl.ds(pl.multiple_of(source * rows, rows), rows)
            if m is None:
                column[here] = ref[at]
            else:
                rows_full[m, here] = ref[at]
    for m in range(steps):
        product = lax.dot_general(rows_full[m], column[...], TRANSPOSED, preferred_element_type=jnp.float32)
        before = trailing[order[m], 0, 0, 0]
        renewed = (before.astype(jnp.float32) - product).astype(held.dtype)
        held[m] = jnp.where(order[m] * grid_rows + r >= c, renewed, before)
        pltpu.make_async_copy(held.at[m], out.at[order[m], 0, 0, 0], out_sems.at[m]).start()
    for m in range(steps):
        pltpu.make_async_copy(held.at[m], out.at[order[m], 0, 0, 0], out_sems.at[m]).wait()


def renew(trailing, chips, operands, plan):
    steps, size = trailing.shape[0], trailing.shape[-1]
    tiles = pltpu.VMEM((steps, size, size), trailing.dtype)
    args = (*operands, trailing)
    return pl.pallas_call(
        functools.partial(renew_kernel, plan, chips),
        out_shape=jax.ShapeDtypeStruct(trailing.shape, trailing.dtype),
        in_specs=[VMEM] * len(args),
        out_specs=HBM,
        scratch_shapes=[
            tiles,
            pltpu.VMEM((size, size), trailing.dtype),
            tiles,
            pltpu.SemaphoreType.DMA((steps,)),
        ],
        compiler_params=pltpu.CompilerParams(vmem_limit_bytes=LIMIT),
        name="renew",
    )(*args)


def body(panel, diag_inv, nonzero, trailing):
    grid_rows, grid_cols = lax.axis_size("prow"), lax.axis_size("pcol")
    chips = grid_cols // 2
    classes = max(1, grid_cols // grid_rows)
    steps = panel.shape[0]
    factor, mask, slabs, rests = solve(panel, diag_inv, nonzero, classes)
    slabs = list(slabs)

    def kind(k):
        return 2 * k // grid_rows

    def gather(parts, relay, ks, held):
        for k in ks:
            low = k & -k
            relayed = relay and low != k and kind(low) == 0
            source = held[k ^ low] if relayed else parts[kind(k)]
            held[k] = swap(source, "pcol", 2 * low if relayed else 2 * k)
        return held

    top = chips // 2
    near = gather(slabs, PREL, range(1, chips), {0: slabs[0]})
    half = max(1, chips // GROUPS)
    firsts = [masked(mask, [near[k] for k in range(n, n + half)]) for n in range(0, chips, half)]
    marks = {"p1": near[1], "p2": near[top], "p3": near[chips - 1], "b": firsts[-1], "a": firsts[0]}
    own_rest = rests[0][0]
    if G1:
        own_rest = hold(own_rest, marks[G1])
    close = [k for k in range(1, chips) if kind(k) == 0]
    far = [k for k in range(1, chips) if kind(k) != 0]
    rest = gather([own_rest], QREL, close, {0: own_rest})
    cuts = CUTS(steps)
    pieces = []
    for i in range(len(cuts)):
        parts = [None] + [row[i] for row in rests[1:]]
        if G2 and parts[1:]:
            parts[1] = hold(parts[1], marks[G2])
        pieces.append(gather(parts, QREL, far, {}))
    operands, plan = [], []

    def use(x, places):
        operands.append(x)
        plan.append(tuple(places))

    def both(x, places):
        use(x, [(m, 0, k) for m, k in places])
        use(swap(x, "pcol", 1), [(m, 1, k) for m, k in places])

    for n, first in enumerate(firsts):
        group = range(n * half, (n + 1) * half)
        if XY == "hyper":
            mine = first
            bit = grid_rows // 2
            while bit > 1:
                mine = choose(bit, mine, swap(mine, "prow", bit))
                bit //= 2
            if GX and n == GX[0]:
                mine = hold(mine, pieces[0][top])
            keep, packed = pack(mine, swap(mine, "prow", 1), first)
        else:
            keep, packed = pick([first] + [swap(first, "prow", k) for k in range(1, grid_rows)])
        use(keep, [(None, 0, k) for k in group])
        use(first, [(0, 0, k) for k in group])
        use(swap(packed, "pcol", 1), [(None, 1, k) for k in group] + [(0, 1, k) for k in group])
    joined = [0] + close
    both(join([rest[k] for k in joined]), [(m, k) for k in joined for m in range(1, steps)])
    for k in far:
        m = 1
        for i, cut in enumerate(cuts):
            both(pieces[i][k], [(m + j, k) for j in range(cut)])
            m += cut
    renewed = renew(trailing, chips, operands, plan)
    return factor, renewed


GX = (1,)


PREL = True
QREL = True
GROUPS = 2
G1 = None
G2 = None
XY = 'hyper'


def CUTS(steps):
    return [steps - 1]


def solution(mesh):
    placed = (
        P(None, "prow", "pcol", None),
        P(),
        P(None, "prow"),
        P(None, "prow", None, "pcol", None, None),
    )
    return jax.shard_map(
        body,
        mesh=mesh,
        in_specs=placed,
        out_specs=(P(None, "prow", "pcol", None), P(None, "prow", None, "pcol", None, None)),
        check_vma=False,
    )
```

time: 34.7 us -> 32.8 us (0.945)
  the two profiles are of different devices: /device:TPU:21 before, /device:TPU:0 now
where the time goes in v3:
time: 32.8 us; the launch traced here: 32.6 us
  starting transfers between devices  16.6 us (51%)
  waiting for transfers between devices  7.51 us (23%)
  Pallas kernels  6.11 us (19%)
  local copies, waits for them, and re-layouts  1.6 us (5%)
  between operations  0.74 us (2%)
    ppermute x15, starting transfers between devices, swap(): return lax.ppermute(x, axis, [(i, i ^ distance) for i in range(size)])  16.6 us
    ppermute x15, waiting for transfers between devices, swap(): return lax.ppermute(x, axis, [(i, i ^ distance) for i in range(size)])  7.51 us
    pallas_call x2, Pallas kernels, solve_call(): pl.pallas_call(kernel, out_shape=outs, in_specs=[pl.BlockSpec(memory_spac...  3.7 us
    pallas_call x1, Pallas kernels, renew(): pl.pallas_call(functools.partial(renew_kernel, plan, chips), out_shape=ja...  2.24 us
    unnamed x6, local copies, waits for them, and re-layouts  1.6 us
  transfers between devices with their start and end apart: 15, of which 6 were waited for; matrix products, arithmetic and copies ran while one was open for 0% of the time, Pallas kernels for 8%

profile of v3, /device:TPU:0, one launch (start us, length us, event | category | flops | bytes accessed | tf_op | source)
XLA Modules:
  0.0 32.6 jit_solution(7071957593994281198)
XLA Ops:
  0.6 1.4 %solve_first.1 = (bf16[1,64,512]{2,1,0:T(8,128)(2,1)S(1)}, bf16[1,64,512]{2,1,0:T(8,128)(2,1)S(1)}) custom-call(bf16[4,1,64,512]{3,2,1,0:T(8,128)(2,1)} %panel.3, bf16[512,512]{1,0:T(8,128)(2,1)} %diag_inv.3), custom_call_target="tpu_custom_call" | custom-call | bytes 1024 | tf_op jit(solution)/shard_map/solve_first/pallas_call | solution.py:66
  2.0 4.1 %collective-permute-start.4 = (bf16[1,64,512]{2,1,0:T(8,128)(2,1)S(1)}, bf16[1,64,512]{2,1,0:T(8,128)(2,1)S(1)}, u32[]{:S(2)}, u32[]{:S(2)}) collective-permute-start(bf16[1,64,512]{2,1,0:T(8,128)(2,1)S(1)} %get-tuple-element.17), channel_id=1, source_target_pairs={{0,4},{1,5},{2,6},{3,7},{4,0},{5,1},{6,2},{7,3},{8,12},{9,13},{10,... | collective-permute-start | bytes 196616 | tf_op jit(solution)/shard_map/ppermute | solution.py:22
  6.1 1.6 %collective-permute-start = (bf16[1,64,512]{2,1,0:T(8,128)(2,1)S(1)}, bf16[1,64,512]{2,1,0:T(8,128)(2,1)S(1)}, u32[]{:S(2)}, u32[]{:S(2)}) collective-permute-start(bf16[1,64,512]{2,1,0:T(8,128)(2,1)S(1)} %get-tuple-element.14.refs_0_), channel_id=1, source_target_pairs={{0,2},{1,3},{2,0},{3,1},{4,6},{5,7},{6,4},{7,5},{8,10},{9,11},{10,... | collective-permute-start | bytes 196616 | tf_op jit(solution)/shard_map/ppermute | solution.py:22
  7.7 2.3 %solve_rest.1 = (bf16[4,1,64,512]{3,2,1,0:T(8,128)(2,1)}, f32[1,512]{1,0:T(1,128)}, bf16[3,64,512]{2,1,0:T(8,128)(2,1)}, bf16[3,64,512]{2,1,0:T(8,128)(2,1)}) custom-call(s32[4]{0:T(128)} %bitcast.1, bf16[4,1,64,512]{3,2,1,0:T(8,128)(2,1)} %panel.3, bf16[512,512]{1,0:T(8,128)(2,1)} %diag_inv.3), custom_call_target="tpu_custom_call" | custom-call | bytes 1024 | tf_op jit(solution)/shard_map/solve_rest/pallas_call | solution.py:66
  10.0 0.4 %collective-permute-start.7 = (bf16[3,64,512]{2,1,0:T(8,128)(2,1)}, bf16[3,64,512]{2,1,0:T(8,128)(2,1)S(1)}, u32[]{:S(2)}, u32[]{:S(2)}) collective-permute-start(bf16[3,64,512]{2,1,0:T(8,128)(2,1)} %get-tuple-element.18), channel_id=1, source_target_pairs={{0,4},{1,5},{2,6},{3,7},{4,0},{5,1},{6,2},{7,3},{8,12},{9,13},{10,... | collective-permute-start | bytes 589832 | tf_op jit(solution)/shard_map/ppermute | solution.py:22
  10.4 0.2 collective-permute-start.5
  10.7 1.8 %collective-permute-start.10 = (bf16[3,64,512]{2,1,0:T(8,128)(2,1)}, bf16[3,64,512]{2,1,0:T(8,128)(2,1)S(1)}, u32[]{:S(2)}, u32[]{:S(2)}) collective-permute-start(bf16[3,64,512]{2,1,0:T(8,128)(2,1)} %get-tuple-element.21.refs_0_), channel_id=1, source_target_pairs={{0,2},{1,3},{2,0},{3,1},{4,6},{5,7},{6,4},{7,5},{8,10},{9,11},{10,... | collective-permute-start | bytes 589832 | tf_op jit(solution)/shard_map/ppermute | solution.py:22
  12.5 0.7 %copy-done.2 = f32[1,512]{1,0:T(1,128)S(1)} copy-done((f32[1,512]{1,0:T(1,128)S(1)}, f32[1,512]{1,0:T(1,128)}, u32[]{:S(2)}) %copy-start.2) | copy-done | bytes 2072
  13.2 1.6 %collective-permute-start.1 = (bf16[2,64,512]{2,1,0:T(8,128)(2,1)S(1)}, bf16[2,64,512]{2,1,0:T(8,128)(2,1)S(1)}, u32[]{:S(2)}, u32[]{:S(2)}) collective-permute-start(bf16[2,64,512]{2,1,0:T(8,128)(2,1)S(1)} %masked.2.mine.first.refs_1_), channel_id=1, source_target_pairs={{0,16},{8,24},{16,0},{24,8},{1,17},{9,25},{17,1},{25,9},{2,18},{10... | collective-permute-start | bytes 393224 | tf_op jit(solution)/shard_map/ppermute | solution.py:22
  14.7 2.7 %collective-permute-done.5.refs_1_ = bf16[1,64,512]{2,1,0:T(8,128)(2,1)S(1)} collective-permute-done((bf16[1,64,512]{2,1,0:T(8,128)(2,1)S(1)}, bf16[1,64,512]{2,1,0:T(8,128)(2,1)S(1)}, u32[]{:S(2)}, u32[]{:S(2)}) %collective-permute-start.5) | collective-permute-done | bytes 65568 | tf_op jit(solution)/shard_map/ppermute | solution.py:22
  17.4 1.6 %collective-permute-start.6 = (bf16[2,64,512]{2,1,0:T(8,128)(2,1)S(1)}, bf16[2,64,512]{2,1,0:T(8,128)(2,1)S(1)}, u32[]{:S(2)}, u32[]{:S(2)}) collective-permute-start(bf16[2,64,512]{2,1,0:T(8,128)(2,1)S(1)} %masked.3.mine.first.refs_4_), channel_id=1, source_target_pairs={{0,16},{8,24},{16,0},{24,8},{1,17},{9,25},{17,1},{25,9},{2,18},{10... | collective-permute-start | bytes 393224 | tf_op jit(solution)/shard_map/ppermute | solution.py:22
  19.0 0.5 %collective-permute-done.1.came = bf16[2,64,512]{2,1,0:T(8,128)(2,1)S(1)} collective-permute-done((bf16[2,64,512]{2,1,0:T(8,128)(2,1)S(1)}, bf16[2,64,512]{2,1,0:T(8,128)(2,1)S(1)}, u32[]{:S(2)}, u32[]{:S(2)}) %collective-permute-start.1) | collective-permute-done | bytes 131104 | tf_op jit(solution)/shard_map/ppermute | solution.py:22
  19.6 1.6 %collective-permute-start.2 = (bf16[2,64,512]{2,1,0:T(8,128)(2,1)S(1)}, bf16[2,64,512]{2,1,0:T(8,128)(2,1)S(1)}, u32[]{:S(2)}, u32[]{:S(2)}) collective-permute-start(bf16[2,64,512]{2,1,0:T(8,128)(2,1)S(1)} %choose.2.mine), channel_id=1, source_target_pairs={{0,8},{8,0},{16,24},{24,16},{1,9},{9,1},{17,25},{25,17},{2,10},{10... | collective-permute-start | bytes 393224 | tf_op jit(solution)/shard_map/ppermute | solution.py:22
  21.2 0.3 collective-permute-done.7._.refs_8_
  21.5 1.6 %collective-permute-start.13 = (bf16[3,64,512]{2,1,0:T(8,128)(2,1)S(1)}, bf16[3,64,512]{2,1,0:T(8,128)(2,1)S(1)}, u32[]{:S(2)}, u32[]{:S(2)}) collective-permute-start(bf16[3,64,512]{2,1,0:T(8,128)(2,1)S(1)} %collective-permute-done.7._.refs_8_), channel_id=1, source_target_pairs={{0,2},{1,3},{2,0},{3,1},{4,6},{5,7},{6,4},{7,5},{8,10},{9,11},{10,... | collective-permute-start | bytes 589832 | tf_op jit(solution)/shard_map/ppermute | solution.py:22
  23.1 0.9 %collective-permute-start.8 = (bf16[2,64,512]{2,1,0:T(8,128)(2,1)S(1)}, bf16[2,64,512]{2,1,0:T(8,128)(2,1)S(1)}, u32[]{:S(2)}, u32[]{:S(2)}) collective-permute-start(bf16[2,64,512]{2,1,0:T(8,128)(2,1)S(1)} %hold.1.mine), channel_id=1, source_target_pairs={{0,8},{8,0},{16,24},{24,16},{1,9},{9,1},{17,25},{25,17},{2,10},{10... | collective-permute-start | bytes 393224 | tf_op jit(solution)/shard_map/ppermute | solution.py:22
  24.1 0.9 %copy-done.1 = bf16[3,64,512]{2,1,0:T(8,128)(2,1)S(1)} copy-done((bf16[3,64,512]{2,1,0:T(8,128)(2,1)S(1)}, bf16[3,64,512]{2,1,0:T(8,128)(2,1)}, u32[]{:S(2)}) %copy-start.1) | copy-done | bytes 196632
  25.2 0.5 %collective-permute-start.3 = (bf16[4,64,512]{2,1,0:T(8,128)(2,1)S(1)}, bf16[4,64,512]{2,1,0:T(8,128)(2,1)S(1)}, u32[]{:S(2)}, u32[]{:S(2)}) collective-permute-start(bf16[4,64,512]{2,1,0:T(8,128)(2,1)S(1)} %get-tuple-element.16), channel_id=1, source_target_pairs={{0,1},{1,0},{2,3},{3,2},{4,5},{5,4},{6,7},{7,6},{8,9},{9,8},{10,11... | collective-permute-start | bytes 786440 | tf_op jit(solution)/shard_map/ppermute | solution.py:22
  25.7 2.4 %collective-permute-done.8.came = bf16[2,64,512]{2,1,0:T(8,128)(2,1)S(1)} collective-permute-done((bf16[2,64,512]{2,1,0:T(8,128)(2,1)S(1)}, bf16[2,64,512]{2,1,0:T(8,128)(2,1)S(1)}, u32[]{:S(2)}, u32[]{:S(2)}) %collective-permute-start.8) | collective-permute-done | bytes 131104 | tf_op jit(solution)/shard_map/ppermute | solution.py:22
  28.3 0.5 %collective-permute-start.12 = (bf16[3,64,512]{2,1,0:T(8,128)(2,1)S(1)}, bf16[3,64,512]{2,1,0:T(8,128)(2,1)S(1)}, u32[]{:S(2)}, u32[]{:S(2)}) collective-permute-start(bf16[3,64,512]{2,1,0:T(8,128)(2,1)S(1)} %collective-permute-done.7._.refs_8_), channel_id=1, source_target_pairs={{0,1},{1,0},{2,3},{3,2},{4,5},{5,4},{6,7},{7,6},{8,9},{9,8},{10,11... | collective-permute-start | bytes 589832 | tf_op jit(solution)/shard_map/ppermute | solution.py:22
  28.8 0.1 collective-permute-start.14
  28.8 1.2 %collective-permute-done.12.refs_9_ = bf16[3,64,512]{2,1,0:T(8,128)(2,1)S(1)} collective-permute-done((bf16[3,64,512]{2,1,0:T(8,128)(2,1)S(1)}, bf16[3,64,512]{2,1,0:T(8,128)(2,1)S(1)}, u32[]{:S(2)}, u32[]{:S(2)}) %collective-permute-start.12) | collective-permute-done | bytes 196640 | tf_op jit(solution)/shard_map/ppermute | solution.py:22
  30.1 0.3 collective-permute-done.14.refs_11_
  30.4 2.2 %renew.1 = bf16[4,1,1,1,512,512]{5,4,3,2,1,0:T(8,128)(2,1)} custom-call(bf16[2,64,512]{2,1,0:T(8,128)(2,1)S(1)} %get-tuple-element.15.refs_0_, bf16[2,64,512]{2,1,0:T(8,128)(2,1)S(1)} %masked.2.mine.first.refs_1_, bf16[4,64,512]{2,1,0:T(8,128)(2,1)S(1)} %collective-permute-done.3.refs_2_, bf16[2,64,512]{2,1,0:T(8,128)(2,1)S(1)} %get-tuple-element.19.refs_3_, ...), custom_call_target="tpu_custom_call" | custom-call | tf_op jit(solution)/shard_map/renew/pallas_call | solution.py:239
  (23 shorter events, 0.4 us)
Async XLA Ops:
  2.0 28.3 %copy-start = (bf16[4,1,1,1,512,512]{5,4,3,2,1,0:T(8,128)(2,1)S(1)}, bf16[4,1,1,1,512,512]{5,4,3,2,1,0:T(8,128)(2,1)}, u32[]{:S(2)}) copy-start(bf16[4,1,1,1,512,512]{5,4,3,2,1,0:T(8,128)(2,1)} %refs_12_.1) | copy-start | bytes 6291460
  2.0 8.4 %collective-permute-start.4 = (bf16[1,64,512]{2,1,0:T(8,128)(2,1)S(1)}, bf16[1,64,512]{2,1,0:T(8,128)(2,1)S(1)}, u32[]{:S(2)}, u32[]{:S(2)}) collective-permute-start(bf16[1,64,512]{2,1,0:T(8,128)(2,1)S(1)} %get-tuple-element.17), channel_id=1, source_target_pairs={{0,4},{1,5},{2,6},{3,7},{4,0},{5,1},{6,2},{7,3},{8,12},{9,13},{10,... | collective-permute-start | bytes 196616 | tf_op jit(solution)/shard_map/ppermute | solution.py:22
  6.1 6.3 %collective-permute-start = (bf16[1,64,512]{2,1,0:T(8,128)(2,1)S(1)}, bf16[1,64,512]{2,1,0:T(8,128)(2,1)S(1)}, u32[]{:S(2)}, u32[]{:S(2)}) collective-permute-start(bf16[1,64,512]{2,1,0:T(8,128)(2,1)S(1)} %get-tuple-element.14.refs_0_), channel_id=1, source_target_pairs={{0,2},{1,3},{2,0},{3,1},{4,6},{5,7},{6,4},{7,5},{8,10},{9,11},{10,... | collective-permute-start | bytes 196616 | tf_op jit(solution)/shard_map/ppermute | solution.py:22
  10.0 11.5 %collective-permute-start.7 = (bf16[3,64,512]{2,1,0:T(8,128)(2,1)}, bf16[3,64,512]{2,1,0:T(8,128)(2,1)S(1)}, u32[]{:S(2)}, u32[]{:S(2)}) collective-permute-start(bf16[3,64,512]{2,1,0:T(8,128)(2,1)} %get-tuple-element.18), channel_id=1, source_target_pairs={{0,4},{1,5},{2,6},{3,7},{4,0},{5,1},{6,2},{7,3},{8,12},{9,13},{10,... | collective-permute-start | bytes 589832 | tf_op jit(solution)/shard_map/ppermute | solution.py:22
  10.4 7.0 %collective-permute-start.5 = (bf16[1,64,512]{2,1,0:T(8,128)(2,1)S(1)}, bf16[1,64,512]{2,1,0:T(8,128)(2,1)S(1)}, u32[]{:S(2)}, u32[]{:S(2)}) collective-permute-start(bf16[1,64,512]{2,1,0:T(8,128)(2,1)S(1)} %collective-permute-done.4.refs_0_), channel_id=1, source_target_pairs={{0,2},{1,3},{2,0},{3,1},{4,6},{5,7},{6,4},{7,5},{8,10},{9,11},{10,... | collective-permute-start | bytes 196616 | tf_op jit(solution)/shard_map/ppermute | solution.py:22
  10.7 13.4 %collective-permute-start.10 = (bf16[3,64,512]{2,1,0:T(8,128)(2,1)}, bf16[3,64,512]{2,1,0:T(8,128)(2,1)S(1)}, u32[]{:S(2)}, u32[]{:S(2)}) collective-permute-start(bf16[3,64,512]{2,1,0:T(8,128)(2,1)} %get-tuple-element.21.refs_0_), channel_id=1, source_target_pairs={{0,2},{1,3},{2,0},{3,1},{4,6},{5,7},{6,4},{7,5},{8,10},{9,11},{10,... | collective-permute-start | bytes 589832 | tf_op jit(solution)/shard_map/ppermute | solution.py:22
  12.5 0.7 %copy-start.2 = (f32[1,512]{1,0:T(1,128)S(1)}, f32[1,512]{1,0:T(1,128)}, u32[]{:S(2)}) copy-start(f32[1,512]{1,0:T(1,128)} %get-tuple-element.13.mask) | copy-start | bytes 6148
  13.2 6.4 %collective-permute-start.1 = (bf16[2,64,512]{2,1,0:T(8,128)(2,1)S(1)}, bf16[2,64,512]{2,1,0:T(8,128)(2,1)S(1)}, u32[]{:S(2)}, u32[]{:S(2)}) collective-permute-start(bf16[2,64,512]{2,1,0:T(8,128)(2,1)S(1)} %masked.2.mine.first.refs_1_), channel_id=1, source_target_pairs={{0,16},{8,24},{16,0},{24,8},{1,17},{9,25},{17,1},{25,9},{2,18},{10... | collective-permute-start | bytes 393224 | tf_op jit(solution)/shard_map/ppermute | solution.py:22
  17.4 5.7 %collective-permute-start.6 = (bf16[2,64,512]{2,1,0:T(8,128)(2,1)S(1)}, bf16[2,64,512]{2,1,0:T(8,128)(2,1)S(1)}, u32[]{:S(2)}, u32[]{:S(2)}) collective-permute-start(bf16[2,64,512]{2,1,0:T(8,128)(2,1)S(1)} %masked.3.mine.first.refs_4_), channel_id=1, source_target_pairs={{0,16},{8,24},{16,0},{24,8},{1,17},{9,25},{17,1},{25,9},{2,18},{10... | collective-permute-start | bytes 393224 | tf_op jit(solution)/shard_map/ppermute | solution.py:22
  19.6 5.5 %collective-permute-start.2 = (bf16[2,64,512]{2,1,0:T(8,128)(2,1)S(1)}, bf16[2,64,512]{2,1,0:T(8,128)(2,1)S(1)}, u32[]{:S(2)}, u32[]{:S(2)}) collective-permute-start(bf16[2,64,512]{2,1,0:T(8,128)(2,1)S(1)} %choose.2.mine), channel_id=1, source_target_pairs={{0,8},{8,0},{16,24},{24,16},{1,9},{9,1},{17,25},{25,17},{2,10},{10... | collective-permute-start | bytes 393224 | tf_op jit(solution)/shard_map/ppermute | solution.py:22
  21.5 7.3 %collective-permute-start.13 = (bf16[3,64,512]{2,1,0:T(8,128)(2,1)S(1)}, bf16[3,64,512]{2,1,0:T(8,128)(2,1)S(1)}, u32[]{:S(2)}, u32[]{:S(2)}) collective-permute-start(bf16[3,64,512]{2,1,0:T(8,128)(2,1)S(1)} %collective-permute-done.7._.refs_8_), channel_id=1, source_target_pairs={{0,2},{1,3},{2,0},{3,1},{4,6},{5,7},{6,4},{7,5},{8,10},{9,11},{10,... | collective-permute-start | bytes 589832 | tf_op jit(solution)/shard_map/ppermute | solution.py:22
  23.1 5.0 %collective-permute-start.8 = (bf16[2,64,512]{2,1,0:T(8,128)(2,1)S(1)}, bf16[2,64,512]{2,1,0:T(8,128)(2,1)S(1)}, u32[]{:S(2)}, u32[]{:S(2)}) collective-permute-start(bf16[2,64,512]{2,1,0:T(8,128)(2,1)S(1)} %hold.1.mine), channel_id=1, source_target_pairs={{0,8},{8,0},{16,24},{24,16},{1,9},{9,1},{17,25},{25,17},{2,10},{10... | collective-permute-start | bytes 393224 | tf_op jit(solution)/shard_map/ppermute | solution.py:22
  24.1 0.9 %copy-start.1 = (bf16[3,64,512]{2,1,0:T(8,128)(2,1)S(1)}, bf16[3,64,512]{2,1,0:T(8,128)(2,1)}, u32[]{:S(2)}) copy-start(bf16[3,64,512]{2,1,0:T(8,128)(2,1)} %get-tuple-element.21.refs_0_) | copy-start | bytes 589828
  25.0 5.3 %collective-permute-start.11 = (bf16[6,64,512]{2,1,0:T(8,128)(2,1)S(1)}, bf16[6,64,512]{2,1,0:T(8,128)(2,1)S(1)}, u32[]{:S(2)}, u32[]{:S(2)}) collective-permute-start(bf16[6,64,512]{2,1,0:T(8,128)(2,1)S(1)} %join.1.refs_6_), channel_id=1, source_target_pairs={{0,1},{1,0},{2,3},{3,2},{4,5},{5,4},{6,7},{7,6},{8,9},{9,8},{10,11... | collective-permute-start | bytes 1179656 | tf_op jit(solution)/shard_map/ppermute | solution.py:22
  25.2 4.9 %collective-permute-start.3 = (bf16[4,64,512]{2,1,0:T(8,128)(2,1)S(1)}, bf16[4,64,512]{2,1,0:T(8,128)(2,1)S(1)}, u32[]{:S(2)}, u32[]{:S(2)}) collective-permute-start(bf16[4,64,512]{2,1,0:T(8,128)(2,1)S(1)} %get-tuple-element.16), channel_id=1, source_target_pairs={{0,1},{1,0},{2,3},{3,2},{4,5},{5,4},{6,7},{7,6},{8,9},{9,8},{10,11... | collective-permute-start | bytes 786440 | tf_op jit(solution)/shard_map/ppermute | solution.py:22
  28.2 2.2 %collective-permute-start.9 = (bf16[4,64,512]{2,1,0:T(8,128)(2,1)S(1)}, bf16[4,64,512]{2,1,0:T(8,128)(2,1)S(1)}, u32[]{:S(2)}, u32[]{:S(2)}) collective-permute-start(bf16[4,64,512]{2,1,0:T(8,128)(2,1)S(1)} %get-tuple-element.20), channel_id=1, source_target_pairs={{0,1},{1,0},{2,3},{3,2},{4,5},{5,4},{6,7},{7,6},{8,9},{9,8},{10,11... | collective-permute-start | bytes 786440 | tf_op jit(solution)/shard_map/ppermute | solution.py:22
  28.3 1.8 %collective-permute-start.12 = (bf16[3,64,512]{2,1,0:T(8,128)(2,1)S(1)}, bf16[3,64,512]{2,1,0:T(8,128)(2,1)S(1)}, u32[]{:S(2)}, u32[]{:S(2)}) collective-permute-start(bf16[3,64,512]{2,1,0:T(8,128)(2,1)S(1)} %collective-permute-done.7._.refs_8_), channel_id=1, source_target_pairs={{0,1},{1,0},{2,3},{3,2},{4,5},{5,4},{6,7},{7,6},{8,9},{9,8},{10,11... | collective-permute-start | bytes 589832 | tf_op jit(solution)/shard_map/ppermute | solution.py:22
  28.8 1.6 %collective-permute-start.14 = (bf16[3,64,512]{2,1,0:T(8,128)(2,1)S(1)}, bf16[3,64,512]{2,1,0:T(8,128)(2,1)S(1)}, u32[]{:S(2)}, u32[]{:S(2)}) collective-permute-start(bf16[3,64,512]{2,1,0:T(8,128)(2,1)S(1)} %collective-permute-done.13.refs_10_), channel_id=1, source_target_pairs={{0,1},{1,0},{2,3},{3,2},{4,5},{5,4},{6,7},{7,6},{8,9},{9,8},{10,11... | collective-permute-start | bytes 589832 | tf_op jit(solution)/shard_map/ppermute | solution.py:22

commit v4 on v3

--- a/solution.py
+++ b/solution.py
@@ -13,7 +13,7 @@
 SMEM = pl.BlockSpec(memory_space=pltpu.SMEM)
 LIMIT = 16 * 1024 * 1024
 FIRST = 56418304
-SOLVE = 62914560
+SOLVE = 56152064
 SMALL = 8 * 1024 * 1024
 
 
@@ -42,31 +42,26 @@
         slabs[n][0] = product[n].astype(strips.dtype)
 
 
-def rest_kernel(classes, nonzero, panel, diag_inv, factor, mask, *refs):
+def rest_kernel(classes, nonzero, panel, diag_inv, _, mask, *refs):
     rests, (live, strips, inverse, sems) = refs[:-4], refs[-4:]
     load([(nonzero, live), (panel, strips), (diag_inv, inverse)], sems)
     steps, _, rows, size = strips.shape
     product = lax.dot_general(strips[...].reshape(steps * rows, size), inverse[...], TRANSPOSED,
                               preferred_element_type=jnp.float32).reshape(steps, rows, size)
     for s in range(steps):
-        factor[s, 0] = (product[s] * live[s].astype(jnp.float32)).astype(factor.dtype)
+        strips[s, 0] = (product[s] * live[s].astype(jnp.float32)).astype(strips.dtype)
     own = lax.axis_index("pcol") // lax.axis_size("prow")
     mask[...] = jnp.full(mask.shape, live[own].astype(jnp.float32), mask.dtype)
-    at = 0
     for n in range(classes):
-        m = 1
-        while m < steps:
-            for i in range(rests[at].shape[0]):
-                rests[at][i] = factor[lax.rem(jnp.bitwise_xor(own, n) + m + i, steps), 0]
-            m += rests[at].shape[0]
-            at += 1
-
-
-def solve_call(kernel, outs, scratch, copies, limit, args, name):
+        for m in range(1, steps):
+            rests[n][m - 1] = strips[lax.rem(jnp.bitwise_xor(own, n) + m, steps), 0]
+
+
+def solve_call(kernel, outs, scratch, copies, limit, args, name, inputs):
     return pl.pallas_call(
         kernel,
         out_shape=outs,
-        in_specs=[pl.BlockSpec(memory_space=pltpu.HBM)] * len(args),
+        in_specs=[pl.BlockSpec(memory_space=pltpu.HBM)] * inputs + [VMEM] * (len(args) - inputs),
         out_specs=[VMEM] * len(outs),
         scratch_shapes=scratch + [pltpu.SemaphoreType.DMA((copies,))],
         cost_estimate=pl.CostEstimate(flops=0, bytes_accessed=1024, transcendentals=0),
@@ -85,13 +80,11 @@
     inverse = pltpu.VMEM(diag_inv.shape, dtype)
     slabs = solve_call(functools.partial(first_kernel, classes), [slab] * classes,
                        [pltpu.VMEM((classes, rows, size), dtype), inverse], 1 + classes, FIRST,
-                       (panel, diag_inv), "solve_first")
-    factor, mask, *rests = solve_call(functools.partial(rest_kernel, classes),
-                                      [jax.ShapeDtypeStruct(panel.shape, dtype), mask] + rest,
-                                      [pltpu.SMEM((steps,), nonzero.dtype), pltpu.VMEM(panel.shape, dtype), inverse], 3,
-                                      SOLVE, (nonzero[:, 0], panel, diag_inv), "solve_rest")
-    far = len(cuts[-1])
-    return factor, mask, slabs, [rests[:1]] + [rests[i:i + far] for i in range(1, len(rests), far)]
+                       (panel, diag_inv), "solve_first", 2)
+    mask, *rests = solve_call(functools.partial(rest_kernel, classes), [mask] + rest,
+                              [pltpu.SMEM((steps,), nonzero.dtype), pltpu.VMEM(panel.shape, dtype), inverse], 3,
+                              SOLVE, (nonzero[:, 0], panel, diag_inv, slabs[0]), "solve_rest", 3)
+    return mask, slabs, [[x] for x in rests]
 
 
 def pick_kernel(sources, *refs):
@@ -187,6 +180,24 @@
 def masked(mask, parts):
     shape = jax.ShapeDtypeStruct((len(parts), *parts[0].shape[1:]), parts[0].dtype)
     return small_call(masked_kernel, shape, (mask, *parts), "masked")
+
+
+def finish_kernel(first, *refs):
+    pair, factor = refs[-2:]
+    join_kernel(*refs[:-1])
+    steps = factor.shape[0]
+    own = lax.axis_index("pcol") // lax.axis_size("prow")
+    factor[own, 0] = first[0]
+    for m in range(1, steps):
+        factor[lax.rem(own + m, steps), 0] = refs[0][m - 1]
+
+
+def finish(first, parts):
+    total = sum(x.shape[0] for x in parts)
+    steps, rows, size = parts[0].shape[0] + 1, *parts[0].shape[1:]
+    outs = [jax.ShapeDtypeStruct((total, rows, size), first.dtype),
+            jax.ShapeDtypeStruct((steps, 1, rows, size), first.dtype)]
+    return small_call(finish_kernel, outs, (first, *parts), "finish")
 
 
 def hold_kernel(x, _, out):
@@ -257,7 +268,7 @@
     chips = grid_cols // 2
     classes = max(1, grid_cols // grid_rows)
     steps = panel.shape[0]
-    factor, mask, slabs, rests = solve(panel, diag_inv, nonzero, classes)
+    mask, slabs, rests = solve(panel, diag_inv, nonzero, classes)
     slabs = list(slabs)
 
     def kind(k):
@@ -316,7 +327,8 @@
         use(first, [(0, 0, k) for k in group])
         use(swap(packed, "pcol", 1), [(None, 1, k) for k in group] + [(0, 1, k) for k in group])
     joined = [0] + close
-    both(join([rest[k] for k in joined]), [(m, k) for k in joined for m in range(1, steps)])
+    pair, factor = finish(firsts[0], [rest[k] for k in joined])
+    both(pair, [(m, k) for k in joined for m in range(1, steps)])
     for k in far:
         m = 1
         for i, cut in enumerate(cuts):
@@ -326,13 +338,13 @@
     return factor, renewed
 
 
-GX = (1,)
-
-
-PREL = True
+GX = None
+
+
+PREL = False
 QREL = True
 GROUPS = 2
-G1 = None
+G1 = 'a'
 G2 = None
 XY = 'hyper'
 

time: 32.8 us -> 32.6 us (level)
  local copies, waits for them, and re-layouts: 1.6 us -> 0.66 us
  Pallas kernels: 6.11 us -> 6.71 us
    unnamed x6 -> x4, local copies, waits for them, and re-layouts: 1.6 us -> 0.66 us
    pallas_call x7, Pallas kernels: 0.16 us -> 0.88 us  [small_call(): pl.pallas_call(kernel, out_shape=outs, in_specs=[VMEM] * len(args), out_s...]
  transfers between devices with their start and end apart: 15 -> 15, of which waited for: 6 -> 5; matrix products, arithmetic and copies ran while one was open for 0% -> 0% of each run, Pallas kernels for 8% -> 10%
where the time goes in v4:
time: 32.6 us; the launch traced here: 32.4 us
  starting transfers between devices  16.7 us (51%)
  waiting for transfers between devices  7.61 us (23%)
  Pallas kernels  6.71 us (21%)
  between operations  0.74 us (2%)
  local copies, waits for them, and re-layouts  0.66 us (2%)
    ppermute x15, starting transfers between devices, swap(): return lax.ppermute(x, axis, [(i, i ^ distance) for i in range(size)])  16.7 us
    ppermute x15, waiting for transfers between devices, swap(): return lax.ppermute(x, axis, [(i, i ^ distance) for i in range(size)])  7.61 us
    pallas_call x2, Pallas kernels, solve_call(): pl.pallas_call(kernel, out_shape=outs, in_specs=[pl.BlockSpec(memory_spac...  3.58 us
    pallas_call x1, Pallas kernels, renew(): pl.pallas_call(functools.partial(renew_kernel, plan, chips), out_shape=ja...  2.25 us
    pallas_call x7, Pallas kernels, small_call(): pl.pallas_call(kernel, out_shape=outs, in_specs=[VMEM] * len(args), out_s...  0.88 us
    unnamed x4, local copies, waits for them, and re-layouts  0.66 us
  transfers between devices with their start and end apart: 15, of which 5 were waited for; matrix products, arithmetic and copies ran while one was open for 0% of the time, Pallas kernels for 10%

profile of v4, /device:TPU:0, one launch (start us, length us, event | category | flops | bytes accessed | tf_op | source)
XLA Modules:
  0.0 32.4 jit_solution(9547496439465772146)
XLA Ops:
  0.6 1.4 %solve_first.1 = (bf16[1,64,512]{2,1,0:T(8,128)(2,1)S(1)}, bf16[1,64,512]{2,1,0:T(8,128)(2,1)S(1)}) custom-call(bf16[4,1,64,512]{3,2,1,0:T(8,128)(2,1)} %panel.3, bf16[512,512]{1,0:T(8,128)(2,1)} %diag_inv.3), custom_call_target="tpu_custom_call" | custom-call | bytes 1024 | tf_op jit(solution)/shard_map/solve_first/pallas_call | solution.py:61
  2.0 3.1 %collective-permute-start = (bf16[1,64,512]{2,1,0:T(8,128)(2,1)S(1)}, bf16[1,64,512]{2,1,0:T(8,128)(2,1)S(1)}, u32[]{:S(2)}, u32[]{:S(2)}) collective-permute-start(bf16[1,64,512]{2,1,0:T(8,128)(2,1)S(1)} %get-tuple-element.13._.refs_0_), channel_id=1, source_target_pairs={{0,2},{1,3},{2,0},{3,1},{4,6},{5,7},{6,4},{7,5},{8,10},{9,11},{10,... | collective-permute-start | bytes 196616 | tf_op jit(solution)/shard_map/ppermute | solution.py:22
  5.1 2.5 %collective-permute-start.6 = (bf16[1,64,512]{2,1,0:T(8,128)(2,1)S(1)}, bf16[1,64,512]{2,1,0:T(8,128)(2,1)S(1)}, u32[]{:S(2)}, u32[]{:S(2)}) collective-permute-start(bf16[1,64,512]{2,1,0:T(8,128)(2,1)S(1)} %get-tuple-element.19), channel_id=1, source_target_pairs={{0,6},{1,7},{2,4},{3,5},{4,2},{5,3},{6,0},{7,1},{8,14},{9,15},{10,... | collective-permute-start | bytes 196616 | tf_op jit(solution)/shard_map/ppermute | solution.py:22
  7.6 0.1 collective-permute-start.5
  7.7 0.7 %copy-done.1 = s32[4,1]{0,1:T(1,128)S(1)} copy-done((s32[4,1]{0,1:T(1,128)S(1)}, s32[4,1]{0,1:T(1,128)}, u32[]{:S(2)}) %copy-start.1) | copy-done | bytes 40
  8.4 2.2 %solve_rest.1 = (f32[1,512]{1,0:T(1,128)S(1)}, bf16[3,64,512]{2,1,0:T(8,128)(2,1)S(1)}, bf16[3,64,512]{2,1,0:T(8,128)(2,1)}) custom-call(s32[4]{0:T(128)S(1)} %bitcast.1, bf16[4,1,64,512]{3,2,1,0:T(8,128)(2,1)} %panel.3, bf16[512,512]{1,0:T(8,128)(2,1)} %diag_inv.3, bf16[1,64,512]{2,1,0:T(8,128)(2,1)S(1)} %get-tuple-element.13._.refs_0_), custom_call_target="tpu_custom_call" | custom-call | bytes 1024 | tf_op jit(solution)/shard_map/solve_rest/pallas_call | solution.py:61
  10.6 2.9 %collective-permute-start.11 = (bf16[3,64,512]{2,1,0:T(8,128)(2,1)}, bf16[3,64,512]{2,1,0:T(8,128)(2,1)S(1)}, u32[]{:S(2)}, u32[]{:S(2)}) collective-permute-start(bf16[3,64,512]{2,1,0:T(8,128)(2,1)} %get-tuple-element.23), channel_id=1, source_target_pairs={{0,4},{1,5},{2,6},{3,7},{4,0},{5,1},{6,2},{7,3},{8,12},{9,13},{10,... | collective-permute-start | bytes 589832 | tf_op jit(solution)/shard_map/ppermute | solution.py:22
  13.5 0.7 %collective-permute-start.1 = (bf16[3,64,512]{2,1,0:T(8,128)(2,1)S(1)}, bf16[3,64,512]{2,1,0:T(8,128)(2,1)S(1)}, u32[]{:S(2)}, u32[]{:S(2)}) collective-permute-start(bf16[3,64,512]{2,1,0:T(8,128)(2,1)S(1)} %hold.1.refs_0_), channel_id=1, source_target_pairs={{0,2},{1,3},{2,0},{3,1},{4,6},{5,7},{6,4},{7,5},{8,10},{9,11},{10,... | collective-permute-start | bytes 589832 | tf_op jit(solution)/shard_map/ppermute | solution.py:22
  14.2 1.5 %collective-permute-start.2 = (bf16[2,64,512]{2,1,0:T(8,128)(2,1)S(1)}, bf16[2,64,512]{2,1,0:T(8,128)(2,1)S(1)}, u32[]{:S(2)}, u32[]{:S(2)}) collective-permute-start(bf16[2,64,512]{2,1,0:T(8,128)(2,1)S(1)} %masked.2._.first.mine.refs_1_), channel_id=1, source_target_pairs={{0,16},{8,24},{16,0},{24,8},{1,17},{9,25},{17,1},{25,9},{2,18},{10... | collective-permute-start | bytes 393224 | tf_op jit(solution)/shard_map/ppermute | solution.py:22
  15.8 0.6 %collective-permute-start.7 = (bf16[2,64,512]{2,1,0:T(8,128)(2,1)S(1)}, bf16[2,64,512]{2,1,0:T(8,128)(2,1)S(1)}, u32[]{:S(2)}, u32[]{:S(2)}) collective-permute-start(bf16[2,64,512]{2,1,0:T(8,128)(2,1)S(1)} %masked.3.mine.first.refs_4_), channel_id=1, source_target_pairs={{0,16},{8,24},{16,0},{24,8},{1,17},{9,25},{17,1},{25,9},{2,18},{10... | collective-permute-start | bytes 393224 | tf_op jit(solution)/shard_map/ppermute | solution.py:22
  16.4 3.2 %collective-permute-done.2.came = bf16[2,64,512]{2,1,0:T(8,128)(2,1)S(1)} collective-permute-done((bf16[2,64,512]{2,1,0:T(8,128)(2,1)S(1)}, bf16[2,64,512]{2,1,0:T(8,128)(2,1)S(1)}, u32[]{:S(2)}, u32[]{:S(2)}) %collective-permute-start.2) | collective-permute-done | bytes 131104 | tf_op jit(solution)/shard_map/ppermute | solution.py:22
  19.5 1.6 %collective-permute-start.3 = (bf16[2,64,512]{2,1,0:T(8,128)(2,1)S(1)}, bf16[2,64,512]{2,1,0:T(8,128)(2,1)S(1)}, u32[]{:S(2)}, u32[]{:S(2)}) collective-permute-start(bf16[2,64,512]{2,1,0:T(8,128)(2,1)S(1)} %choose.2.mine), channel_id=1, source_target_pairs={{0,8},{8,0},{16,24},{24,16},{1,9},{9,1},{17,25},{25,17},{2,10},{10... | collective-permute-start | bytes 393224 | tf_op jit(solution)/shard_map/ppermute | solution.py:22
  21.1 1.4 %collective-permute-start.8 = (bf16[2,64,512]{2,1,0:T(8,128)(2,1)S(1)}, bf16[2,64,512]{2,1,0:T(8,128)(2,1)S(1)}, u32[]{:S(2)}, u32[]{:S(2)}) collective-permute-start(bf16[2,64,512]{2,1,0:T(8,128)(2,1)S(1)} %choose.3.mine), channel_id=1, source_target_pairs={{0,8},{8,0},{16,24},{24,16},{1,9},{9,1},{17,25},{25,17},{2,10},{10... | collective-permute-start | bytes 393224 | tf_op jit(solution)/shard_map/ppermute | solution.py:22
  22.5 0.1 collective-permute-done.11.refs_8_
  22.6 1.2 %collective-permute-start.13 = (bf16[3,64,512]{2,1,0:T(8,128)(2,1)S(1)}, bf16[3,64,512]{2,1,0:T(8,128)(2,1)S(1)}, u32[]{:S(2)}, u32[]{:S(2)}) collective-permute-start(bf16[3,64,512]{2,1,0:T(8,128)(2,1)S(1)} %collective-permute-done.11.refs_8_), channel_id=1, source_target_pairs={{0,2},{1,3},{2,0},{3,1},{4,6},{5,7},{6,4},{7,5},{8,10},{9,11},{10,... | collective-permute-start | bytes 589832 | tf_op jit(solution)/shard_map/ppermute | solution.py:22
  23.8 0.7 %finish.1 = (bf16[6,64,512]{2,1,0:T(8,128)(2,1)S(1)}, bf16[4,1,64,512]{3,2,1,0:T(8,128)(2,1)}) custom-call(bf16[2,64,512]{2,1,0:T(8,128)(2,1)S(1)} %masked.2._.first.mine.refs_1_, bf16[3,64,512]{2,1,0:T(8,128)(2,1)S(1)} %hold.1.refs_0_, bf16[3,64,512]{2,1,0:T(8,128)(2,1)S(1)} %collective-permute-done.1.refs_1_), custom_call_target="tpu_custom_call" | custom-call | bytes 1024 | tf_op jit(solution)/shard_map/finish/pallas_call | solution.py:112
  24.6 0.0 collective-permute-done.3.came
  24.6 0.6 %collective-permute-start.4 = (bf16[4,64,512]{2,1,0:T(8,128)(2,1)S(1)}, bf16[4,64,512]{2,1,0:T(8,128)(2,1)S(1)}, u32[]{:S(2)}, u32[]{:S(2)}) collective-permute-start(bf16[4,64,512]{2,1,0:T(8,128)(2,1)S(1)} %get-tuple-element.18), channel_id=1, source_target_pairs={{0,1},{1,0},{2,3},{3,2},{4,5},{5,4},{6,7},{7,6},{8,9},{9,8},{10,11... | collective-permute-start | bytes 786440 | tf_op jit(solution)/shard_map/ppermute | solution.py:22
  25.2 1.0 %collective-permute-done.8.came = bf16[2,64,512]{2,1,0:T(8,128)(2,1)S(1)} collective-permute-done((bf16[2,64,512]{2,1,0:T(8,128)(2,1)S(1)}, bf16[2,64,512]{2,1,0:T(8,128)(2,1)S(1)}, u32[]{:S(2)}, u32[]{:S(2)}) %collective-permute-start.8) | collective-permute-done | bytes 131104 | tf_op jit(solution)/shard_map/ppermute | solution.py:22
  26.2 0.1 collective-permute-start.9
  26.3 0.5 %collective-permute-start.12 = (bf16[3,64,512]{2,1,0:T(8,128)(2,1)S(1)}, bf16[3,64,512]{2,1,0:T(8,128)(2,1)S(1)}, u32[]{:S(2)}, u32[]{:S(2)}) collective-permute-start(bf16[3,64,512]{2,1,0:T(8,128)(2,1)S(1)} %collective-permute-done.11.refs_8_), channel_id=1, source_target_pairs={{0,1},{1,0},{2,3},{3,2},{4,5},{5,4},{6,7},{7,6},{8,9},{9,8},{10,11... | collective-permute-start | bytes 589832 | tf_op jit(solution)/shard_map/ppermute | solution.py:22
  26.8 1.9 %collective-permute-done.13.refs_10_ = bf16[3,64,512]{2,1,0:T(8,128)(2,1)S(1)} collective-permute-done((bf16[3,64,512]{2,1,0:T(8,128)(2,1)S(1)}, bf16[3,64,512]{2,1,0:T(8,128)(2,1)S(1)}, u32[]{:S(2)}, u32[]{:S(2)}) %collective-permute-start.13) | collective-permute-done | bytes 196640 | tf_op jit(solution)/shard_map/ppermute | solution.py:22
  28.7 1.4 %collective-permute-done.14.refs_11_ = bf16[3,64,512]{2,1,0:T(8,128)(2,1)S(1)} collective-permute-done((bf16[3,64,512]{2,1,0:T(8,128)(2,1)S(1)}, bf16[3,64,512]{2,1,0:T(8,128)(2,1)S(1)}, u32[]{:S(2)}, u32[]{:S(2)}) %collective-permute-start.14) | collective-permute-done | bytes 196640 | tf_op jit(solution)/shard_map/ppermute | solution.py:22
  30.1 2.3 %renew.1 = bf16[4,1,1,1,512,512]{5,4,3,2,1,0:T(8,128)(2,1)} custom-call(bf16[2,64,512]{2,1,0:T(8,128)(2,1)S(1)} %get-tuple-element.17.refs_0_, bf16[2,64,512]{2,1,0:T(8,128)(2,1)S(1)} %masked.2._.first.mine.refs_1_, bf16[4,64,512]{2,1,0:T(8,128)(2,1)S(1)} %collective-permute-done.4.refs_2_, bf16[2,64,512]{2,1,0:T(8,128)(2,1)S(1)} %get-tuple-element.20.refs_3_, ...), custom_call_target="tpu_custom_call" | custom-call | tf_op jit(solution)/shard_map/renew/pallas_call | solution.py:250
  (21 shorter events, 0.2 us)
Async XLA Ops:
  2.0 28.1 %copy-start = (bf16[4,1,1,1,512,512]{5,4,3,2,1,0:T(8,128)(2,1)S(1)}, bf16[4,1,1,1,512,512]{5,4,3,2,1,0:T(8,128)(2,1)}, u32[]{:S(2)}) copy-start(bf16[4,1,1,1,512,512]{5,4,3,2,1,0:T(8,128)(2,1)} %refs_12_.1) | copy-start | bytes 6291460
  2.0 11.4 %collective-permute-start = (bf16[1,64,512]{2,1,0:T(8,128)(2,1)S(1)}, bf16[1,64,512]{2,1,0:T(8,128)(2,1)S(1)}, u32[]{:S(2)}, u32[]{:S(2)}) collective-permute-start(bf16[1,64,512]{2,1,0:T(8,128)(2,1)S(1)} %get-tuple-element.13._.refs_0_), channel_id=1, source_target_pairs={{0,2},{1,3},{2,0},{3,1},{4,6},{5,7},{6,4},{7,5},{8,10},{9,11},{10,... | collective-permute-start | bytes 196616 | tf_op jit(solution)/shard_map/ppermute | solution.py:22
  5.1 10.6 %collective-permute-start.6 = (bf16[1,64,512]{2,1,0:T(8,128)(2,1)S(1)}, bf16[1,64,512]{2,1,0:T(8,128)(2,1)S(1)}, u32[]{:S(2)}, u32[]{:S(2)}) collective-permute-start(bf16[1,64,512]{2,1,0:T(8,128)(2,1)S(1)} %get-tuple-element.19), channel_id=1, source_target_pairs={{0,6},{1,7},{2,4},{3,5},{4,2},{5,3},{6,0},{7,1},{8,14},{9,15},{10,... | collective-permute-start | bytes 196616 | tf_op jit(solution)/shard_map/ppermute | solution.py:22
  7.6 8.2 %collective-permute-start.5 = (bf16[1,64,512]{2,1,0:T(8,128)(2,1)S(1)}, bf16[1,64,512]{2,1,0:T(8,128)(2,1)S(1)}, u32[]{:S(2)}, u32[]{:S(2)}) collective-permute-start(bf16[1,64,512]{2,1,0:T(8,128)(2,1)S(1)} %get-tuple-element.19), channel_id=1, source_target_pairs={{0,4},{1,5},{2,6},{3,7},{4,0},{5,1},{6,2},{7,3},{8,12},{9,13},{10,... | collective-permute-start | bytes 196616 | tf_op jit(solution)/shard_map/ppermute | solution.py:22
  7.7 0.7 %copy-start.1 = (s32[4,1]{0,1:T(1,128)S(1)}, s32[4,1]{0,1:T(1,128)}, u32[]{:S(2)}) copy-start(s32[4,1]{0,1:T(1,128)} %param.6) | copy-start | bytes 52
  10.6 12.0 %collective-permute-start.11 = (bf16[3,64,512]{2,1,0:T(8,128)(2,1)}, bf16[3,64,512]{2,1,0:T(8,128)(2,1)S(1)}, u32[]{:S(2)}, u32[]{:S(2)}) collective-permute-start(bf16[3,64,512]{2,1,0:T(8,128)(2,1)} %get-tuple-element.23), channel_id=1, source_target_pairs={{0,4},{1,5},{2,6},{3,7},{4,0},{5,1},{6,2},{7,3},{8,12},{9,13},{10,... | collective-permute-start | bytes 589832 | tf_op jit(solution)/shard_map/ppermute | solution.py:22
  13.5 10.3 %collective-permute-start.1 = (bf16[3,64,512]{2,1,0:T(8,128)(2,1)S(1)}, bf16[3,64,512]{2,1,0:T(8,128)(2,1)S(1)}, u32[]{:S(2)}, u32[]{:S(2)}) collective-permute-start(bf16[3,64,512]{2,1,0:T(8,128)(2,1)S(1)} %hold.1.refs_0_), channel_id=1, source_target_pairs={{0,2},{1,3},{2,0},{3,1},{4,6},{5,7},{6,4},{7,5},{8,10},{9,11},{10,... | collective-permute-start | bytes 589832 | tf_op jit(solution)/shard_map/ppermute | solution.py:22
  14.2 5.3 %collective-permute-start.2 = (bf16[2,64,512]{2,1,0:T(8,128)(2,1)S(1)}, bf16[2,64,512]{2,1,0:T(8,128)(2,1)S(1)}, u32[]{:S(2)}, u32[]{:S(2)}) collective-permute-start(bf16[2,64,512]{2,1,0:T(8,128)(2,1)S(1)} %masked.2._.first.mine.refs_1_), channel_id=1, source_target_pairs={{0,16},{8,24},{16,0},{24,8},{1,17},{9,25},{17,1},{25,9},{2,18},{10... | collective-permute-start | bytes 393224 | tf_op jit(solution)/shard_map/ppermute | solution.py:22
  15.8 5.3 %collective-permute-start.7 = (bf16[2,64,512]{2,1,0:T(8,128)(2,1)S(1)}, bf16[2,64,512]{2,1,0:T(8,128)(2,1)S(1)}, u32[]{:S(2)}, u32[]{:S(2)}) collective-permute-start(bf16[2,64,512]{2,1,0:T(8,128)(2,1)S(1)} %masked.3.mine.first.refs_4_), channel_id=1, source_target_pairs={{0,16},{8,24},{16,0},{24,8},{1,17},{9,25},{17,1},{25,9},{2,18},{10... | collective-permute-start | bytes 393224 | tf_op jit(solution)/shard_map/ppermute | solution.py:22
  19.5 5.0 %collective-permute-start.3 = (bf16[2,64,512]{2,1,0:T(8,128)(2,1)S(1)}, bf16[2,64,512]{2,1,0:T(8,128)(2,1)S(1)}, u32[]{:S(2)}, u32[]{:S(2)}) collective-permute-start(bf16[2,64,512]{2,1,0:T(8,128)(2,1)S(1)} %choose.2.mine), channel_id=1, source_target_pairs={{0,8},{8,0},{16,24},{24,16},{1,9},{9,1},{17,25},{25,17},{2,10},{10... | collective-permute-start | bytes 393224 | tf_op jit(solution)/shard_map/ppermute | solution.py:22
  21.1 5.0 %collective-permute-start.8 = (bf16[2,64,512]{2,1,0:T(8,128)(2,1)S(1)}, bf16[2,64,512]{2,1,0:T(8,128)(2,1)S(1)}, u32[]{:S(2)}, u32[]{:S(2)}) collective-permute-start(bf16[2,64,512]{2,1,0:T(8,128)(2,1)S(1)} %choose.3.mine), channel_id=1, source_target_pairs={{0,8},{8,0},{16,24},{24,16},{1,9},{9,1},{17,25},{25,17},{2,10},{10... | collective-permute-start | bytes 393224 | tf_op jit(solution)/shard_map/ppermute | solution.py:22
  22.6 6.1 %collective-permute-start.13 = (bf16[3,64,512]{2,1,0:T(8,128)(2,1)S(1)}, bf16[3,64,512]{2,1,0:T(8,128)(2,1)S(1)}, u32[]{:S(2)}, u32[]{:S(2)}) collective-permute-start(bf16[3,64,512]{2,1,0:T(8,128)(2,1)S(1)} %collective-permute-done.11.refs_8_), channel_id=1, source_target_pairs={{0,2},{1,3},{2,0},{3,1},{4,6},{5,7},{6,4},{7,5},{8,10},{9,11},{10,... | collective-permute-start | bytes 589832 | tf_op jit(solution)/shard_map/ppermute | solution.py:22
  24.5 5.6 %collective-permute-start.10 = (bf16[6,64,512]{2,1,0:T(8,128)(2,1)S(1)}, bf16[6,64,512]{2,1,0:T(8,128)(2,1)S(1)}, u32[]{:S(2)}, u32[]{:S(2)}) collective-permute-start(bf16[6,64,512]{2,1,0:T(8,128)(2,1)S(1)} %get-tuple-element.22.refs_6_), channel_id=1, source_target_pairs={{0,1},{1,0},{2,3},{3,2},{4,5},{5,4},{6,7},{7,6},{8,9},{9,8},{10,11... | collective-permute-start | bytes 1179656 | tf_op jit(solution)/shard_map/ppermute | solution.py:22
  24.6 4.1 %collective-permute-start.4 = (bf16[4,64,512]{2,1,0:T(8,128)(2,1)S(1)}, bf16[4,64,512]{2,1,0:T(8,128)(2,1)S(1)}, u32[]{:S(2)}, u32[]{:S(2)}) collective-permute-start(bf16[4,64,512]{2,1,0:T(8,128)(2,1)S(1)} %get-tuple-element.18), channel_id=1, source_target_pairs={{0,1},{1,0},{2,3},{3,2},{4,5},{5,4},{6,7},{7,6},{8,9},{9,8},{10,11... | collective-permute-start | bytes 786440 | tf_op jit(solution)/shard_map/ppermute | solution.py:22
  26.2 2.5 %collective-permute-start.9 = (bf16[4,64,512]{2,1,0:T(8,128)(2,1)S(1)}, bf16[4,64,512]{2,1,0:T(8,128)(2,1)S(1)}, u32[]{:S(2)}, u32[]{:S(2)}) collective-permute-start(bf16[4,64,512]{2,1,0:T(8,128)(2,1)S(1)} %get-tuple-element.21), channel_id=1, source_target_pairs={{0,1},{1,0},{2,3},{3,2},{4,5},{5,4},{6,7},{7,6},{8,9},{9,8},{10,11... | collective-permute-start | bytes 786440 | tf_op jit(solution)/shard_map/ppermute | solution.py:22
  26.3 2.4 %collective-permute-start.12 = (bf16[3,64,512]{2,1,0:T(8,128)(2,1)S(1)}, bf16[3,64,512]{2,1,0:T(8,128)(2,1)S(1)}, u32[]{:S(2)}, u32[]{:S(2)}) collective-permute-start(bf16[3,64,512]{2,1,0:T(8,128)(2,1)S(1)} %collective-permute-done.11.refs_8_), channel_id=1, source_target_pairs={{0,1},{1,0},{2,3},{3,2},{4,5},{5,4},{6,7},{7,6},{8,9},{9,8},{10,11... | collective-permute-start | bytes 589832 | tf_op jit(solution)/shard_map/ppermute | solution.py:22
  28.7 1.4 %collective-permute-start.14 = (bf16[3,64,512]{2,1,0:T(8,128)(2,1)S(1)}, bf16[3,64,512]{2,1,0:T(8,128)(2,1)S(1)}, u32[]{:S(2)}, u32[]{:S(2)}) collective-permute-start(bf16[3,64,512]{2,1,0:T(8,128)(2,1)S(1)} %collective-permute-done.13.refs_10_), channel_id=1, source_target_pairs={{0,1},{1,0},{2,3},{3,2},{4,5},{5,4},{6,7},{7,6},{8,9},{9,8},{10,11... | collective-permute-start | bytes 589832 | tf_op jit(solution)/shard_map/ppermute | solution.py:22

commit v5 on v4

--- a/solution.py
+++ b/solution.py
@@ -42,7 +42,7 @@
         slabs[n][0] = product[n].astype(strips.dtype)
 
 
-def rest_kernel(classes, nonzero, panel, diag_inv, _, mask, *refs):
+def rest_kernel(classes, nonzero, panel, diag_inv, mask, *refs):
     rests, (live, strips, inverse, sems) = refs[:-4], refs[-4:]
     load([(nonzero, live), (panel, strips), (diag_inv, inverse)], sems)
     steps, _, rows, size = strips.shape
@@ -57,11 +57,11 @@
             rests[n][m - 1] = strips[lax.rem(jnp.bitwise_xor(own, n) + m, steps), 0]
 
 
-def solve_call(kernel, outs, scratch, copies, limit, args, name, inputs):
+def solve_call(kernel, outs, scratch, copies, limit, args, name):
     return pl.pallas_call(
         kernel,
         out_shape=outs,
-        in_specs=[pl.BlockSpec(memory_space=pltpu.HBM)] * inputs + [VMEM] * (len(args) - inputs),
+        in_specs=[pl.BlockSpec(memory_space=pltpu.HBM)] * len(args),
         out_specs=[VMEM] * len(outs),
         scratch_shapes=scratch + [pltpu.SemaphoreType.DMA((copies,))],
         cost_estimate=pl.CostEstimate(flops=0, bytes_accessed=1024, transcendentals=0),
@@ -80,10 +80,10 @@
     inverse = pltpu.VMEM(diag_inv.shape, dtype)
     slabs = solve_call(functools.partial(first_kernel, classes), [slab] * classes,
                        [pltpu.VMEM((classes, rows, size), dtype), inverse], 1 + classes, FIRST,
-                       (panel, diag_inv), "solve_first", 2)
+                       (panel, diag_inv), "solve_first")
     mask, *rests = solve_call(functools.partial(rest_kernel, classes), [mask] + rest,
                               [pltpu.SMEM((steps,), nonzero.dtype), pltpu.VMEM(panel.shape, dtype), inverse], 3,
-                              SOLVE, (nonzero[:, 0], panel, diag_inv, slabs[0]), "solve_rest", 3)
+                              SOLVE, (nonzero[:, 0], panel, diag_inv), "solve_rest")
     return mask, slabs, [[x] for x in rests]
 
 
@@ -344,7 +344,7 @@
 PREL = False
 QREL = True
 GROUPS = 2
-G1 = 'a'
+G1 = 'b'
 G2 = None
 XY = 'hyper'
 

time: 32.6 us -> 32.2 us (0.988)
  starting transfers between devices: 16.7 us -> 17.5 us
  Pallas kernels: 6.71 us -> 6.04 us
  waiting for transfers between devices: 7.61 us -> 7.12 us
    ppermute x15, starting transfers between devices: 16.7 us -> 17.5 us  [swap(): return lax.ppermute(x, axis, [(i, i ^ distance) for i in range(size)])]
    pallas_call x2, Pallas kernels: 3.58 us -> 2.9 us  [solve_call(): pl.pallas_call(kernel, out_shape=outs, in_specs=[pl.BlockSpec(memory_spac...]
    ppermute x15, waiting for transfers between devices: 7.61 us -> 7.12 us  [swap(): return lax.ppermute(x, axis, [(i, i ^ distance) for i in range(size)])]
  transfers between devices with their start and end apart: 15 -> 15, of which waited for: 5 -> 5; matrix products, arithmetic and copies ran while one was open for 0% -> 0% of each run, Pallas kernels for 10% -> 7%
where the time goes in v5:
time: 32.2 us; the launch traced here: 32.1 us
  starting transfers between devices  17.5 us (54%)
  waiting for transfers between devices  7.12 us (22%)
  Pallas kernels  6.04 us (19%)
  between operations  0.74 us (2%)
  local copies, waits for them, and re-layouts  0.66 us (2%)
    ppermute x15, starting transfers between devices, swap(): return lax.ppermute(x, axis, [(i, i ^ distance) for i in range(size)])  17.5 us
    ppermute x15, waiting for transfers between devices, swap(): return lax.ppermute(x, axis, [(i, i ^ distance) for i in range(size)])  7.12 us
    pallas_call x2, Pallas kernels, solve_call(): pl.pallas_call(kernel, out_shape=outs, in_specs=[pl.BlockSpec(memory_spac...  2.9 us
    pallas_call x1, Pallas kernels, renew(): pl.pallas_call(functools.partial(renew_kernel, plan, chips), out_shape=ja...  2.25 us
    pallas_call x7, Pallas kernels, small_call(): pl.pallas_call(kernel, out_shape=outs, in_specs=[VMEM] * len(args), out_s...  0.88 us
    unnamed x4, local copies, waits for them, and re-layouts  0.66 us
  transfers between devices with their start and end apart: 15, of which 5 were waited for; matrix products, arithmetic and copies ran while one was open for 0% of the time, Pallas kernels for 7%

profile of v5, /device:TPU:0, one launch (start us, length us, event | category | flops | bytes accessed | tf_op | source)
XLA Modules:
  0.0 32.1 jit_solution(6396594129462658643)
XLA Ops:
  0.6 1.4 %solve_first.1 = (bf16[1,64,512]{2,1,0:T(8,128)(2,1)S(1)}, bf16[1,64,512]{2,1,0:T(8,128)(2,1)S(1)}) custom-call(bf16[4,1,64,512]{3,2,1,0:T(8,128)(2,1)} %panel.3, bf16[512,512]{1,0:T(8,128)(2,1)} %diag_inv.3), custom_call_target="tpu_custom_call" | custom-call | bytes 1024 | tf_op jit(solution)/shard_map/solve_first/pallas_call | solution.py:61
  2.0 0.0 copy-start
  2.0 5.1 %collective-permute-start.2 = (bf16[1,64,512]{2,1,0:T(8,128)(2,1)S(1)}, bf16[1,64,512]{2,1,0:T(8,128)(2,1)S(1)}, u32[]{:S(2)}, u32[]{:S(2)}) collective-permute-start(bf16[1,64,512]{2,1,0:T(8,128)(2,1)S(1)} %get-tuple-element.16), channel_id=1, source_target_pairs={{0,6},{1,7},{2,4},{3,5},{4,2},{5,3},{6,0},{7,1},{8,14},{9,15},{10,... | collective-permute-start | bytes 196616 | tf_op jit(solution)/shard_map/ppermute | solution.py:22
  7.1 0.6 %collective-permute-start = (bf16[1,64,512]{2,1,0:T(8,128)(2,1)S(1)}, bf16[1,64,512]{2,1,0:T(8,128)(2,1)S(1)}, u32[]{:S(2)}, u32[]{:S(2)}) collective-permute-start(bf16[1,64,512]{2,1,0:T(8,128)(2,1)S(1)} %get-tuple-element.14.refs_0_), channel_id=1, source_target_pairs={{0,2},{1,3},{2,0},{3,1},{4,6},{5,7},{6,4},{7,5},{8,10},{9,11},{10,... | collective-permute-start | bytes 196616 | tf_op jit(solution)/shard_map/ppermute | solution.py:22
  7.8 0.7 %copy-done.1 = s32[4,1]{0,1:T(1,128)S(1)} copy-done((s32[4,1]{0,1:T(1,128)S(1)}, s32[4,1]{0,1:T(1,128)}, u32[]{:S(2)}) %copy-start.1) | copy-done | bytes 40
  8.4 1.5 %solve_rest.1 = (f32[1,512]{1,0:T(1,128)S(1)}, bf16[3,64,512]{2,1,0:T(8,128)(2,1)S(1)}, bf16[3,64,512]{2,1,0:T(8,128)(2,1)S(1)}) custom-call(s32[4]{0:T(128)S(1)} %bitcast.1, bf16[4,1,64,512]{3,2,1,0:T(8,128)(2,1)} %panel.3, bf16[512,512]{1,0:T(8,128)(2,1)} %diag_inv.3), custom_call_target="tpu_custom_call" | custom-call | bytes 1024 | tf_op jit(solution)/shard_map/solve_rest/pallas_call | solution.py:61
  10.0 2.4 %collective-permute-start.11 = (bf16[3,64,512]{2,1,0:T(8,128)(2,1)S(1)}, bf16[3,64,512]{2,1,0:T(8,128)(2,1)S(1)}, u32[]{:S(2)}, u32[]{:S(2)}) collective-permute-start(bf16[3,64,512]{2,1,0:T(8,128)(2,1)S(1)} %get-tuple-element.23), channel_id=1, source_target_pairs={{0,4},{1,5},{2,6},{3,7},{4,0},{5,1},{6,2},{7,3},{8,12},{9,13},{10,... | collective-permute-start | bytes 589832 | tf_op jit(solution)/shard_map/ppermute | solution.py:22
  12.3 0.0 collective-permute-done.2.refs_1_
  12.3 0.4 %collective-permute-done.1.refs_0_ = bf16[1,64,512]{2,1,0:T(8,128)(2,1)S(1)} collective-permute-done((bf16[1,64,512]{2,1,0:T(8,128)(2,1)S(1)}, bf16[1,64,512]{2,1,0:T(8,128)(2,1)S(1)}, u32[]{:S(2)}, u32[]{:S(2)}) %collective-permute-start.1) | collective-permute-done | bytes 65568 | tf_op jit(solution)/shard_map/ppermute | solution.py:22
  12.8 1.7 %collective-permute-start.3 = (bf16[3,64,512]{2,1,0:T(8,128)(2,1)S(1)}, bf16[3,64,512]{2,1,0:T(8,128)(2,1)S(1)}, u32[]{:S(2)}, u32[]{:S(2)}) collective-permute-start(bf16[3,64,512]{2,1,0:T(8,128)(2,1)S(1)} %hold.1.refs_0_), channel_id=1, source_target_pairs={{0,2},{1,3},{2,0},{3,1},{4,6},{5,7},{6,4},{7,5},{8,10},{9,11},{10,... | collective-permute-start | bytes 589832 | tf_op jit(solution)/shard_map/ppermute | solution.py:22
  14.5 1.5 %collective-permute-start.7 = (bf16[2,64,512]{2,1,0:T(8,128)(2,1)S(1)}, bf16[2,64,512]{2,1,0:T(8,128)(2,1)S(1)}, u32[]{:S(2)}, u32[]{:S(2)}) collective-permute-start(bf16[2,64,512]{2,1,0:T(8,128)(2,1)S(1)} %masked.3._.mine.first.refs_4_), channel_id=1, source_target_pairs={{0,16},{8,24},{16,0},{24,8},{1,17},{9,25},{17,1},{25,9},{2,18},{10... | collective-permute-start | bytes 393224 | tf_op jit(solution)/shard_map/ppermute | solution.py:22
  16.0 0.6 %collective-permute-start.4 = (bf16[2,64,512]{2,1,0:T(8,128)(2,1)S(1)}, bf16[2,64,512]{2,1,0:T(8,128)(2,1)S(1)}, u32[]{:S(2)}, u32[]{:S(2)}) collective-permute-start(bf16[2,64,512]{2,1,0:T(8,128)(2,1)S(1)} %masked.2.first.mine.refs_1_), channel_id=1, source_target_pairs={{0,16},{8,24},{16,0},{24,8},{1,17},{9,25},{17,1},{25,9},{2,18},{10... | collective-permute-start | bytes 393224 | tf_op jit(solution)/shard_map/ppermute | solution.py:22
  16.6 3.1 %collective-permute-done.7.came = bf16[2,64,512]{2,1,0:T(8,128)(2,1)S(1)} collective-permute-done((bf16[2,64,512]{2,1,0:T(8,128)(2,1)S(1)}, bf16[2,64,512]{2,1,0:T(8,128)(2,1)S(1)}, u32[]{:S(2)}, u32[]{:S(2)}) %collective-permute-start.7) | collective-permute-done | bytes 131104 | tf_op jit(solution)/shard_map/ppermute | solution.py:22
  19.7 1.6 %collective-permute-start.8 = (bf16[2,64,512]{2,1,0:T(8,128)(2,1)S(1)}, bf16[2,64,512]{2,1,0:T(8,128)(2,1)S(1)}, u32[]{:S(2)}, u32[]{:S(2)}) collective-permute-start(bf16[2,64,512]{2,1,0:T(8,128)(2,1)S(1)} %choose.3.mine), channel_id=1, source_target_pairs={{0,8},{8,0},{16,24},{24,16},{1,9},{9,1},{17,25},{25,17},{2,10},{10... | collective-permute-start | bytes 393224 | tf_op jit(solution)/shard_map/ppermute | solution.py:22
  21.3 1.4 %collective-permute-start.5 = (bf16[2,64,512]{2,1,0:T(8,128)(2,1)S(1)}, bf16[2,64,512]{2,1,0:T(8,128)(2,1)S(1)}, u32[]{:S(2)}, u32[]{:S(2)}) collective-permute-start(bf16[2,64,512]{2,1,0:T(8,128)(2,1)S(1)} %choose.2.mine), channel_id=1, source_target_pairs={{0,8},{8,0},{16,24},{24,16},{1,9},{9,1},{17,25},{25,17},{2,10},{10... | collective-permute-start | bytes 393224 | tf_op jit(solution)/shard_map/ppermute | solution.py:22
  22.7 1.6 %collective-permute-start.13 = (bf16[3,64,512]{2,1,0:T(8,128)(2,1)S(1)}, bf16[3,64,512]{2,1,0:T(8,128)(2,1)S(1)}, u32[]{:S(2)}, u32[]{:S(2)}) collective-permute-start(bf16[3,64,512]{2,1,0:T(8,128)(2,1)S(1)} %collective-permute-done.11.refs_8_), channel_id=1, source_target_pairs={{0,2},{1,3},{2,0},{3,1},{4,6},{5,7},{6,4},{7,5},{8,10},{9,11},{10,... | collective-permute-start | bytes 589832 | tf_op jit(solution)/shard_map/ppermute | solution.py:22
  24.2 0.7 %finish.1 = (bf16[6,64,512]{2,1,0:T(8,128)(2,1)S(1)}, bf16[4,1,64,512]{3,2,1,0:T(8,128)(2,1)}) custom-call(bf16[2,64,512]{2,1,0:T(8,128)(2,1)S(1)} %masked.2.first.mine.refs_1_, bf16[3,64,512]{2,1,0:T(8,128)(2,1)S(1)} %hold.1.refs_0_, bf16[3,64,512]{2,1,0:T(8,128)(2,1)S(1)} %collective-permute-done.3.refs_1_), custom_call_target="tpu_custom_call" | custom-call | bytes 1024 | tf_op jit(solution)/shard_map/finish/pallas_call | solution.py:112
  25.0 0.6 %collective-permute-start.9 = (bf16[4,64,512]{2,1,0:T(8,128)(2,1)S(1)}, bf16[4,64,512]{2,1,0:T(8,128)(2,1)S(1)}, u32[]{:S(2)}, u32[]{:S(2)}) collective-permute-start(bf16[4,64,512]{2,1,0:T(8,128)(2,1)S(1)} %get-tuple-element.21), channel_id=1, source_target_pairs={{0,1},{1,0},{2,3},{3,2},{4,5},{5,4},{6,7},{7,6},{8,9},{9,8},{10,11... | collective-permute-start | bytes 786440 | tf_op jit(solution)/shard_map/ppermute | solution.py:22
  25.6 0.7 %collective-permute-done.5.came = bf16[2,64,512]{2,1,0:T(8,128)(2,1)S(1)} collective-permute-done((bf16[2,64,512]{2,1,0:T(8,128)(2,1)S(1)}, bf16[2,64,512]{2,1,0:T(8,128)(2,1)S(1)}, u32[]{:S(2)}, u32[]{:S(2)}) %collective-permute-start.5) | collective-permute-done | bytes 131104 | tf_op jit(solution)/shard_map/ppermute | solution.py:22
  26.4 0.1 collective-permute-start.6
  26.4 0.5 %collective-permute-start.12 = (bf16[3,64,512]{2,1,0:T(8,128)(2,1)S(1)}, bf16[3,64,512]{2,1,0:T(8,128)(2,1)S(1)}, u32[]{:S(2)}, u32[]{:S(2)}) collective-permute-start(bf16[3,64,512]{2,1,0:T(8,128)(2,1)S(1)} %collective-permute-done.11.refs_8_), channel_id=1, source_target_pairs={{0,1},{1,0},{2,3},{3,2},{4,5},{5,4},{6,7},{7,6},{8,9},{9,8},{10,11... | collective-permute-start | bytes 589832 | tf_op jit(solution)/shard_map/ppermute | solution.py:22
  26.9 1.4 %collective-permute-done.13.refs_10_ = bf16[3,64,512]{2,1,0:T(8,128)(2,1)S(1)} collective-permute-done((bf16[3,64,512]{2,1,0:T(8,128)(2,1)S(1)}, bf16[3,64,512]{2,1,0:T(8,128)(2,1)S(1)}, u32[]{:S(2)}, u32[]{:S(2)}) %collective-permute-start.13) | collective-permute-done | bytes 196640 | tf_op jit(solution)/shard_map/ppermute | solution.py:22
  28.4 1.4 %collective-permute-done.14.refs_11_ = bf16[3,64,512]{2,1,0:T(8,128)(2,1)S(1)} collective-permute-done((bf16[3,64,512]{2,1,0:T(8,128)(2,1)S(1)}, bf16[3,64,512]{2,1,0:T(8,128)(2,1)S(1)}, u32[]{:S(2)}, u32[]{:S(2)}) %collective-permute-start.14) | collective-permute-done | bytes 196640 | tf_op jit(solution)/shard_map/ppermute | solution.py:22
  29.8 2.3 %renew.1 = bf16[4,1,1,1,512,512]{5,4,3,2,1,0:T(8,128)(2,1)} custom-call(bf16[2,64,512]{2,1,0:T(8,128)(2,1)S(1)} %get-tuple-element.18.refs_0_, bf16[2,64,512]{2,1,0:T(8,128)(2,1)S(1)} %masked.2.first.mine.refs_1_, bf16[4,64,512]{2,1,0:T(8,128)(2,1)S(1)} %collective-permute-done.6.refs_2_, bf16[2,64,512]{2,1,0:T(8,128)(2,1)S(1)} %get-tuple-element.20.refs_3_, ...), custom_call_target="tpu_custom_call" | custom-call | tf_op jit(solution)/shard_map/renew/pallas_call | solution.py:250
  (21 shorter events, 0.2 us)
Async XLA Ops:
  2.0 27.8 %copy-start = (bf16[4,1,1,1,512,512]{5,4,3,2,1,0:T(8,128)(2,1)S(1)}, bf16[4,1,1,1,512,512]{5,4,3,2,1,0:T(8,128)(2,1)}, u32[]{:S(2)}) copy-start(bf16[4,1,1,1,512,512]{5,4,3,2,1,0:T(8,128)(2,1)} %refs_12_.1) | copy-start | bytes 6291460
  2.0 10.3 %collective-permute-start.2 = (bf16[1,64,512]{2,1,0:T(8,128)(2,1)S(1)}, bf16[1,64,512]{2,1,0:T(8,128)(2,1)S(1)}, u32[]{:S(2)}, u32[]{:S(2)}) collective-permute-start(bf16[1,64,512]{2,1,0:T(8,128)(2,1)S(1)} %get-tuple-element.16), channel_id=1, source_target_pairs={{0,6},{1,7},{2,4},{3,5},{4,2},{5,3},{6,0},{7,1},{8,14},{9,15},{10,... | collective-permute-start | bytes 196616 | tf_op jit(solution)/shard_map/ppermute | solution.py:22
  7.1 5.6 %collective-permute-start.1 = (bf16[1,64,512]{2,1,0:T(8,128)(2,1)S(1)}, bf16[1,64,512]{2,1,0:T(8,128)(2,1)S(1)}, u32[]{:S(2)}, u32[]{:S(2)}) collective-permute-start(bf16[1,64,512]{2,1,0:T(8,128)(2,1)S(1)} %get-tuple-element.16), channel_id=1, source_target_pairs={{0,4},{1,5},{2,6},{3,7},{4,0},{5,1},{6,2},{7,3},{8,12},{9,13},{10,... | collective-permute-start | bytes 196616 | tf_op jit(solution)/shard_map/ppermute | solution.py:22
  7.1 8.8 %collective-permute-start = (bf16[1,64,512]{2,1,0:T(8,128)(2,1)S(1)}, bf16[1,64,512]{2,1,0:T(8,128)(2,1)S(1)}, u32[]{:S(2)}, u32[]{:S(2)}) collective-permute-start(bf16[1,64,512]{2,1,0:T(8,128)(2,1)S(1)} %get-tuple-element.14.refs_0_), channel_id=1, source_target_pairs={{0,2},{1,3},{2,0},{3,1},{4,6},{5,7},{6,4},{7,5},{8,10},{9,11},{10,... | collective-permute-start | bytes 196616 | tf_op jit(solution)/shard_map/ppermute | solution.py:22
  7.8 0.7 %copy-start.1 = (s32[4,1]{0,1:T(1,128)S(1)}, s32[4,1]{0,1:T(1,128)}, u32[]{:S(2)}) copy-start(s32[4,1]{0,1:T(1,128)} %param.6) | copy-start | bytes 52
  10.0 12.7 %collective-permute-start.11 = (bf16[3,64,512]{2,1,0:T(8,128)(2,1)S(1)}, bf16[3,64,512]{2,1,0:T(8,128)(2,1)S(1)}, u32[]{:S(2)}, u32[]{:S(2)}) collective-permute-start(bf16[3,64,512]{2,1,0:T(8,128)(2,1)S(1)} %get-tuple-element.23), channel_id=1, source_target_pairs={{0,4},{1,5},{2,6},{3,7},{4,0},{5,1},{6,2},{7,3},{8,12},{9,13},{10,... | collective-permute-start | bytes 589832 | tf_op jit(solution)/shard_map/ppermute | solution.py:22
  12.8 11.4 %collective-permute-start.3 = (bf16[3,64,512]{2,1,0:T(8,128)(2,1)S(1)}, bf16[3,64,512]{2,1,0:T(8,128)(2,1)S(1)}, u32[]{:S(2)}, u32[]{:S(2)}) collective-permute-start(bf16[3,64,512]{2,1,0:T(8,128)(2,1)S(1)} %hold.1.refs_0_), channel_id=1, source_target_pairs={{0,2},{1,3},{2,0},{3,1},{4,6},{5,7},{6,4},{7,5},{8,10},{9,11},{10,... | collective-permute-start | bytes 589832 | tf_op jit(solution)/shard_map/ppermute | solution.py:22
  14.5 5.2 %collective-permute-start.7 = (bf16[2,64,512]{2,1,0:T(8,128)(2,1)S(1)}, bf16[2,64,512]{2,1,0:T(8,128)(2,1)S(1)}, u32[]{:S(2)}, u32[]{:S(2)}) collective-permute-start(bf16[2,64,512]{2,1,0:T(8,128)(2,1)S(1)} %masked.3._.mine.first.refs_4_), channel_id=1, source_target_pairs={{0,16},{8,24},{16,0},{24,8},{1,17},{9,25},{17,1},{25,9},{2,18},{10... | collective-permute-start | bytes 393224 | tf_op jit(solution)/shard_map/ppermute | solution.py:22
  16.0 5.3 %collective-permute-start.4 = (bf16[2,64,512]{2,1,0:T(8,128)(2,1)S(1)}, bf16[2,64,512]{2,1,0:T(8,128)(2,1)S(1)}, u32[]{:S(2)}, u32[]{:S(2)}) collective-permute-start(bf16[2,64,512]{2,1,0:T(8,128)(2,1)S(1)} %masked.2.first.mine.refs_1_), channel_id=1, source_target_pairs={{0,16},{8,24},{16,0},{24,8},{1,17},{9,25},{17,1},{25,9},{2,18},{10... | collective-permute-start | bytes 393224 | tf_op jit(solution)/shard_map/ppermute | solution.py:22
  19.7 5.3 %collective-permute-start.8 = (bf16[2,64,512]{2,1,0:T(8,128)(2,1)S(1)}, bf16[2,64,512]{2,1,0:T(8,128)(2,1)S(1)}, u32[]{:S(2)}, u32[]{:S(2)}) collective-permute-start(bf16[2,64,512]{2,1,0:T(8,128)(2,1)S(1)} %choose.3.mine), channel_id=1, source_target_pairs={{0,8},{8,0},{16,24},{24,16},{1,9},{9,1},{17,25},{25,17},{2,10},{10... | collective-permute-start | bytes 393224 | tf_op jit(solution)/shard_map/ppermute | solution.py:22
  21.3 5.0 %collective-permute-start.5 = (bf16[2,64,512]{2,1,0:T(8,128)(2,1)S(1)}, bf16[2,64,512]{2,1,0:T(8,128)(2,1)S(1)}, u32[]{:S(2)}, u32[]{:S(2)}) collective-permute-start(bf16[2,64,512]{2,1,0:T(8,128)(2,1)S(1)} %choose.2.mine), channel_id=1, source_target_pairs={{0,8},{8,0},{16,24},{24,16},{1,9},{9,1},{17,25},{25,17},{2,10},{10... | collective-permute-start | bytes 393224 | tf_op jit(solution)/shard_map/ppermute | solution.py:22
  22.7 5.7 %collective-permute-start.13 = (bf16[3,64,512]{2,1,0:T(8,128)(2,1)S(1)}, bf16[3,64,512]{2,1,0:T(8,128)(2,1)S(1)}, u32[]{:S(2)}, u32[]{:S(2)}) collective-permute-start(bf16[3,64,512]{2,1,0:T(8,128)(2,1)S(1)} %collective-permute-done.11.refs_8_), channel_id=1, source_target_pairs={{0,2},{1,3},{2,0},{3,1},{4,6},{5,7},{6,4},{7,5},{8,10},{9,11},{10,... | collective-permute-start | bytes 589832 | tf_op jit(solution)/shard_map/ppermute | solution.py:22
  25.0 4.8 %collective-permute-start.10 = (bf16[6,64,512]{2,1,0:T(8,128)(2,1)S(1)}, bf16[6,64,512]{2,1,0:T(8,128)(2,1)S(1)}, u32[]{:S(2)}, u32[]{:S(2)}) collective-permute-start(bf16[6,64,512]{2,1,0:T(8,128)(2,1)S(1)} %get-tuple-element.22.refs_6_), channel_id=1, source_target_pairs={{0,1},{1,0},{2,3},{3,2},{4,5},{5,4},{6,7},{7,6},{8,9},{9,8},{10,11... | collective-permute-start | bytes 1179656 | tf_op jit(solution)/shard_map/ppermute | solution.py:22
  25.0 3.3 %collective-permute-start.9 = (bf16[4,64,512]{2,1,0:T(8,128)(2,1)S(1)}, bf16[4,64,512]{2,1,0:T(8,128)(2,1)S(1)}, u32[]{:S(2)}, u32[]{:S(2)}) collective-permute-start(bf16[4,64,512]{2,1,0:T(8,128)(2,1)S(1)} %get-tuple-element.21), channel_id=1, source_target_pairs={{0,1},{1,0},{2,3},{3,2},{4,5},{5,4},{6,7},{7,6},{8,9},{9,8},{10,11... | collective-permute-start | bytes 786440 | tf_op jit(solution)/shard_map/ppermute | solution.py:22
  26.4 2.0 %collective-permute-start.6 = (bf16[4,64,512]{2,1,0:T(8,128)(2,1)S(1)}, bf16[4,64,512]{2,1,0:T(8,128)(2,1)S(1)}, u32[]{:S(2)}, u32[]{:S(2)}) collective-permute-start(bf16[4,64,512]{2,1,0:T(8,128)(2,1)S(1)} %get-tuple-element.19), channel_id=1, source_target_pairs={{0,1},{1,0},{2,3},{3,2},{4,5},{5,4},{6,7},{7,6},{8,9},{9,8},{10,11... | collective-permute-start | bytes 786440 | tf_op jit(solution)/shard_map/ppermute | solution.py:22
  26.4 1.9 %collective-permute-start.12 = (bf16[3,64,512]{2,1,0:T(8,128)(2,1)S(1)}, bf16[3,64,512]{2,1,0:T(8,128)(2,1)S(1)}, u32[]{:S(2)}, u32[]{:S(2)}) collective-permute-start(bf16[3,64,512]{2,1,0:T(8,128)(2,1)S(1)} %collective-permute-done.11.refs_8_), channel_id=1, source_target_pairs={{0,1},{1,0},{2,3},{3,2},{4,5},{5,4},{6,7},{7,6},{8,9},{9,8},{10,11... | collective-permute-start | bytes 589832 | tf_op jit(solution)/shard_map/ppermute | solution.py:22
  28.4 1.4 %collective-permute-start.14 = (bf16[3,64,512]{2,1,0:T(8,128)(2,1)S(1)}, bf16[3,64,512]{2,1,0:T(8,128)(2,1)S(1)}, u32[]{:S(2)}, u32[]{:S(2)}) collective-permute-start(bf16[3,64,512]{2,1,0:T(8,128)(2,1)S(1)} %collective-permute-done.13.refs_10_), channel_id=1, source_target_pairs={{0,1},{1,0},{2,3},{3,2},{4,5},{5,4},{6,7},{7,6},{8,9},{9,8},{10,11... | collective-permute-start | bytes 589832 | tf_op jit(solution)/shard_map/ppermute | solution.py:22

commit v6 on v5

--- a/solution.py
+++ b/solution.py
@@ -174,7 +174,7 @@
 
 def masked_kernel(mask, *refs):
     for n, ref in enumerate(refs[:-1]):
-        refs[-1][n] = (ref[0].astype(jnp.float32) * mask[...]).astype(ref.dtype)
+        refs[-1][n] = jnp.where(mask[...] > 0, ref[0], jnp.zeros_like(ref[0]))
 
 
 def masked(mask, parts):

time: 32.2 us -> 32.2 us (level)
  no operation moved by 1% of the time
where the time goes in v6:
time: 32.2 us; the launch traced here: 32 us
  starting transfers between devices  17.5 us (54%)
  waiting for transfers between devices  7.13 us (22%)
  Pallas kernels  6.01 us (19%)
  between operations  0.74 us (2%)
  local copies, waits for them, and re-layouts  0.66 us (2%)
    ppermute x15, starting transfers between devices, swap(): return lax.ppermute(x, axis, [(i, i ^ distance) for i in range(size)])  17.5 us
    ppermute x15, waiting for transfers between devices, swap(): return lax.ppermute(x, axis, [(i, i ^ distance) for i in range(size)])  7.13 us
    pallas_call x2, Pallas kernels, solve_call(): pl.pallas_call(kernel, out_shape=outs, in_specs=[pl.BlockSpec(memory_spac...  2.9 us
    pallas_call x1, Pallas kernels, renew(): pl.pallas_call(functools.partial(renew_kernel, plan, chips), out_shape=ja...  2.24 us
    pallas_call x7, Pallas kernels, small_call(): pl.pallas_call(kernel, out_shape=outs, in_specs=[VMEM] * len(args), out_s...  0.86 us
    unnamed x4, local copies, waits for them, and re-layouts  0.66 us
  transfers between devices with their start and end apart: 15, of which 5 were waited for; matrix products, arithmetic and copies ran while one was open for 0% of the time, Pallas kernels for 7%

profile of v6, /device:TPU:0, one launch (start us, length us, event | category | flops | bytes accessed | tf_op | source)
XLA Modules:
  0.0 32.0 jit_solution(16859307634699524340)
XLA Ops:
  0.6 1.4 %solve_first.1 = (bf16[1,64,512]{2,1,0:T(8,128)(2,1)S(1)}, bf16[1,64,512]{2,1,0:T(8,128)(2,1)S(1)}) custom-call(bf16[4,1,64,512]{3,2,1,0:T(8,128)(2,1)} %panel.3, bf16[512,512]{1,0:T(8,128)(2,1)} %diag_inv.3), custom_call_target="tpu_custom_call" | custom-call | bytes 1024 | tf_op jit(solution)/shard_map/solve_first/pallas_call | solution.py:61
  2.0 0.0 copy-start
  2.0 5.1 %collective-permute-start.2 = (bf16[1,64,512]{2,1,0:T(8,128)(2,1)S(1)}, bf16[1,64,512]{2,1,0:T(8,128)(2,1)S(1)}, u32[]{:S(2)}, u32[]{:S(2)}) collective-permute-start(bf16[1,64,512]{2,1,0:T(8,128)(2,1)S(1)} %get-tuple-element.16), channel_id=1, source_target_pairs={{0,6},{1,7},{2,4},{3,5},{4,2},{5,3},{6,0},{7,1},{8,14},{9,15},{10,... | collective-permute-start | bytes 196616 | tf_op jit(solution)/shard_map/ppermute | solution.py:22
  7.1 0.0 collective-permute-start.1
  7.1 0.6 %collective-permute-start = (bf16[1,64,512]{2,1,0:T(8,128)(2,1)S(1)}, bf16[1,64,512]{2,1,0:T(8,128)(2,1)S(1)}, u32[]{:S(2)}, u32[]{:S(2)}) collective-permute-start(bf16[1,64,512]{2,1,0:T(8,128)(2,1)S(1)} %get-tuple-element.14.refs_0_), channel_id=1, source_target_pairs={{0,2},{1,3},{2,0},{3,1},{4,6},{5,7},{6,4},{7,5},{8,10},{9,11},{10,... | collective-permute-start | bytes 196616 | tf_op jit(solution)/shard_map/ppermute | solution.py:22
  7.8 0.7 %copy-done.1 = s32[4,1]{0,1:T(1,128)S(1)} copy-done((s32[4,1]{0,1:T(1,128)S(1)}, s32[4,1]{0,1:T(1,128)}, u32[]{:S(2)}) %copy-start.1) | copy-done | bytes 40
  8.4 1.5 %solve_rest.1 = (f32[1,512]{1,0:T(1,128)S(1)}, bf16[3,64,512]{2,1,0:T(8,128)(2,1)S(1)}, bf16[3,64,512]{2,1,0:T(8,128)(2,1)S(1)}) custom-call(s32[4]{0:T(128)S(1)} %bitcast.1, bf16[4,1,64,512]{3,2,1,0:T(8,128)(2,1)} %panel.3, bf16[512,512]{1,0:T(8,128)(2,1)} %diag_inv.3), custom_call_target="tpu_custom_call" | custom-call | bytes 1024 | tf_op jit(solution)/shard_map/solve_rest/pallas_call | solution.py:61
  10.0 2.4 %collective-permute-start.11 = (bf16[3,64,512]{2,1,0:T(8,128)(2,1)S(1)}, bf16[3,64,512]{2,1,0:T(8,128)(2,1)S(1)}, u32[]{:S(2)}, u32[]{:S(2)}) collective-permute-start(bf16[3,64,512]{2,1,0:T(8,128)(2,1)S(1)} %get-tuple-element.23), channel_id=1, source_target_pairs={{0,4},{1,5},{2,6},{3,7},{4,0},{5,1},{6,2},{7,3},{8,12},{9,13},{10,... | collective-permute-start | bytes 589832 | tf_op jit(solution)/shard_map/ppermute | solution.py:22
  12.3 0.4 %collective-permute-done.1.refs_0_ = bf16[1,64,512]{2,1,0:T(8,128)(2,1)S(1)} collective-permute-done((bf16[1,64,512]{2,1,0:T(8,128)(2,1)S(1)}, bf16[1,64,512]{2,1,0:T(8,128)(2,1)S(1)}, u32[]{:S(2)}, u32[]{:S(2)}) %collective-permute-start.1) | collective-permute-done | bytes 65568 | tf_op jit(solution)/shard_map/ppermute | solution.py:22
  12.8 1.7 %collective-permute-start.3 = (bf16[3,64,512]{2,1,0:T(8,128)(2,1)S(1)}, bf16[3,64,512]{2,1,0:T(8,128)(2,1)S(1)}, u32[]{:S(2)}, u32[]{:S(2)}) collective-permute-start(bf16[3,64,512]{2,1,0:T(8,128)(2,1)S(1)} %hold.1.refs_0_), channel_id=1, source_target_pairs={{0,2},{1,3},{2,0},{3,1},{4,6},{5,7},{6,4},{7,5},{8,10},{9,11},{10,... | collective-permute-start | bytes 589832 | tf_op jit(solution)/shard_map/ppermute | solution.py:22
  14.4 1.5 %collective-permute-start.7 = (bf16[2,64,512]{2,1,0:T(8,128)(2,1)S(1)}, bf16[2,64,512]{2,1,0:T(8,128)(2,1)S(1)}, u32[]{:S(2)}, u32[]{:S(2)}) collective-permute-start(bf16[2,64,512]{2,1,0:T(8,128)(2,1)S(1)} %masked.3._.mine.first.refs_4_), channel_id=1, source_target_pairs={{0,16},{8,24},{16,0},{24,8},{1,17},{9,25},{17,1},{25,9},{2,18},{10... | collective-permute-start | bytes 393224 | tf_op jit(solution)/shard_map/ppermute | solution.py:22
  16.0 0.6 %collective-permute-start.4 = (bf16[2,64,512]{2,1,0:T(8,128)(2,1)S(1)}, bf16[2,64,512]{2,1,0:T(8,128)(2,1)S(1)}, u32[]{:S(2)}, u32[]{:S(2)}) collective-permute-start(bf16[2,64,512]{2,1,0:T(8,128)(2,1)S(1)} %masked.2.first.mine.refs_1_), channel_id=1, source_target_pairs={{0,16},{8,24},{16,0},{24,8},{1,17},{9,25},{17,1},{25,9},{2,18},{10... | collective-permute-start | bytes 393224 | tf_op jit(solution)/shard_map/ppermute | solution.py:22
  16.6 3.1 %collective-permute-done.7.came = bf16[2,64,512]{2,1,0:T(8,128)(2,1)S(1)} collective-permute-done((bf16[2,64,512]{2,1,0:T(8,128)(2,1)S(1)}, bf16[2,64,512]{2,1,0:T(8,128)(2,1)S(1)}, u32[]{:S(2)}, u32[]{:S(2)}) %collective-permute-start.7) | collective-permute-done | bytes 131104 | tf_op jit(solution)/shard_map/ppermute | solution.py:22
  19.7 1.6 %collective-permute-start.8 = (bf16[2,64,512]{2,1,0:T(8,128)(2,1)S(1)}, bf16[2,64,512]{2,1,0:T(8,128)(2,1)S(1)}, u32[]{:S(2)}, u32[]{:S(2)}) collective-permute-start(bf16[2,64,512]{2,1,0:T(8,128)(2,1)S(1)} %choose.3.mine), channel_id=1, source_target_pairs={{0,8},{8,0},{16,24},{24,16},{1,9},{9,1},{17,25},{25,17},{2,10},{10... | collective-permute-start | bytes 393224 | tf_op jit(solution)/shard_map/ppermute | solution.py:22
  21.3 1.4 %collective-permute-start.5 = (bf16[2,64,512]{2,1,0:T(8,128)(2,1)S(1)}, bf16[2,64,512]{2,1,0:T(8,128)(2,1)S(1)}, u32[]{:S(2)}, u32[]{:S(2)}) collective-permute-start(bf16[2,64,512]{2,1,0:T(8,128)(2,1)S(1)} %choose.2.mine), channel_id=1, source_target_pairs={{0,8},{8,0},{16,24},{24,16},{1,9},{9,1},{17,25},{25,17},{2,10},{10... | collective-permute-start | bytes 393224 | tf_op jit(solution)/shard_map/ppermute | solution.py:22
  22.7 1.6 %collective-permute-start.13 = (bf16[3,64,512]{2,1,0:T(8,128)(2,1)S(1)}, bf16[3,64,512]{2,1,0:T(8,128)(2,1)S(1)}, u32[]{:S(2)}, u32[]{:S(2)}) collective-permute-start(bf16[3,64,512]{2,1,0:T(8,128)(2,1)S(1)} %collective-permute-done.11.refs_8_), channel_id=1, source_target_pairs={{0,2},{1,3},{2,0},{3,1},{4,6},{5,7},{6,4},{7,5},{8,10},{9,11},{10,... | collective-permute-start | bytes 589832 | tf_op jit(solution)/shard_map/ppermute | solution.py:22
  24.2 0.7 %finish.1 = (bf16[6,64,512]{2,1,0:T(8,128)(2,1)S(1)}, bf16[4,1,64,512]{3,2,1,0:T(8,128)(2,1)}) custom-call(bf16[2,64,512]{2,1,0:T(8,128)(2,1)S(1)} %masked.2.first.mine.refs_1_, bf16[3,64,512]{2,1,0:T(8,128)(2,1)S(1)} %hold.1.refs_0_, bf16[3,64,512]{2,1,0:T(8,128)(2,1)S(1)} %collective-permute-done.3.refs_1_), custom_call_target="tpu_custom_call" | custom-call | bytes 1024 | tf_op jit(solution)/shard_map/finish/pallas_call | solution.py:112
  25.0 0.6 %collective-permute-start.9 = (bf16[4,64,512]{2,1,0:T(8,128)(2,1)S(1)}, bf16[4,64,512]{2,1,0:T(8,128)(2,1)S(1)}, u32[]{:S(2)}, u32[]{:S(2)}) collective-permute-start(bf16[4,64,512]{2,1,0:T(8,128)(2,1)S(1)} %get-tuple-element.21), channel_id=1, source_target_pairs={{0,1},{1,0},{2,3},{3,2},{4,5},{5,4},{6,7},{7,6},{8,9},{9,8},{10,11... | collective-permute-start | bytes 786440 | tf_op jit(solution)/shard_map/ppermute | solution.py:22
  25.6 0.7 %collective-permute-done.5.came = bf16[2,64,512]{2,1,0:T(8,128)(2,1)S(1)} collective-permute-done((bf16[2,64,512]{2,1,0:T(8,128)(2,1)S(1)}, bf16[2,64,512]{2,1,0:T(8,128)(2,1)S(1)}, u32[]{:S(2)}, u32[]{:S(2)}) %collective-permute-start.5) | collective-permute-done | bytes 131104 | tf_op jit(solution)/shard_map/ppermute | solution.py:22
  26.4 0.1 collective-permute-start.6
  26.4 0.5 %collective-permute-start.12 = (bf16[3,64,512]{2,1,0:T(8,128)(2,1)S(1)}, bf16[3,64,512]{2,1,0:T(8,128)(2,1)S(1)}, u32[]{:S(2)}, u32[]{:S(2)}) collective-permute-start(bf16[3,64,512]{2,1,0:T(8,128)(2,1)S(1)} %collective-permute-done.11.refs_8_), channel_id=1, source_target_pairs={{0,1},{1,0},{2,3},{3,2},{4,5},{5,4},{6,7},{7,6},{8,9},{9,8},{10,11... | collective-permute-start | bytes 589832 | tf_op jit(solution)/shard_map/ppermute | solution.py:22
  26.9 1.4 %collective-permute-done.13.refs_10_ = bf16[3,64,512]{2,1,0:T(8,128)(2,1)S(1)} collective-permute-done((bf16[3,64,512]{2,1,0:T(8,128)(2,1)S(1)}, bf16[3,64,512]{2,1,0:T(8,128)(2,1)S(1)}, u32[]{:S(2)}, u32[]{:S(2)}) %collective-permute-start.13) | collective-permute-done | bytes 196640 | tf_op jit(solution)/shard_map/ppermute | solution.py:22
  28.4 1.4 %collective-permute-done.14.refs_11_ = bf16[3,64,512]{2,1,0:T(8,128)(2,1)S(1)} collective-permute-done((bf16[3,64,512]{2,1,0:T(8,128)(2,1)S(1)}, bf16[3,64,512]{2,1,0:T(8,128)(2,1)S(1)}, u32[]{:S(2)}, u32[]{:S(2)}) %collective-permute-start.14) | collective-permute-done | bytes 196640 | tf_op jit(solution)/shard_map/ppermute | solution.py:22
  29.8 2.2 %renew.1 = bf16[4,1,1,1,512,512]{5,4,3,2,1,0:T(8,128)(2,1)} custom-call(bf16[2,64,512]{2,1,0:T(8,128)(2,1)S(1)} %get-tuple-element.18.refs_0_, bf16[2,64,512]{2,1,0:T(8,128)(2,1)S(1)} %masked.2.first.mine.refs_1_, bf16[4,64,512]{2,1,0:T(8,128)(2,1)S(1)} %collective-permute-done.6.refs_2_, bf16[2,64,512]{2,1,0:T(8,128)(2,1)S(1)} %get-tuple-element.20.refs_3_, ...), custom_call_target="tpu_custom_call" | custom-call | tf_op jit(solution)/shard_map/renew/pallas_call | solution.py:250
  (21 shorter events, 0.1 us)
Async XLA Ops:
  2.0 27.8 %copy-start = (bf16[4,1,1,1,512,512]{5,4,3,2,1,0:T(8,128)(2,1)S(1)}, bf16[4,1,1,1,512,512]{5,4,3,2,1,0:T(8,128)(2,1)}, u32[]{:S(2)}) copy-start(bf16[4,1,1,1,512,512]{5,4,3,2,1,0:T(8,128)(2,1)} %refs_12_.1) | copy-start | bytes 6291460
  2.0 10.3 %collective-permute-start.2 = (bf16[1,64,512]{2,1,0:T(8,128)(2,1)S(1)}, bf16[1,64,512]{2,1,0:T(8,128)(2,1)S(1)}, u32[]{:S(2)}, u32[]{:S(2)}) collective-permute-start(bf16[1,64,512]{2,1,0:T(8,128)(2,1)S(1)} %get-tuple-element.16), channel_id=1, source_target_pairs={{0,6},{1,7},{2,4},{3,5},{4,2},{5,3},{6,0},{7,1},{8,14},{9,15},{10,... | collective-permute-start | bytes 196616 | tf_op jit(solution)/shard_map/ppermute | solution.py:22
  7.1 5.6 %collective-permute-start.1 = (bf16[1,64,512]{2,1,0:T(8,128)(2,1)S(1)}, bf16[1,64,512]{2,1,0:T(8,128)(2,1)S(1)}, u32[]{:S(2)}, u32[]{:S(2)}) collective-permute-start(bf16[1,64,512]{2,1,0:T(8,128)(2,1)S(1)} %get-tuple-element.16), channel_id=1, source_target_pairs={{0,4},{1,5},{2,6},{3,7},{4,0},{5,1},{6,2},{7,3},{8,12},{9,13},{10,... | collective-permute-start | bytes 196616 | tf_op jit(solution)/shard_map/ppermute | solution.py:22
  7.1 8.8 %collective-permute-start = (bf16[1,64,512]{2,1,0:T(8,128)(2,1)S(1)}, bf16[1,64,512]{2,1,0:T(8,128)(2,1)S(1)}, u32[]{:S(2)}, u32[]{:S(2)}) collective-permute-start(bf16[1,64,512]{2,1,0:T(8,128)(2,1)S(1)} %get-tuple-element.14.refs_0_), channel_id=1, source_target_pairs={{0,2},{1,3},{2,0},{3,1},{4,6},{5,7},{6,4},{7,5},{8,10},{9,11},{10,... | collective-permute-start | bytes 196616 | tf_op jit(solution)/shard_map/ppermute | solution.py:22
  7.8 0.7 %copy-start.1 = (s32[4,1]{0,1:T(1,128)S(1)}, s32[4,1]{0,1:T(1,128)}, u32[]{:S(2)}) copy-start(s32[4,1]{0,1:T(1,128)} %param.6) | copy-start | bytes 52
  10.0 12.7 %collective-permute-start.11 = (bf16[3,64,512]{2,1,0:T(8,128)(2,1)S(1)}, bf16[3,64,512]{2,1,0:T(8,128)(2,1)S(1)}, u32[]{:S(2)}, u32[]{:S(2)}) collective-permute-start(bf16[3,64,512]{2,1,0:T(8,128)(2,1)S(1)} %get-tuple-element.23), channel_id=1, source_target_pairs={{0,4},{1,5},{2,6},{3,7},{4,0},{5,1},{6,2},{7,3},{8,12},{9,13},{10,... | collective-permute-start | bytes 589832 | tf_op jit(solution)/shard_map/ppermute | solution.py:22
  12.8 11.4 %collective-permute-start.3 = (bf16[3,64,512]{2,1,0:T(8,128)(2,1)S(1)}, bf16[3,64,512]{2,1,0:T(8,128)(2,1)S(1)}, u32[]{:S(2)}, u32[]{:S(2)}) collective-permute-start(bf16[3,64,512]{2,1,0:T(8,128)(2,1)S(1)} %hold.1.refs_0_), channel_id=1, source_target_pairs={{0,2},{1,3},{2,0},{3,1},{4,6},{5,7},{6,4},{7,5},{8,10},{9,11},{10,... | collective-permute-start | bytes 589832 | tf_op jit(solution)/shard_map/ppermute | solution.py:22
  14.4 5.2 %collective-permute-start.7 = (bf16[2,64,512]{2,1,0:T(8,128)(2,1)S(1)}, bf16[2,64,512]{2,1,0:T(8,128)(2,1)S(1)}, u32[]{:S(2)}, u32[]{:S(2)}) collective-permute-start(bf16[2,64,512]{2,1,0:T(8,128)(2,1)S(1)} %masked.3._.mine.first.refs_4_), channel_id=1, source_target_pairs={{0,16},{8,24},{16,0},{24,8},{1,17},{9,25},{17,1},{25,9},{2,18},{10... | collective-permute-start | bytes 393224 | tf_op jit(solution)/shard_map/ppermute | solution.py:22
  16.0 5.3 %collective-permute-start.4 = (bf16[2,64,512]{2,1,0:T(8,128)(2,1)S(1)}, bf16[2,64,512]{2,1,0:T(8,128)(2,1)S(1)}, u32[]{:S(2)}, u32[]{:S(2)}) collective-permute-start(bf16[2,64,512]{2,1,0:T(8,128)(2,1)S(1)} %masked.2.first.mine.refs_1_), channel_id=1, source_target_pairs={{0,16},{8,24},{16,0},{24,8},{1,17},{9,25},{17,1},{25,9},{2,18},{10... | collective-permute-start | bytes 393224 | tf_op jit(solution)/shard_map/ppermute | solution.py:22
  19.7 5.3 %collective-permute-start.8 = (bf16[2,64,512]{2,1,0:T(8,128)(2,1)S(1)}, bf16[2,64,512]{2,1,0:T(8,128)(2,1)S(1)}, u32[]{:S(2)}, u32[]{:S(2)}) collective-permute-start(bf16[2,64,512]{2,1,0:T(8,128)(2,1)S(1)} %choose.3.mine), channel_id=1, source_target_pairs={{0,8},{8,0},{16,24},{24,16},{1,9},{9,1},{17,25},{25,17},{2,10},{10... | collective-permute-start | bytes 393224 | tf_op jit(solution)/shard_map/ppermute | solution.py:22
  21.3 5.0 %collective-permute-start.5 = (bf16[2,64,512]{2,1,0:T(8,128)(2,1)S(1)}, bf16[2,64,512]{2,1,0:T(8,128)(2,1)S(1)}, u32[]{:S(2)}, u32[]{:S(2)}) collective-permute-start(bf16[2,64,512]{2,1,0:T(8,128)(2,1)S(1)} %choose.2.mine), channel_id=1, source_target_pairs={{0,8},{8,0},{16,24},{24,16},{1,9},{9,1},{17,25},{25,17},{2,10},{10... | collective-permute-start | bytes 393224 | tf_op jit(solution)/shard_map/ppermute | solution.py:22
  22.7 5.7 %collective-permute-start.13 = (bf16[3,64,512]{2,1,0:T(8,128)(2,1)S(1)}, bf16[3,64,512]{2,1,0:T(8,128)(2,1)S(1)}, u32[]{:S(2)}, u32[]{:S(2)}) collective-permute-start(bf16[3,64,512]{2,1,0:T(8,128)(2,1)S(1)} %collective-permute-done.11.refs_8_), channel_id=1, source_target_pairs={{0,2},{1,3},{2,0},{3,1},{4,6},{5,7},{6,4},{7,5},{8,10},{9,11},{10,... | collective-permute-start | bytes 589832 | tf_op jit(solution)/shard_map/ppermute | solution.py:22
  25.0 4.8 %collective-permute-start.10 = (bf16[6,64,512]{2,1,0:T(8,128)(2,1)S(1)}, bf16[6,64,512]{2,1,0:T(8,128)(2,1)S(1)}, u32[]{:S(2)}, u32[]{:S(2)}) collective-permute-start(bf16[6,64,512]{2,1,0:T(8,128)(2,1)S(1)} %get-tuple-element.22.refs_6_), channel_id=1, source_target_pairs={{0,1},{1,0},{2,3},{3,2},{4,5},{5,4},{6,7},{7,6},{8,9},{9,8},{10,11... | collective-permute-start | bytes 1179656 | tf_op jit(solution)/shard_map/ppermute | solution.py:22
  25.0 3.3 %collective-permute-start.9 = (bf16[4,64,512]{2,1,0:T(8,128)(2,1)S(1)}, bf16[4,64,512]{2,1,0:T(8,128)(2,1)S(1)}, u32[]{:S(2)}, u32[]{:S(2)}) collective-permute-start(bf16[4,64,512]{2,1,0:T(8,128)(2,1)S(1)} %get-tuple-element.21), channel_id=1, source_target_pairs={{0,1},{1,0},{2,3},{3,2},{4,5},{5,4},{6,7},{7,6},{8,9},{9,8},{10,11... | collective-permute-start | bytes 786440 | tf_op jit(solution)/shard_map/ppermute | solution.py:22
  26.4 2.0 %collective-permute-start.6 = (bf16[4,64,512]{2,1,0:T(8,128)(2,1)S(1)}, bf16[4,64,512]{2,1,0:T(8,128)(2,1)S(1)}, u32[]{:S(2)}, u32[]{:S(2)}) collective-permute-start(bf16[4,64,512]{2,1,0:T(8,128)(2,1)S(1)} %get-tuple-element.19), channel_id=1, source_target_pairs={{0,1},{1,0},{2,3},{3,2},{4,5},{5,4},{6,7},{7,6},{8,9},{9,8},{10,11... | collective-permute-start | bytes 786440 | tf_op jit(solution)/shard_map/ppermute | solution.py:22
  26.4 1.9 %collective-permute-start.12 = (bf16[3,64,512]{2,1,0:T(8,128)(2,1)S(1)}, bf16[3,64,512]{2,1,0:T(8,128)(2,1)S(1)}, u32[]{:S(2)}, u32[]{:S(2)}) collective-permute-start(bf16[3,64,512]{2,1,0:T(8,128)(2,1)S(1)} %collective-permute-done.11.refs_8_), channel_id=1, source_target_pairs={{0,1},{1,0},{2,3},{3,2},{4,5},{5,4},{6,7},{7,6},{8,9},{9,8},{10,11... | collective-permute-start | bytes 589832 | tf_op jit(solution)/shard_map/ppermute | solution.py:22
  28.3 1.4 %collective-permute-start.14 = (bf16[3,64,512]{2,1,0:T(8,128)(2,1)S(1)}, bf16[3,64,512]{2,1,0:T(8,128)(2,1)S(1)}, u32[]{:S(2)}, u32[]{:S(2)}) collective-permute-start(bf16[3,64,512]{2,1,0:T(8,128)(2,1)S(1)} %collective-permute-done.13.refs_10_), channel_id=1, source_target_pairs={{0,1},{1,0},{2,3},{3,2},{4,5},{5,4},{6,7},{7,6},{8,9},{9,8},{10,11... | collective-permute-start | bytes 589832 | tf_op jit(solution)/shard_map/ppermute | solution.py:22
